TPU v7x, 256 devices: a whole 4x4x8 slice. The times are simulated.
256 devices in a mesh: dp: 4 (over x_hi, core), mp: 64 (over x_lo, y, z).
Axes of the slice: x: 4 (x_hi: 2, x_lo: 2; x = x_hi * 2 + x_lo), y: 4, z: 8, core: 2. Of those that a mesh axis runs over, the one named last changes fastest.
Arguments:
- tokens: bfloat16 [2304, 4096], P(('dp', 'mp')), may hold values from -6 to 6
- out_grad: bfloat16 [2304, 4096], P(('dp', 'mp')), may hold values from -6 to 6
- gate_weight: bfloat16 [16384, 4096], P('mp', 'dp'), may hold values from -0.125 to 0.125
- up_weight: bfloat16 [16384, 4096], P('mp', 'dp'), may hold values from -0.125 to 0.125
- down_weight: bfloat16 [16384, 4096], P('mp', 'dp'), may hold values from -0.0625 to 0.0625
- block_mask: int32 [3, 128, 32], replicated, may hold values 0 or 1
- assignment: int32 [128], P('mp'), may hold values from 0 to 127, each once
Outputs:
- input_grad: bfloat16 [2304, 4096], P(('dp', 'mp'))
- gate_grad_out: bfloat16 [16384, 4096], P('mp', 'dp')
- up_grad_out: bfloat16 [16384, 4096], P('mp', 'dp')
- down_grad_out: bfloat16 [16384, 4096], P('mp', 'dp')
Inputs may be any that keep to these rules, and one draw needn't show every extreme that they name: `assignment`: each of the 128 panel numbers appears once.
All inputs are finite; a program needn't handle non-finite values.
Results may differ from a plain program's by a relative error of at most 0.0049.
Values may be sent and summed in bfloat16 or wider, within the bound.
No kernel may reach another device: no remote copies, remote signals or barrier semaphores. Data moves between devices by JAX's collectives and lax.ppermute only.
A program may use at most 128 MiB of HBM per device.

v0:
```python
import jax
import jax.numpy as jnp
from jax import lax
from jax.experimental import pallas as pl
from jax.experimental.pallas import tpu as pltpu
from jax.sharding import Mesh
from jax.sharding import PartitionSpec as P

BLK = 128
AXES = ("x_hi", "core", "x_lo", "y", "z")
SIZES = (2, 2, 2, 4, 8)
DP = ("x_hi", "core")
MP = ("x_lo", "y", "z")
N_X, N_Y, N_Z = 2, 4, 8
BF = jnp.bfloat16
F32 = jnp.float32
WHOLE = pl.BlockSpec(memory_space=pltpu.VMEM)
VMEM_LIMIT = 6 << 20
BIG_LIMIT = 52 << 20
ANYWHERE = pl.BlockSpec(memory_space=pl.ANY)
SCALARS = pl.BlockSpec(memory_space=pltpu.SMEM)


def call(kernel, out_shape, in_specs, bytes_accessed, flops=0, **more):
    return pl.pallas_call(
        kernel,
        out_shape=out_shape,
        in_specs=in_specs,
        out_specs=more.pop("out_specs", jax.tree.map(lambda _: WHOLE, out_shape)),
        compiler_params=pltpu.CompilerParams(vmem_limit_bytes=more.pop("limit", VMEM_LIMIT)),
        cost_estimate=pl.CostEstimate(
            flops=flops, bytes_accessed=bytes_accessed, transcendentals=0
        ),
        **more,
    )


def local(function, *arrays):
    out = jax.eval_shape(function, *arrays)

    def kernel(*refs):
        results = function(*(ref[...] for ref in refs[: len(arrays)]))
        for ref, value in zip(refs[len(arrays) :], results):
            ref[...] = value

    size = sum(a.size * a.dtype.itemsize for a in (*arrays, *out))
    return call(kernel, list(out), [WHOLE] * len(arrays), size)(*arrays)


def fetch(block, axis, offset):
    size = SIZES[AXES.index(axis)]
    return lax.ppermute(block, axis, [(i, (i - offset) % size) for i in range(size)])


def pack(arrays):
    own, width = arrays[0].shape
    tail, rows = width // (own - 1), own - 1

    def kernel(*refs):
        out = refs[-1]
        for k, ref in enumerate(refs[:-1]):
            out[k * rows : (k + 1) * rows, :width] = ref[:rows, :]
            for i in range(rows):
                spot = k * rows + i
                out[spot : spot + 1, width:] = ref[rows : rows + 1, i * tail : (i + 1) * tail]

    out = jax.ShapeDtypeStruct((rows * len(arrays), width + tail), BF)
    return call(kernel, out, [WHOLE] * len(arrays), 4 * own * width * len(arrays))(*arrays)


def by_array(mine, other):
    rows = mine.shape[0] // 2

    def kernel(mine_ref, other_ref, *out):
        for k in range(2):
            out[k][:rows, :] = mine_ref[k * rows : (k + 1) * rows, :]
            out[k][rows:, :] = other_ref[k * rows : (k + 1) * rows, :]

    out = [jax.ShapeDtypeStruct(mine.shape, BF)] * 2
    return call(kernel, out, [WHOLE] * 2, 4 * mine.shape[0] * mine.shape[1])(mine, other)


def stack(blocks):
    starts = [sum(b.shape[0] for b in blocks[:i]) for i in range(len(blocks) + 1)]

    def kernel(*refs):
        for ref, start in zip(refs[:-1], starts):
            refs[-1][start : start + ref.shape[0], :] = ref[...]

    whole = jax.ShapeDtypeStruct((starts[-1], blocks[0].shape[1]), blocks[0].dtype)
    size = 4 * starts[-1] * blocks[0].shape[1]
    return call(kernel, whole, [WHOLE] * len(blocks), size)(*blocks)


def join(lines):
    spots, flat, top = [], [], 0
    for line in lines:
        left = 0
        for block in line:
            spots.append((top, left))
            flat.append(block)
            left += block.shape[1]
        top += line[0].shape[0]

    def kernel(*refs):
        for ref, (row, col) in zip(refs[:-1], spots):
            refs[-1][row : row + ref.shape[0], col : col + ref.shape[1]] = ref[...]

    whole = jax.ShapeDtypeStruct((top, left), flat[0].dtype)
    return call(kernel, whole, [WHOLE] * len(flat), 4 * top * left)(*flat)


def unpack(pieces, units, own, width):
    tail = width // (own - 1)
    flat = [block for _, blocks in pieces for block in blocks]

    def kernel(*refs):
        out, at = refs[-1], 0
        for firsts, blocks in pieces:
            held = refs[at : at + len(blocks)]
            at += len(blocks)
            for i, unit in enumerate(firsts):
                rows = slice(8 * i, 8 * i + 8)
                top = unit * own
                value = jnp.concatenate([ref[rows, :] for ref in held], axis=1)
                out[top : top + own - 1, :] = value[:, :width]
                for j in range(own - 1):
                    part = value[j : j + 1, width:]
                    out[top + own - 1 : top + own, j * tail : (j + 1) * tail] = part

    whole = jax.ShapeDtypeStruct((units * own, width), BF)
    return call(kernel, whole, [WHOLE] * len(flat), 4 * units * own * width)(*flat)


def mask_weights(weights, keep_rows):
    rows, cols = weights[0].shape
    panels = rows // BLK

    def kernel(keep_ref, *refs):
        for m in range(len(weights)):
            for p in range(panels):
                row = m * panels + p
                keep = keep_ref[row : row + 1, :]
                kept = refs[m][p * BLK : (p + 1) * BLK, :].astype(F32) * keep
                half, row = divmod(row, len(weights) * panels // 2)
                refs[half - 2][row * BLK : (row + 1) * BLK, :] = kept.astype(BF)

    out = [jax.ShapeDtypeStruct((rows * len(weights) // 2, cols), BF)] * 2
    return call(kernel, out, [WHOLE] * 4, 12 * rows * cols)(keep_rows, *weights)


def turn(halves):
    rows, cols = halves[0].shape

    def kernel(top, bottom, out):
        out[:, :rows] = top[...].T
        out[:, rows:] = bottom[...].T

    out = jax.ShapeDtypeStruct((cols, 2 * rows), BF)
    return call(kernel, out, [WHOLE] * 2, 8 * rows * cols)(*halves)


def deal(total, own):
    width = total.shape[1]
    unit, rows, tail = N_X * own, own - 1, width // (own - 1)
    count = total.shape[0] // unit

    def kernel(ref, *out):
        for u in range(count):
            for k in range(N_X):
                top = u * unit + k * own
                out[u][k * rows : (k + 1) * rows, :width] = ref[top : top + rows, :]
                for i in range(rows):
                    part = ref[top + rows : top + own, i * tail : (i + 1) * tail]
                    out[u][k * rows + i : k * rows + i + 1, width:] = part

    spec = [jax.ShapeDtypeStruct((N_X * rows, width + tail), BF)] * count
    return call(kernel, spec, [WHOLE], 6 * total.shape[0] * width)(total)


def place_rows(place, mine, other):
    rows, packed = mine.shape
    width = packed * rows // (rows + 1)
    cols, tail = width // 4, width // rows

    def kernel(place_ref, mine_ref, other_ref, out):
        total = (mine_ref[...] + other_ref[...]).astype(BF)
        for b in range(4):
            start = place_ref[b] * cols
            where = pl.ds(pl.multiple_of(start, tail), cols)
            out[:rows, where] = total[:, b * cols : (b + 1) * cols]
            for j in range(cols // tail):
                i = b * (cols // tail) + j
                where = pl.ds(pl.multiple_of(start + j * tail, tail), tail)
                out[rows : rows + 1, where] = total[i : i + 1, width:]

    out = jax.ShapeDtypeStruct((rows + 1, width), BF)
    return call(kernel, out, [SCALARS, WHOLE, WHOLE], 10 * rows * packed)(place, mine, other)


def middle(z, place, tok, pieces, turned, blocks, own):
    total, width = tok.shape
    cut, cols = blocks[0][0].shape
    hid = 2 * cut // 3
    unit, tail = N_X * own, width // (own - 1)
    block = N_Y * unit
    flat = [part for _, held in pieces for part in held]
    n, m = len(flat), len(pieces)

    def kernel(z_ref, place_ref, tok_ref, *refs):
        piece_refs, turned_refs, block_refs = refs[:n], refs[n : n + 4], refs[n + 4 : n + 12]
        first_ref, grd_out, hidden_ref, out = refs[n + 12 : n + 16]
        packed = refs[n + 16 : n + 16 + m]
        x, wt, w, grd, g, total_ref, pre, by_z, held, sems, out_sems = refs[n + 16 + m :]

        def bring(source, target, i):
            copy = pltpu.make_async_copy(source, target, sems.at[i])
            copy.start()
            return copy

        def spot(dz):
            return lax.rem(z_ref[0] + dz, N_Z)

        def at(b):
            return pl.ds(pl.multiple_of(place_ref[b] * cols, cols), cols)

        for b in range(4):
            bring(turned_refs[b], wt.at[b], n + b)
            bring(tok_ref.at[:, at(b)], x.at[b], n + 4 + b)
        come, i = [], 0
        for target, (_, parts) in zip(packed, pieces):
            size = target.shape[1] // len(parts)
            for j in range(len(parts)):
                come.append(bring(piece_refs[i], target.at[:, j * size : (j + 1) * size], i))
                i += 1
        come_w = []
        for b in range(4):
            top, bottom = block_refs[2 * b], block_refs[2 * b + 1].at[: 2 * hid - cut, :]
            come_w.append(bring(top, w.at[b, :cut, :], n + 8 + b))
            come_w.append(bring(bottom, w.at[b, cut:, :], n + 12 + b))
        def pre_part(b, _):
            pltpu.make_async_copy(turned_refs[0], wt.at[b], sems.at[n + b]).wait()
            pltpu.make_async_copy(tok_ref.at[:, :cols], x.at[b], sems.at[n + 4 + b]).wait()
            part = jnp.dot(x[b], wt[b, :, : 2 * hid], preferred_element_type=F32)

            @pl.when(b == 0)
            def _():
                total_ref[...] = part

            @pl.when(b > 0)
            def _():
                total_ref[...] += part

            return 0

        lax.fori_loop(0, 4, pre_part, 0)
        for i in range(N_Z):
            pre[i] = total_ref[i * block : (i + 1) * block, :]
        for copy in come:
            copy.wait()
        for source, (firsts, _) in zip(packed, pieces):
            for i, first in enumerate(firsts):
                value = source[8 * i : 8 * i + 8, width:]
                top = first * own
                for j in range(own - 1):
                    spot_j = slice(j * tail, (j + 1) * tail)
                    grd[top + own - 1 : top + own, spot_j] = value[j : j + 1]

        def columns(c, _):
            where = pl.ds(pl.multiple_of(c * tail, tail), tail)
            for source, (firsts, _) in zip(packed, pieces):
                for i, first in enumerate(firsts):
                    top = first * own
                    grd[top : top + own - 1, where] = source[8 * i : 8 * i + 8, where]
            return 0

        lax.fori_loop(0, own - 1, columns, 0)
        gone = [pltpu.make_async_copy(grd, grd_out, sems.at[0])]
        gone[0].start()
        g[...] = jnp.zeros_like(g)

        def grad_part(b, _):
            g[...] += jnp.dot(grd[:, at(b)], wt[b, :, 2 * hid :], preferred_element_type=F32)
            return 0

        lax.fori_loop(0, 4, grad_part, 0)
        for dz in range(N_Z):
            gate_pre, up_pre = pre[spot(dz), :, :hid], pre[spot(dz), :, hid:]
            rows = [slice((dy * N_Z + dz) * unit, (dy * N_Z + dz + 1) * unit) for dy in range(N_Y)]
            grad = jnp.concatenate([g[r, :] for r in rows], axis=0)
            sigma = jax.nn.sigmoid(gate_pre)
            swish = gate_pre * sigma
            hidden = (swish * up_pre).astype(BF)
            up_grad = (grad * swish).astype(BF)
            gate_grad = (grad * up_pre * sigma * (1.0 + gate_pre * (1.0 - sigma))).astype(BF)
            both = jnp.concatenate([gate_grad, up_grad], axis=1)
            first_ref[spot(dz)] = both
            by_z[dz * block : (dz + 1) * block, :] = both
            for dy in range(N_Y):
                hidden_ref[rows[dy], :] = hidden[dy * unit : (dy + 1) * unit]
        for copy in come_w:
            copy.wait()

        def send(b, dz):
            there = out.at[spot(dz), :, pl.ds(pl.multiple_of(b * cols, cols), cols)]
            return pltpu.make_async_copy(held.at[b, dz], there, out_sems.at[b, dz])

        def spread_part(b, _):
            part = jnp.dot(by_z[...], w[b], preferred_element_type=F32).astype(BF)
            for dz in range(N_Z):
                held[b, dz] = part[dz * block : (dz + 1) * block]
                send(b, dz).start()
            return 0

        lax.fori_loop(0, 4, spread_part, 0)

        def sent(i, _):
            send(i // N_Z, i % N_Z).wait()
            return 0

        lax.fori_loop(0, 4 * N_Z, sent, 0)
        for copy in gone:
            copy.wait()

    first, grd, hidden, sums = call(
        kernel,
        [
            jax.ShapeDtypeStruct((N_Z, block, 2 * hid), BF),
            jax.ShapeDtypeStruct((total, width), BF),
            jax.ShapeDtypeStruct((total, hid), BF),
            jax.ShapeDtypeStruct((N_Z, block, width), BF),
        ],
        [SCALARS] * 2 + [ANYWHERE] * (n + 13),
        8 * total * width + 12 * hid * width,
        flops=10 * total * hid * width,
        limit=BIG_LIMIT,
        out_specs=[WHOLE, ANYWHERE, WHOLE, ANYWHERE],
        scratch_shapes=[
            pltpu.VMEM((8 * len(firsts), width + tail), BF) for firsts, _ in pieces
        ]
        + [
            pltpu.VMEM((4, total, cols), BF),
            pltpu.VMEM((4, cols, 3 * hid), BF),
            pltpu.VMEM((4, 2 * hid, cols), BF),
            pltpu.VMEM((total, width), BF),
            pltpu.VMEM((total, hid), F32),
            pltpu.VMEM((total, 2 * hid), F32),
            pltpu.VMEM((N_Z, block, 2 * hid), F32),
            pltpu.VMEM((total, 2 * hid), BF),
            pltpu.VMEM((4, N_Z, block, cols), BF),
            pltpu.SemaphoreType.DMA((n + 16,)),
            pltpu.SemaphoreType.DMA((4, N_Z)),
        ],
    )(z, place, tok, *flat, *turned, *[half for pair in blocks for half in pair])
    return first.reshape(total, 2 * hid), grd, hidden, sums.reshape(total, width)


def weight_grads(order, lefts, rights):
    hid, cols, n = lefts[0].shape[1], rights[0].shape[1] // 4, len(lefts)
    rows = lefts[0].shape[0]

    def kernel(order_ref, *refs):
        give_ref, keep_ref, held, turned_ref, sems = refs[2 * n :]
        for b in range(4):
            where = pl.ds(pl.multiple_of(order_ref[b] * cols, cols), cols)
            for i, right in enumerate(refs[n : 2 * n]):
                there = held.at[b, i * rows : (i + 1) * rows, :]
                pltpu.make_async_copy(right.at[:, where], there, sems.at[b, i]).start()
        left = jnp.concatenate([ref[...] for ref in refs[:n]], axis=0).T
        turned_ref[...] = left

        def column_part(b, _):
            for i, right in enumerate(refs[n : 2 * n]):
                there = held.at[b, i * rows : (i + 1) * rows, :]
                pltpu.make_async_copy(right.at[:, :cols], there, sems.at[b, i]).wait()
            part = jnp.dot(turned_ref[...], held[b], preferred_element_type=F32)

            @pl.when(b < 2)
            def _():
                give_ref[b] = part.astype(BF)

            @pl.when(b >= 2)
            def _():
                keep_ref[b - 2] = part

            return 0

        lax.fori_loop(0, 4, column_part, 0)

    return call(
        kernel,
        [jax.ShapeDtypeStruct((2, hid, cols), BF), jax.ShapeDtypeStruct((2, hid, cols), F32)],
        [SCALARS] + [WHOLE] * n + [ANYWHERE] * n,
        12 * hid * cols + 8 * n * rows * cols,
        flops=8 * n * rows * hid * cols,
        limit=BIG_LIMIT,
        scratch_shapes=[
            pltpu.VMEM((4, n * rows, cols), BF),
            pltpu.VMEM((hid, n * rows), BF),
            pltpu.SemaphoreType.DMA((4, n)),
        ],
    )(order, *lefts, *rights)


def per_device(tokens, out_grad, gate_weight, up_weight, down_weight, block_mask, assignment):
    own, width = tokens.shape
    hid, cols = gate_weight.shape
    panels, col_blocks = hid // BLK, cols // BLK
    unit = 2 * own
    x_hi, core, z = (lax.axis_index(a) for a in ("x_hi", "core", "z"))
    place = jnp.stack(
        [2 * x_hi + core, 2 * (1 - x_hi) + core, 2 * x_hi + 1 - core, 2 * (1 - x_hi) + 1 - core]
    )
    tie = lax.optimization_barrier

    panel_ids = lax.broadcasted_iota(jnp.int32, (panels, block_mask.shape[1]), 1)
    selector = (assignment[:, None] == panel_ids).astype(F32)
    slot_mask = jnp.einsum("sp,mpb->msb", selector, block_mask.astype(F32))
    slot_mask = lax.dynamic_slice_in_dim(slot_mask, place[0] * col_blocks, col_blocks, 2)
    keep = jnp.repeat(slot_mask, BLK, axis=2)

    mine = pack([tokens, out_grad])
    tok16, grd16 = by_array(mine, fetch(mine, "x_lo", 1))
    kept = mask_weights([gate_weight, up_weight, down_weight], keep.reshape(-1, cols))
    tok16, grd16, kept = tie((tok16, grd16, kept))

    t1, t3, t2 = fetch(tok16, "y", 1), fetch(tok16, "y", -1), fetch(tok16, "y", 2)
    z1, z7 = fetch(grd16, "z", 1), fetch(grd16, "z", -1)
    z1, z7, t1, t3, t2 = tie((z1, z7, t1, t3, t2))
    tok = unpack(
        [([2 * dy, 2 * dy + 1], [t]) for dy, t in enumerate((tok16, t1, t2, t3))], N_X * N_Y, own, width
    )
    tok = lax.all_gather(tok, "z", axis=0, tiled=True)
    away = [fetch(kept[0], "x_hi", 1)]
    beside_kept = [fetch(half, "core", 1) for half in kept]
    z2, z6, beside_kept = tie((fetch(z1, "z", 1), fetch(z7, "z", -1), beside_kept))
    near = stack([grd16, z1, z7, z2, z6])
    cut = near.shape[1] // 2
    n1, n3 = fetch(near, "y", 1), fetch(near, "y", -1)
    z3, z5 = tie((fetch(z2, "z", 1), fetch(z6, "z", -1)))
    z4 = [fetch(z3[:, :cut], "z", 1), fetch(z5[:, cut:], "z", -1)]
    z4, later = tie((z4, kept[1]))
    rest = join([[z3], [z5], z4])
    kept_turned = turn(kept)
    n1, n3, rest, kept_turned, away = tie((n1, n3, rest, kept_turned, away))
    n2 = [fetch(n1[:, :cut], "y", 1), fetch(n3[:, cut:], "y", -1)]
    r1, r3 = fetch(rest, "y", 1), fetch(rest, "y", -1)
    away = [away[0], fetch(later, "x_hi", 1)]
    n2, r1, r3, away = tie((n2, r1, r3, away))
    r2 = [fetch(r1[:, :cut], "y", 1), fetch(r3[:, cut:], "y", -1)]
    beside_away = [fetch(half, "core", 1) for half in away]
    blocks = [kept, away, beside_kept, beside_away]
    turned = [kept_turned, turn(away), turn(beside_kept), turn(beside_away)]
    tok, r2, turned = tie((tok, r2, turned))
    pieces = []
    for dy, n, r in ((0, [near], [rest]), (1, [n1], [r1]), (2, n2, r2), (3, [n3], [r3])):
        for offsets, held in (((0, 1, 7, 2, 6), n), ((3, 5, 4), r)):
            pieces.append(([2 * (N_Z * dy + dz) + dx for dz in offsets for dx in range(N_X)], held))
    by_z, grd, hidden, total = middle(z[None], place, tok, pieces, turned, blocks, own)
    total = lax.psum_scatter(total, "z", scatter_dimension=0, tiled=True)

    order = place[::-1]
    give_a, keep_a = weight_grads(order, [by_z], [tok])
    give_a = fetch(give_a, "core", 1)
    give_b, keep_b = weight_grads(order, [hidden], [grd])
    give_a, give_b, keep_b = tie((give_a, give_b, keep_b))
    far_a = fetch((keep_a[0] + give_a[0].astype(F32)).astype(BF), "x_hi", 1)
    give_b = fetch(give_b, "core", 1)
    far_b = fetch((keep_b[0] + give_b[0].astype(F32)).astype(BF), "x_hi", 1)

    def finish(keep_sum, give, far, rows):
        total = keep_sum[1] + give[1].astype(F32) + far.astype(F32)
        total = total.reshape(-1, panels, BLK, cols) * rows[:, :, None, :]
        return total.astype(BF).reshape(-1, hid, cols)

    gate_up_grad = finish(keep_a, give_a, far_a, keep[:2])
    down_grad = finish(keep_b, give_b, far_b, keep[2:])

    parts = deal(total, own)
    parts = [parts[0]] + [fetch(parts[dy], "y", -dy) for dy in (1, 3, 2)]

    def last(*parts):
        both = sum(part.astype(F32) for part in parts)
        return both[: own - 1], both[own - 1 :]

    parts, gate_up_grad, down_grad = tie((parts, gate_up_grad, down_grad))
    mine, other = local(last, *parts)
    input_grad = place_rows(place, mine, fetch(other, "x_lo", 1))
    return (input_grad, gate_up_grad[0], gate_up_grad[1], down_grad[0])


def solution(mesh):
    fine = Mesh(mesh.devices.reshape(SIZES), AXES)
    rows = P(DP + MP, None)
    weights = P(MP, DP)
    return jax.shard_map(
        per_device,
        mesh=fine,
        in_specs=(rows, rows, weights, weights, weights, P(), P(MP)),
        out_specs=(rows, weights, weights, weights),
        check_vma=False,
    )
```

profile of v0, /device:TPU:2, one launch (start us, length us, event | category | flops | bytes accessed | tf_op | source)
XLA Modules:
  0.0 194.1 jit_solution(13932268502321377410)
XLA Ops:
  9.1 2.4 %collective-permute-start = (bf16[16,4608]{1,0:T(8,128)(2,1)S(1)}, bf16[16,4608]{1,0:T(8,128)(2,1)S(1)}, u32[]{:S(2)}, u32[]{:S(2)}) collective-permute-start(bf16[16,4608]{1,0:T(8,128)(2,1)S(1)} %shard_map.102.mine_ref), channel_id=1, source_target_pairs={{0,32},{32,0},{1,33},{33,1},{2,34},{34,2},{3,35},{35,3},{4,36},{36... | collective-permute-start | bytes 442376 | tf_op jit(solution)/shard_map/ppermute | solution.py:52
  13.6 1.0 copy-done.13
  14.7 1.0 copy-done.14
  16.0 1.8 collective-permute-start.3
  18.1 1.9 collective-permute-start.5
  20.1 5.9 %collective-permute-start.1 = (bf16[16,4608]{1,0:T(8,128)(2,1)S(1)}, bf16[16,4608]{1,0:T(8,128)(2,1)S(1)}, u32[]{:S(2)}, u32[]{:S(2)}) collective-permute-start(bf16[16,4608]{1,0:T(8,128)(2,1)S(1)} %get-tuple-element.72.refs_0_), channel_id=1, source_target_pairs={{0,7},{1,0},{2,1},{3,2},{4,3},{5,4},{6,5},{7,6},{8,15},{9,8},{10,9... | collective-permute-start | bytes 442376 | tf_op jit(solution)/shard_map/ppermute | solution.py:52
  26.8 1.8 collective-permute-done.1.refs_1_
  28.6 3.8 %collective-permute-done.2.refs_2_ = bf16[16,4608]{1,0:T(8,128)(2,1)} collective-permute-done((bf16[16,4608]{1,0:T(8,128)(2,1)S(1)}, bf16[16,4608]{1,0:T(8,128)(2,1)}, u32[]{:S(2)}, u32[]{:S(2)}) %collective-permute-start.2) | collective-permute-done | bytes 147488 | tf_op jit(solution)/shard_map/ppermute | solution.py:52
  34.3 1.7 collective-permute-start.7
  36.1 2.1 %collective-permute-start.16 = (bf16[384,1024]{1,0:T(8,128)(2,1)S(1)}, bf16[384,1024]{1,0:T(8,128)(2,1)}, u32[]{:S(2)}, u32[]{:S(2)}) collective-permute-start(bf16[384,1024]{1,0:T(8,128)(2,1)S(1)} %get-tuple-element.78.top.refs_14_), channel_id=1, source_target_pairs={{0,128},{128,0},{1,129},{129,1},{2,130},{130,2},{3,131},{131,3},{4... | collective-permute-start | bytes 2359304 | tf_op jit(solution)/shard_map/ppermute | solution.py:52
  38.2 1.7 collective-permute-done.6.refs_3_
  39.9 1.4 collective-permute-done.7.refs_4_
  41.4 1.1 shard_map.106.refs_0_
  42.5 1.1 collective-permute-start.10
  44.7 2.0 %collective-permute-start.13 = (bf16[16,4608]{1,0:T(8,128)(2,1)S(1)}, bf16[16,4608]{1,0:T(8,128)(2,1)S(1)}, u32[]{:S(2)}, u32[]{:S(2)}) collective-permute-start(bf16[16,4608]{1,0:T(8,128)(2,1)S(1)} %collective-permute-done.7.refs_4_), channel_id=1, source_target_pairs={{0,1},{1,2},{2,3},{3,4},{4,5},{5,6},{6,7},{7,0},{8,9},{9,10},{10,1... | collective-permute-start | bytes 442376 | tf_op jit(solution)/shard_map/ppermute | solution.py:52
  46.7 7.1 %collective-permute-done.12.refs_0_ = bf16[16,4608]{1,0:T(8,128)(2,1)S(1)} collective-permute-done((bf16[16,4608]{1,0:T(8,128)(2,1)S(1)}, bf16[16,4608]{1,0:T(8,128)(2,1)S(1)}, u32[]{:S(2)}, u32[]{:S(2)}) %collective-permute-start.12) | collective-permute-done | bytes 147488 | tf_op jit(solution)/shard_map/ppermute | solution.py:52
  53.8 1.3 collective-permute-done.13.refs_1_
  55.3 1.9 collective-permute-start.15
  57.1 3.9 %collective-permute-done.14.refs_2_ = bf16[16,2304]{1,0:T(8,128)(2,1)S(1)} collective-permute-done((bf16[16,2304]{1,0:T(8,128)(2,1)S(1)}, bf16[16,2304]{1,0:T(8,128)(2,1)S(1)}, u32[]{:S(2)}, u32[]{:S(2)}) %collective-permute-start.14) | collective-permute-done | bytes 73760 | tf_op jit(solution)/shard_map/ppermute | solution.py:52
  61.0 1.5 collective-permute-done.15.refs_3_
  62.5 2.3 %collective-permute-start.21 = (bf16[384,1024]{1,0:T(8,128)(2,1)S(1)}, bf16[384,1024]{1,0:T(8,128)(2,1)}, u32[]{:S(2)}, u32[]{:S(2)}) collective-permute-start(bf16[384,1024]{1,0:T(8,128)(2,1)S(1)} %get-tuple-element.90.bottom.refs_15_), channel_id=1, source_target_pairs={{0,128},{128,0},{1,129},{129,1},{2,130},{130,2},{3,131},{131,3},{4... | collective-permute-start | bytes 2359304 | tf_op jit(solution)/shard_map/ppermute | solution.py:52
  65.3 1.1 copy-done
  66.6 2.0 %collective-permute-start.19 = (bf16[48,4608]{1,0:T(8,128)(2,1)S(1)}, bf16[48,4608]{1,0:T(8,128)(2,1)S(1)}, u32[]{:S(2)}, u32[]{:S(2)}) collective-permute-start(bf16[48,4608]{1,0:T(8,128)(2,1)S(1)} %shard_map.107.refs_1_), channel_id=1, source_target_pairs={{0,24},{8,0},{16,8},{24,16},{1,25},{9,1},{17,9},{25,17},{2,26},{10... | collective-permute-start | bytes 1327112 | tf_op jit(solution)/shard_map/ppermute | solution.py:52
  68.7 3.2 %collective-permute-start.17 = (bf16[80,2304]{1,0:T(8,128)(2,1)S(1)}, bf16[80,2304]{1,0:T(8,128)(2,1)S(1)}, u32[]{:S(2)}, u32[]{:S(2)}) collective-permute-start(bf16[80,2304]{1,0:T(8,128)(2,1)S(1)} %slice.62), channel_id=1, source_target_pairs={{0,24},{8,0},{16,8},{24,16},{1,25},{9,1},{17,9},{25,17},{2,26},{10... | collective-permute-start | bytes 1105928 | tf_op jit(solution)/shard_map/ppermute | solution.py:52
  72.0 9.0 %collective-permute-done.21.bottom.refs_17_ = bf16[384,1024]{1,0:T(8,128)(2,1)} collective-permute-done((bf16[384,1024]{1,0:T(8,128)(2,1)S(1)}, bf16[384,1024]{1,0:T(8,128)(2,1)}, u32[]{:S(2)}, u32[]{:S(2)}) %collective-permute-start.21) | collective-permute-done | bytes 786464 | tf_op jit(solution)/shard_map/ppermute | solution.py:52
  81.1 2.5 %collective-permute-done.17.refs_4_ = bf16[80,2304]{1,0:T(8,128)(2,1)S(1)} collective-permute-done((bf16[80,2304]{1,0:T(8,128)(2,1)S(1)}, bf16[80,2304]{1,0:T(8,128)(2,1)S(1)}, u32[]{:S(2)}, u32[]{:S(2)}) %collective-permute-start.17) | collective-permute-done | bytes 368672 | tf_op jit(solution)/shard_map/ppermute | solution.py:52
  83.5 2.7 %collective-permute-done.18.refs_5_ = bf16[80,2304]{1,0:T(8,128)(2,1)S(1)} collective-permute-done((bf16[80,2304]{1,0:T(8,128)(2,1)S(1)}, bf16[80,2304]{1,0:T(8,128)(2,1)S(1)}, u32[]{:S(2)}, u32[]{:S(2)}) %collective-permute-start.18) | collective-permute-done | bytes 368672 | tf_op jit(solution)/shard_map/ppermute | solution.py:52
  89.5 1.7 collective-permute-start.23
  91.8 1.1 copy-done.1
  92.9 1.8 shard_map.109.refs_11_
  94.7 1.2 copy-done.2
  96.4 1.1 copy-done.3
  98.1 14.9 %shard_map.112 = (bf16[8,72,512]{2,1,0:T(8,128)(2,1)}, bf16[576,4096]{1,0:T(8,128)(2,1)}, bf16[576,256]{1,0:T(8,128)(2,1)S(1)}, bf16[8,72,4096]{2,1,0:T(8,128)(2,1)}) custom-call(s32[1]{0:T(128)} %bitcast.4.z_ref, s32[4]{0:T(128)S(1)} %pad_add_fusion.place_ref, bf16[576,4096]{1,0:T(8,128)(2,1)} %all-gather.2.cloned.1.call-done.tok_ref.refs_1_, ...), custom_call_target="tpu_custom_call" | custom-call | flops 6039797760 | bytes 31457280 | tf_op jit(solution)/shard_map/pallas_call | solution.py:325
  114.0 8.9 %shard_map.114 = (bf16[2,512,1024]{2,1,0:T(8,128)(2,1)}, f32[2,512,1024]{2,1,0:T(8,128)}) custom-call(s32[4]{0:T(128)S(1)} %rev.3.order_ref, bf16[576,512]{1,0:T(8,128)(2,1)S(1)} %bitcast.52, bf16[576,4096]{1,0:T(8,128)(2,1)} %all-gather.2.cloned.1.call-done.tok_ref.refs_1_), custom_call_target="tpu_custom_call" | custom-call | flops 2415919104 | bytes 11010048 | tf_op jit(solution)/shard_map/pallas_call | solution.py:390
  123.0 6.0 %shard_map.115 = (bf16[2,256,1024]{2,1,0:T(8,128)(2,1)S(1)}, f32[2,256,1024]{2,1,0:T(8,128)}) custom-call(s32[4]{0:T(128)S(1)} %rev.3.order_ref, bf16[576,256]{1,0:T(8,128)(2,1)S(1)} %get-tuple-element.115.refs_0_, bf16[576,4096]{1,0:T(8,128)(2,1)} %get-tuple-element.116.refs_1_), custom_call_target="tpu_custom_call" | custom-call | flops 1207959552 | bytes 7864320 | tf_op jit(solution)/shard_map/pallas_call | solution.py:390
  129.6 1.4 fusion.1
  131.0 1.5 collective-permute-start.30
  133.5 2.1 %collective-permute-start.32 = (bf16[256,1024]{1,0:T(8,128)(2,1)S(1)}, bf16[256,1024]{1,0:T(8,128)(2,1)S(1)}, u32[]{:S(2)}, u32[]{:S(2)}) collective-permute-start(bf16[256,1024]{1,0:T(8,128)(2,1)S(1)} %fusion.3), channel_id=1, source_target_pairs={{0,128},{128,0},{1,129},{129,1},{2,130},{130,2},{3,131},{131,3},{4... | collective-permute-start | bytes 1572872 | tf_op jit(solution)/shard_map/ppermute | solution.py:52
  135.7 32.7 %reduce-scatter.2.cloned.1.call-done.ref = bf16[72,4096]{1,0:T(8,128)(2,1)} async-done(((bf16[576,4096]{1,0:T(8,128)(2,1)}), bf16[72,4096]{1,0:T(8,128)(2,1)}) %reduce-scatter.2.cloned.1.call-update) | async-done | bytes 589840 | tf_op jit(solution)/shard_map/reduce_scatter | solution.py:460
  168.4 1.1 copy-done.11
  169.7 1.6 collective-permute-start.26
  171.3 1.8 collective-permute-start.27
  173.0 1.8 collective-permute-start.28
  174.8 2.4 %bitcast_add_fusion = f32[512,1024]{1,0:T(8,128)S(1)} fusion(bf16[512,1024]{1,0:T(8,128)(2,1)} %collective-permute-done.30, f32[2,512,1024]{2,1,0:T(8,128)} %get-tuple-element.113, bf16[2,512,1024]{2,1,0:T(8,128)(2,1)S(1)} %copy-done.26), kind=kLoop, calls=%fused_computation.2 | loop fusion | flops 2097152 | bytes 6291456 | tf_op jit(solution)/shard_map/add | solution.py:472
  177.5 1.3 copy-done.24
  179.1 1.1 fusion.2
  182.5 3.5 %collective-permute-done.33.other_ref = f32[8,4608]{1,0:T(8,128)S(1)} collective-permute-done((f32[8,4608]{1,0:T(8,128)S(1)}, f32[8,4608]{1,0:T(8,128)S(1)}, u32[]{:S(2)}, u32[]{:S(2)}) %collective-permute-start.33) | collective-permute-done | bytes 147488 | tf_op jit(solution)/shard_map/ppermute | solution.py:52
  186.1 1.2 shard_map.117
  (135 shorter events, 20.1 us)
Async XLA Ops:
  7.2 90.9 %all-gather.2.cloned.1.call-start = ((), (), s32[]{:S(2)}) async-start(), calls=%async_computation.1 | async-start | bytes 5308416 | tf_op jit(solution)/shard_map/all_gather | solution.py:433
  9.1 6.9 %collective-permute-start = (bf16[16,4608]{1,0:T(8,128)(2,1)S(1)}, bf16[16,4608]{1,0:T(8,128)(2,1)S(1)}, u32[]{:S(2)}, u32[]{:S(2)}) collective-permute-start(bf16[16,4608]{1,0:T(8,128)(2,1)S(1)} %shard_map.102.mine_ref), channel_id=1, source_target_pairs={{0,32},{32,0},{1,33},{33,1},{2,34},{34,2},{3,35},{35,3},{4,36},{36... | collective-permute-start | bytes 442376 | tf_op jit(solution)/shard_map/ppermute | solution.py:52
  12.5 120.0 %copy-start.33 = (f32[3,2,8]{2,1,0:T(2,128)}, f32[3,2,8]{2,1,0:T(2,128)S(1)}, u32[]{:S(2)}) copy-start(f32[3,2,8]{2,1,0:T(2,128)S(1)} %dynamic-slice_bitcast_fusion) | copy-start | bytes 580
  16.0 49.3 %copy-start.4 = (bf16[384,1024]{1,0:T(8,128)(2,1)}, bf16[384,1024]{1,0:T(8,128)(2,1)S(1)}, u32[]{:S(2)}) copy-start(bf16[384,1024]{1,0:T(8,128)(2,1)S(1)} %get-tuple-element.78.top.refs_14_) | copy-start | bytes 2359300
  16.0 49.3 %copy-start.5 = (bf16[384,1024]{1,0:T(8,128)(2,1)}, bf16[384,1024]{1,0:T(8,128)(2,1)S(1)}, u32[]{:S(2)}) copy-start(bf16[384,1024]{1,0:T(8,128)(2,1)S(1)} %get-tuple-element.90.bottom.refs_15_) | copy-start | bytes 2359300
  16.0 9.9 %collective-permute-start.3 = (bf16[16,4608]{1,0:T(8,128)(2,1)S(1)}, bf16[16,4608]{1,0:T(8,128)(2,1)S(1)}, u32[]{:S(2)}, u32[]{:S(2)}) collective-permute-start(bf16[16,4608]{1,0:T(8,128)(2,1)S(1)} %get-tuple-element.71.refs_0_), channel_id=1, source_target_pairs={{0,24},{8,0},{16,8},{24,16},{1,25},{9,1},{17,9},{25,17},{2,26},{10... | collective-permute-start | bytes 442376 | tf_op jit(solution)/shard_map/ppermute | solution.py:52
  17.9 8.9 %collective-permute-start.4 = (bf16[16,4608]{1,0:T(8,128)(2,1)S(1)}, bf16[16,4608]{1,0:T(8,128)(2,1)S(1)}, u32[]{:S(2)}, u32[]{:S(2)}) collective-permute-start(bf16[16,4608]{1,0:T(8,128)(2,1)S(1)} %get-tuple-element.71.refs_0_), channel_id=1, source_target_pairs={{0,8},{8,16},{16,24},{24,0},{1,9},{9,17},{17,25},{25,1},{2,10},{10... | collective-permute-start | bytes 442376 | tf_op jit(solution)/shard_map/ppermute | solution.py:52
  18.1 8.7 %collective-permute-start.5 = (bf16[16,4608]{1,0:T(8,128)(2,1)S(1)}, bf16[16,4608]{1,0:T(8,128)(2,1)S(1)}, u32[]{:S(2)}, u32[]{:S(2)}) collective-permute-start(bf16[16,4608]{1,0:T(8,128)(2,1)S(1)} %get-tuple-element.71.refs_0_), channel_id=1, source_target_pairs={{0,16},{8,24},{16,0},{24,8},{1,17},{9,25},{17,1},{25,9},{2,18},{10... | collective-permute-start | bytes 442376 | tf_op jit(solution)/shard_map/ppermute | solution.py:52
  20.1 8.5 %collective-permute-start.1 = (bf16[16,4608]{1,0:T(8,128)(2,1)S(1)}, bf16[16,4608]{1,0:T(8,128)(2,1)S(1)}, u32[]{:S(2)}, u32[]{:S(2)}) collective-permute-start(bf16[16,4608]{1,0:T(8,128)(2,1)S(1)} %get-tuple-element.72.refs_0_), channel_id=1, source_target_pairs={{0,7},{1,0},{2,1},{3,2},{4,3},{5,4},{6,5},{7,6},{8,15},{9,8},{10,9... | collective-permute-start | bytes 442376 | tf_op jit(solution)/shard_map/ppermute | solution.py:52
  25.9 6.5 %collective-permute-start.2 = (bf16[16,4608]{1,0:T(8,128)(2,1)S(1)}, bf16[16,4608]{1,0:T(8,128)(2,1)}, u32[]{:S(2)}, u32[]{:S(2)}) collective-permute-start(bf16[16,4608]{1,0:T(8,128)(2,1)S(1)} %get-tuple-element.72.refs_0_), channel_id=1, source_target_pairs={{0,1},{1,2},{2,3},{3,4},{4,5},{5,6},{6,7},{7,0},{8,9},{9,10},{10,1... | collective-permute-start | bytes 442376 | tf_op jit(solution)/shard_map/ppermute | solution.py:52
  33.4 135.0 %reduce-scatter.2.cloned.1.call-start = ((), (), s32[]{:S(2)}) async-start(), calls=%async_computation.2 | async-start | bytes 5308416 | tf_op jit(solution)/shard_map/reduce_scatter | solution.py:460
  33.5 7.9 %collective-permute-start.8 = (bf16[384,1024]{1,0:T(8,128)(2,1)S(1)}, bf16[384,1024]{1,0:T(8,128)(2,1)S(1)}, u32[]{:S(2)}, u32[]{:S(2)}) collective-permute-start(bf16[384,1024]{1,0:T(8,128)(2,1)S(1)} %get-tuple-element.78.top.refs_14_), channel_id=1, source_target_pairs={{0,64},{64,0},{1,65},{65,1},{2,66},{66,2},{3,67},{67,3},{4,68},{68... | collective-permute-start | bytes 2359304 | tf_op jit(solution)/shard_map/ppermute | solution.py:52
  33.6 7.8 %collective-permute-start.9 = (bf16[384,1024]{1,0:T(8,128)(2,1)S(1)}, bf16[384,1024]{1,0:T(8,128)(2,1)S(1)}, u32[]{:S(2)}, u32[]{:S(2)}) collective-permute-start(bf16[384,1024]{1,0:T(8,128)(2,1)S(1)} %get-tuple-element.90.bottom.refs_15_), channel_id=1, source_target_pairs={{0,64},{64,0},{1,65},{65,1},{2,66},{66,2},{3,67},{67,3},{4,68},{68... | collective-permute-start | bytes 2359304 | tf_op jit(solution)/shard_map/ppermute | solution.py:52
  34.1 5.9 %collective-permute-start.6 = (bf16[16,4608]{1,0:T(8,128)(2,1)S(1)}, bf16[16,4608]{1,0:T(8,128)(2,1)S(1)}, u32[]{:S(2)}, u32[]{:S(2)}) collective-permute-start(bf16[16,4608]{1,0:T(8,128)(2,1)S(1)} %collective-permute-done.1.refs_1_), channel_id=1, source_target_pairs={{0,7},{1,0},{2,1},{3,2},{4,3},{5,4},{6,5},{7,6},{8,15},{9,8},{10,9... | collective-permute-start | bytes 442376 | tf_op jit(solution)/shard_map/ppermute | solution.py:52
  34.3 7.0 %collective-permute-start.7 = (bf16[16,4608]{1,0:T(8,128)(2,1)}, bf16[16,4608]{1,0:T(8,128)(2,1)S(1)}, u32[]{:S(2)}, u32[]{:S(2)}) collective-permute-start(bf16[16,4608]{1,0:T(8,128)(2,1)} %collective-permute-done.2.refs_2_), channel_id=1, source_target_pairs={{0,1},{1,2},{2,3},{3,4},{4,5},{5,6},{6,7},{7,0},{8,9},{9,10},{10,1... | collective-permute-start | bytes 442376 | tf_op jit(solution)/shard_map/ppermute | solution.py:52
  36.1 30.4 %collective-permute-start.16 = (bf16[384,1024]{1,0:T(8,128)(2,1)S(1)}, bf16[384,1024]{1,0:T(8,128)(2,1)}, u32[]{:S(2)}, u32[]{:S(2)}) collective-permute-start(bf16[384,1024]{1,0:T(8,128)(2,1)S(1)} %get-tuple-element.78.top.refs_14_), channel_id=1, source_target_pairs={{0,128},{128,0},{1,129},{129,1},{2,130},{130,2},{3,131},{131,3},{4... | collective-permute-start | bytes 2359304 | tf_op jit(solution)/shard_map/ppermute | solution.py:52
  41.3 50.0 %copy-start.6 = (bf16[384,1024]{1,0:T(8,128)(2,1)}, bf16[384,1024]{1,0:T(8,128)(2,1)S(1)}, u32[]{:S(2)}) copy-start(bf16[384,1024]{1,0:T(8,128)(2,1)S(1)} %collective-permute-done.8.top.refs_18_) | copy-start | bytes 2359300
  41.3 49.9 %copy-start.7 = (bf16[384,1024]{1,0:T(8,128)(2,1)}, bf16[384,1024]{1,0:T(8,128)(2,1)S(1)}, u32[]{:S(2)}) copy-start(bf16[384,1024]{1,0:T(8,128)(2,1)S(1)} %collective-permute-done.9.bottom.refs_19_) | copy-start | bytes 2359300
  42.5 24.0 %copy-start.10 = (bf16[80,4608]{1,0:T(8,128)(2,1)}, bf16[80,4608]{1,0:T(8,128)(2,1)S(1)}, u32[]{:S(2)}) copy-start(bf16[80,4608]{1,0:T(8,128)(2,1)S(1)} %shard_map.106.refs_0_) | copy-start | bytes 2211844
  42.5 24.0 %collective-permute-start.10 = (bf16[80,4608]{1,0:T(8,128)(2,1)S(1)}, bf16[80,4608]{1,0:T(8,128)(2,1)S(1)}, u32[]{:S(2)}, u32[]{:S(2)}) collective-permute-start(bf16[80,4608]{1,0:T(8,128)(2,1)S(1)} %shard_map.106.refs_0_), channel_id=1, source_target_pairs={{0,24},{8,0},{16,8},{24,16},{1,25},{9,1},{17,9},{25,17},{2,26},{10... | collective-permute-start | bytes 2211848 | tf_op jit(solution)/shard_map/ppermute | solution.py:52
  43.7 22.9 %collective-permute-start.11 = (bf16[80,4608]{1,0:T(8,128)(2,1)S(1)}, bf16[80,4608]{1,0:T(8,128)(2,1)S(1)}, u32[]{:S(2)}, u32[]{:S(2)}) collective-permute-start(bf16[80,4608]{1,0:T(8,128)(2,1)S(1)} %shard_map.106.refs_0_), channel_id=1, source_target_pairs={{0,8},{8,16},{16,24},{24,0},{1,9},{9,17},{17,25},{25,1},{2,10},{10... | collective-permute-start | bytes 2211848 | tf_op jit(solution)/shard_map/ppermute | solution.py:52
  44.6 9.2 %collective-permute-start.12 = (bf16[16,4608]{1,0:T(8,128)(2,1)S(1)}, bf16[16,4608]{1,0:T(8,128)(2,1)S(1)}, u32[]{:S(2)}, u32[]{:S(2)}) collective-permute-start(bf16[16,4608]{1,0:T(8,128)(2,1)S(1)} %collective-permute-done.6.refs_3_), channel_id=1, source_target_pairs={{0,7},{1,0},{2,1},{3,2},{4,3},{5,4},{6,5},{7,6},{8,15},{9,8},{10,9... | collective-permute-start | bytes 442376 | tf_op jit(solution)/shard_map/ppermute | solution.py:52
  44.7 10.4 %collective-permute-start.13 = (bf16[16,4608]{1,0:T(8,128)(2,1)S(1)}, bf16[16,4608]{1,0:T(8,128)(2,1)S(1)}, u32[]{:S(2)}, u32[]{:S(2)}) collective-permute-start(bf16[16,4608]{1,0:T(8,128)(2,1)S(1)} %collective-permute-done.7.refs_4_), channel_id=1, source_target_pairs={{0,1},{1,2},{2,3},{3,4},{4,5},{5,6},{6,7},{7,0},{8,9},{9,10},{10,1... | collective-permute-start | bytes 442376 | tf_op jit(solution)/shard_map/ppermute | solution.py:52
  55.1 5.9 %collective-permute-start.14 = (bf16[16,2304]{1,0:T(8,128)(2,1)S(1)}, bf16[16,2304]{1,0:T(8,128)(2,1)S(1)}, u32[]{:S(2)}, u32[]{:S(2)}) collective-permute-start(bf16[16,2304]{1,0:T(8,128)(2,1)S(1)} %slice.60), channel_id=1, source_target_pairs={{0,7},{1,0},{2,1},{3,2},{4,3},{5,4},{6,5},{7,6},{8,15},{9,8},{10,9... | collective-permute-start | bytes 221192 | tf_op jit(solution)/shard_map/ppermute | solution.py:52
  55.3 7.2 %collective-permute-start.15 = (bf16[16,2304]{1,0:T(8,128)(2,1)S(1)}, bf16[16,2304]{1,0:T(8,128)(2,1)S(1)}, u32[]{:S(2)}, u32[]{:S(2)}) collective-permute-start(bf16[16,2304]{1,0:T(8,128)(2,1)S(1)} %slice.61), channel_id=1, source_target_pairs={{0,1},{1,2},{2,3},{3,4},{4,5},{5,6},{6,7},{7,0},{8,9},{9,10},{10,1... | collective-permute-start | bytes 221192 | tf_op jit(solution)/shard_map/ppermute | solution.py:52
  62.5 18.5 %collective-permute-start.21 = (bf16[384,1024]{1,0:T(8,128)(2,1)S(1)}, bf16[384,1024]{1,0:T(8,128)(2,1)}, u32[]{:S(2)}, u32[]{:S(2)}) collective-permute-start(bf16[384,1024]{1,0:T(8,128)(2,1)S(1)} %get-tuple-element.90.bottom.refs_15_), channel_id=1, source_target_pairs={{0,128},{128,0},{1,129},{129,1},{2,130},{130,2},{3,131},{131,3},{4... | collective-permute-start | bytes 2359304 | tf_op jit(solution)/shard_map/ppermute | solution.py:52
  66.5 20.5 %copy-start.15 = (bf16[48,4608]{1,0:T(8,128)(2,1)}, bf16[48,4608]{1,0:T(8,128)(2,1)S(1)}, u32[]{:S(2)}) copy-start(bf16[48,4608]{1,0:T(8,128)(2,1)S(1)} %shard_map.107.refs_1_) | copy-start | bytes 1327108
  66.6 20.6 %copy-start.30 = (bf16[80,4608]{1,0:T(8,128)(2,1)}, bf16[80,4608]{1,0:T(8,128)(2,1)S(1)}, u32[]{:S(2)}) copy-start(bf16[80,4608]{1,0:T(8,128)(2,1)S(1)} %collective-permute-done.11.refs_8_) | copy-start | bytes 2211844
  66.6 20.4 %collective-permute-start.19 = (bf16[48,4608]{1,0:T(8,128)(2,1)S(1)}, bf16[48,4608]{1,0:T(8,128)(2,1)S(1)}, u32[]{:S(2)}, u32[]{:S(2)}) collective-permute-start(bf16[48,4608]{1,0:T(8,128)(2,1)S(1)} %shard_map.107.refs_1_), channel_id=1, source_target_pairs={{0,24},{8,0},{16,8},{24,16},{1,25},{9,1},{17,9},{25,17},{2,26},{10... | collective-permute-start | bytes 1327112 | tf_op jit(solution)/shard_map/ppermute | solution.py:52
  68.6 18.4 %collective-permute-start.20 = (bf16[48,4608]{1,0:T(8,128)(2,1)S(1)}, bf16[48,4608]{1,0:T(8,128)(2,1)S(1)}, u32[]{:S(2)}, u32[]{:S(2)}) collective-permute-start(bf16[48,4608]{1,0:T(8,128)(2,1)S(1)} %shard_map.107.refs_1_), channel_id=1, source_target_pairs={{0,8},{8,16},{16,24},{24,0},{1,9},{9,17},{17,25},{25,1},{2,10},{10... | collective-permute-start | bytes 1327112 | tf_op jit(solution)/shard_map/ppermute | solution.py:52
  68.7 14.8 %collective-permute-start.17 = (bf16[80,2304]{1,0:T(8,128)(2,1)S(1)}, bf16[80,2304]{1,0:T(8,128)(2,1)S(1)}, u32[]{:S(2)}, u32[]{:S(2)}) collective-permute-start(bf16[80,2304]{1,0:T(8,128)(2,1)S(1)} %slice.62), channel_id=1, source_target_pairs={{0,24},{8,0},{16,8},{24,16},{1,25},{9,1},{17,9},{25,17},{2,26},{10... | collective-permute-start | bytes 1105928 | tf_op jit(solution)/shard_map/ppermute | solution.py:52
  72.0 14.3 %collective-permute-start.18 = (bf16[80,2304]{1,0:T(8,128)(2,1)S(1)}, bf16[80,2304]{1,0:T(8,128)(2,1)S(1)}, u32[]{:S(2)}, u32[]{:S(2)}) collective-permute-start(bf16[80,2304]{1,0:T(8,128)(2,1)S(1)} %slice.63), channel_id=1, source_target_pairs={{0,8},{8,16},{16,24},{24,0},{1,9},{9,17},{17,25},{25,1},{2,10},{10... | collective-permute-start | bytes 1105928 | tf_op jit(solution)/shard_map/ppermute | solution.py:52
  87.0 8.9 %collective-permute-start.24 = (bf16[384,1024]{1,0:T(8,128)(2,1)}, bf16[384,1024]{1,0:T(8,128)(2,1)S(1)}, u32[]{:S(2)}, u32[]{:S(2)}) collective-permute-start(bf16[384,1024]{1,0:T(8,128)(2,1)} %collective-permute-done.16.top.refs_16_), channel_id=1, source_target_pairs={{0,64},{64,0},{1,65},{65,1},{2,66},{66,2},{3,67},{67,3},{4,68},{68... | collective-permute-start | bytes 2359304 | tf_op jit(solution)/shard_map/ppermute | solution.py:52
  87.2 8.8 %collective-permute-start.25 = (bf16[384,1024]{1,0:T(8,128)(2,1)}, bf16[384,1024]{1,0:T(8,128)(2,1)S(1)}, u32[]{:S(2)}, u32[]{:S(2)}) collective-permute-start(bf16[384,1024]{1,0:T(8,128)(2,1)} %collective-permute-done.21.bottom.refs_17_), channel_id=1, source_target_pairs={{0,64},{64,0},{1,65},{65,1},{2,66},{66,2},{3,67},{67,3},{4,68},{68... | collective-permute-start | bytes 2359304 | tf_op jit(solution)/shard_map/ppermute | solution.py:52
  88.5 9.1 %collective-permute-start.22 = (bf16[48,2304]{1,0:T(8,128)(2,1)}, bf16[48,2304]{1,0:T(8,128)(2,1)}, u32[]{:S(2)}, u32[]{:S(2)}) collective-permute-start(bf16[48,2304]{1,0:T(8,128)(2,1)} %slice.64), channel_id=1, source_target_pairs={{0,24},{8,0},{16,8},{24,16},{1,25},{9,1},{17,9},{25,17},{2,26},{10... | collective-permute-start | bytes 663560 | tf_op jit(solution)/shard_map/ppermute | solution.py:52
  89.5 8.6 %collective-permute-start.23 = (bf16[48,2304]{1,0:T(8,128)(2,1)}, bf16[48,2304]{1,0:T(8,128)(2,1)}, u32[]{:S(2)}, u32[]{:S(2)}) collective-permute-start(bf16[48,2304]{1,0:T(8,128)(2,1)} %slice.65), channel_id=1, source_target_pairs={{0,8},{8,16},{16,24},{24,0},{1,9},{9,17},{17,25},{25,1},{2,10},{10... | collective-permute-start | bytes 663560 | tf_op jit(solution)/shard_map/ppermute | solution.py:52
  122.9 6.1 %collective-permute-start.29 = (bf16[2,512,1024]{2,1,0:T(8,128)(2,1)}, bf16[2,512,1024]{2,1,0:T(8,128)(2,1)S(1)}, u32[]{:S(2)}, u32[]{:S(2)}) collective-permute-start(bf16[2,512,1024]{2,1,0:T(8,128)(2,1)} %get-tuple-element.114), channel_id=1, source_target_pairs={{0,64},{64,0},{1,65},{65,1},{2,66},{66,2},{3,67},{67,3},{4,68},{68... | collective-permute-start | bytes 6291464 | tf_op jit(solution)/shard_map/ppermute | solution.py:52
  123.0 6.6 %copy-start.22 = (f32[2,512,1024]{2,1,0:T(8,128)S(1)}, f32[2,512,1024]{2,1,0:T(8,128)}, u32[]{:S(2)}) copy-start(f32[2,512,1024]{2,1,0:T(8,128)} %get-tuple-element.113) | copy-start | bytes 12582916
  129.0 3.4 %collective-permute-start.31 = (bf16[2,256,1024]{2,1,0:T(8,128)(2,1)S(1)}, bf16[2,256,1024]{2,1,0:T(8,128)(2,1)S(1)}, u32[]{:S(2)}, u32[]{:S(2)}) collective-permute-start(bf16[2,256,1024]{2,1,0:T(8,128)(2,1)S(1)} %get-tuple-element.121), channel_id=1, source_target_pairs={{0,64},{64,0},{1,65},{65,1},{2,66},{66,2},{3,67},{67,3},{4,68},{68... | collective-permute-start | bytes 3145736 | tf_op jit(solution)/shard_map/ppermute | solution.py:52
  129.6 2.9 %copy-start.23 = (f32[2,256,1024]{2,1,0:T(8,128)S(1)}, f32[2,256,1024]{2,1,0:T(8,128)}, u32[]{:S(2)}) copy-start(f32[2,256,1024]{2,1,0:T(8,128)} %get-tuple-element.120) | copy-start | bytes 6291460
  131.0 43.8 %collective-permute-start.30 = (bf16[512,1024]{1,0:T(8,128)(2,1)}, bf16[512,1024]{1,0:T(8,128)(2,1)}, u32[]{:S(2)}, u32[]{:S(2)}) collective-permute-start(bf16[512,1024]{1,0:T(8,128)(2,1)} %fusion.1), channel_id=1, source_target_pairs={{0,128},{128,0},{1,129},{129,1},{2,130},{130,2},{3,131},{131,3},{4... | collective-permute-start | bytes 3145736 | tf_op jit(solution)/shard_map/ppermute | solution.py:52
  132.5 3.2 %slice-start = ((f32[3,2,8]{2,1,0:T(2,128)}), f32[2,2,8]{2,1,0:T(2,128)S(1)}, s32[]{:S(2)}) async-start(f32[3,2,8]{2,1,0:T(2,128)} %copy-done.33), calls=%async_computation.3 | async-start | bytes 4096 | tf_op jit(solution)/shard_map/slice | solution.py:476
  132.5 42.3 %copy-start.26 = (bf16[2,512,1024]{2,1,0:T(8,128)(2,1)S(1)}, bf16[2,512,1024]{2,1,0:T(8,128)(2,1)}, u32[]{:S(2)}) copy-start(bf16[2,512,1024]{2,1,0:T(8,128)(2,1)} %copy-done.25) | copy-start | bytes 6291460
  133.5 44.1 %collective-permute-start.32 = (bf16[256,1024]{1,0:T(8,128)(2,1)S(1)}, bf16[256,1024]{1,0:T(8,128)(2,1)S(1)}, u32[]{:S(2)}, u32[]{:S(2)}) collective-permute-start(bf16[256,1024]{1,0:T(8,128)(2,1)S(1)} %fusion.3), channel_id=1, source_target_pairs={{0,128},{128,0},{1,129},{129,1},{2,130},{130,2},{3,131},{131,3},{4... | collective-permute-start | bytes 1572872 | tf_op jit(solution)/shard_map/ppermute | solution.py:52
  169.7 10.4 %collective-permute-start.26 = (bf16[16,4608]{1,0:T(8,128)(2,1)S(1)}, bf16[16,4608]{1,0:T(8,128)(2,1)S(1)}, u32[]{:S(2)}, u32[]{:S(2)}) collective-permute-start(bf16[16,4608]{1,0:T(8,128)(2,1)S(1)} %get-tuple-element.109), channel_id=1, source_target_pairs={{0,8},{8,16},{16,24},{24,0},{1,9},{9,17},{17,25},{25,1},{2,10},{10... | collective-permute-start | bytes 442376 | tf_op jit(solution)/shard_map/ppermute | solution.py:52
  171.3 8.9 %collective-permute-start.27 = (bf16[16,4608]{1,0:T(8,128)(2,1)S(1)}, bf16[16,4608]{1,0:T(8,128)(2,1)S(1)}, u32[]{:S(2)}, u32[]{:S(2)}) collective-permute-start(bf16[16,4608]{1,0:T(8,128)(2,1)S(1)} %get-tuple-element.110), channel_id=1, source_target_pairs={{0,24},{8,0},{16,8},{24,16},{1,25},{9,1},{17,9},{25,17},{2,26},{10... | collective-permute-start | bytes 442376 | tf_op jit(solution)/shard_map/ppermute | solution.py:52
  173.0 7.7 %collective-permute-start.28 = (bf16[16,4608]{1,0:T(8,128)(2,1)S(1)}, bf16[16,4608]{1,0:T(8,128)(2,1)S(1)}, u32[]{:S(2)}, u32[]{:S(2)}) collective-permute-start(bf16[16,4608]{1,0:T(8,128)(2,1)S(1)} %get-tuple-element.111), channel_id=1, source_target_pairs={{0,16},{8,24},{16,0},{24,8},{1,17},{9,25},{17,1},{25,9},{2,18},{10... | collective-permute-start | bytes 442376 | tf_op jit(solution)/shard_map/ppermute | solution.py:52
  180.8 5.2 %collective-permute-start.33 = (f32[8,4608]{1,0:T(8,128)S(1)}, f32[8,4608]{1,0:T(8,128)S(1)}, u32[]{:S(2)}, u32[]{:S(2)}) collective-permute-start(f32[8,4608]{1,0:T(8,128)S(1)} %get-tuple-element.127), channel_id=1, source_target_pairs={{0,32},{32,0},{1,33},{33,1},{2,34},{34,2},{3,35},{35,3},{4,36},{36... | collective-permute-start | bytes 442376 | tf_op jit(solution)/shard_map/ppermute | solution.py:52
  (23 other events, 32.0 us)
Sparse Core Ops, SparseCore 0:
  33.5 60.5 all-gather.1
  113.1 55.2 reduce-scatter.1
where the time goes:
time: 195 us; the launch traced here: 194 us
  waiting for transfers between devices  75 us (38%)
  starting transfers between devices  43.5 us (22%)
  Pallas kernels  37 us (19%)
  local copies, waits for them, and re-layouts  17.8 us (9%)
  between operations  14.5 us (7%)
  other arithmetic  5.36 us (3%)
    ppermute x34, starting transfers between devices, fetch(): lax.ppermute(block, axis, [(i, (i - offset) % size) for i in range(size)])  43.4 us
    ppermute x34, waiting for transfers between devices, fetch(): lax.ppermute(block, axis, [(i, (i - offset) % size) for i in range(size)])  42.3 us
    reduce_scatter x1, waiting for transfers between devices, per_device(): total = lax.psum_scatter(total, 'z', scatter_dimension=0, tiled=True)  32.7 us
    unnamed x71, local copies, waits for them, and re-layouts  14.9 us
    pallas_call x2, Pallas kernels, weight_grads(): call(kernel, [jax.ShapeDtypeStruct((2, hid, cols), BF), jax.ShapeDtypeStr...  14.9 us
    pallas_call x1, Pallas kernels, middle(): call(kernel, [jax.ShapeDtypeStruct((N_Z, block, 2 * hid), BF), jax.ShapeD...  14.9 us
  transfers between devices with their start and end apart: 36, of which 16 were waited for; matrix products, arithmetic and copies ran while one was open for 5% of the time, Pallas kernels for 10%

commit v1 on v0

--- a/solution.py
+++ b/solution.py
@@ -54,18 +54,29 @@
 
 def pack(arrays):
     own, width = arrays[0].shape
-    tail, rows = width // (own - 1), own - 1
+    tail, rows, n = width // (own - 1), own - 1, len(arrays)
 
     def kernel(*refs):
-        out = refs[-1]
-        for k, ref in enumerate(refs[:-1]):
-            out[k * rows : (k + 1) * rows, :width] = ref[:rows, :]
+        out, held, sems = refs[n:]
+        come = [pltpu.make_async_copy(refs[k], held.at[k], sems.at[k]) for k in range(n)]
+        for copy in come:
+            copy.start()
+        for k in range(n):
+            come[k].wait()
+            out[k * rows : (k + 1) * rows, :width] = held[k, :rows, :]
             for i in range(rows):
                 spot = k * rows + i
-                out[spot : spot + 1, width:] = ref[rows : rows + 1, i * tail : (i + 1) * tail]
-
-    out = jax.ShapeDtypeStruct((rows * len(arrays), width + tail), BF)
-    return call(kernel, out, [WHOLE] * len(arrays), 4 * own * width * len(arrays))(*arrays)
+                part = held[k, rows : rows + 1, i * tail : (i + 1) * tail]
+                out[spot : spot + 1, width:] = part
+
+    return call(
+        kernel,
+        jax.ShapeDtypeStruct((rows * n, width + tail), BF),
+        [ANYWHERE] * n,
+        4 * own * width * n,
+        limit=BIG_LIMIT,
+        scratch_shapes=[pltpu.VMEM((n, own, width), BF), pltpu.SemaphoreType.DMA((n,))],
+    )(*arrays)
 
 
 def by_array(mine, other):
@@ -152,12 +163,33 @@
 def turn(halves):
     rows, cols = halves[0].shape
 
-    def kernel(top, bottom, out):
-        out[:, :rows] = top[...].T
-        out[:, rows:] = bottom[...].T
-
-    out = jax.ShapeDtypeStruct((cols, 2 * rows), BF)
-    return call(kernel, out, [WHOLE] * 2, 8 * rows * cols)(*halves)
+    def kernel(top, bottom, out, held, turned, sems):
+        come = [
+            pltpu.make_async_copy(half, held.at[i], sems.at[i])
+            for i, half in enumerate((top, bottom))
+        ]
+        for copy in come:
+            copy.start()
+        for i in range(2):
+            come[i].wait()
+            turned[:, i * rows : (i + 1) * rows] = held[i].T
+        gone = pltpu.make_async_copy(turned, out, sems.at[2])
+        gone.start()
+        gone.wait()
+
+    return call(
+        kernel,
+        jax.ShapeDtypeStruct((cols, 2 * rows), BF),
+        [ANYWHERE] * 2,
+        8 * rows * cols,
+        limit=BIG_LIMIT,
+        out_specs=ANYWHERE,
+        scratch_shapes=[
+            pltpu.VMEM((2, rows, cols), BF),
+            pltpu.VMEM((cols, 2 * rows), BF),
+            pltpu.SemaphoreType.DMA((3,)),
+        ],
+    )(*halves)
 
 
 def deal(total, own):
@@ -209,9 +241,9 @@
 
     def kernel(z_ref, place_ref, tok_ref, *refs):
         piece_refs, turned_refs, block_refs = refs[:n], refs[n : n + 4], refs[n + 4 : n + 12]
-        first_ref, grd_out, hidden_ref, out = refs[n + 12 : n + 16]
+        first_out, grd_out, hidden_out, out = refs[n + 12 : n + 16]
         packed = refs[n + 16 : n + 16 + m]
-        x, wt, w, grd, g, total_ref, pre, by_z, held, sems, out_sems = refs[n + 16 + m :]
+        x, wt, w, grd, g, total_ref, pre, by_z, first_ref, hidden_ref, held, sems, out_sems = refs[n + 16 + m :]
 
         def bring(source, target, i):
             copy = pltpu.make_async_copy(source, target, sems.at[i])
@@ -298,6 +330,10 @@
             by_z[dz * block : (dz + 1) * block, :] = both
             for dy in range(N_Y):
                 hidden_ref[rows[dy], :] = hidden[dy * unit : (dy + 1) * unit]
+        gone.append(pltpu.make_async_copy(first_ref, first_out, sems.at[1]))
+        gone.append(pltpu.make_async_copy(hidden_ref, hidden_out, sems.at[2]))
+        for copy in gone[1:]:
+            copy.start()
         for copy in come_w:
             copy.wait()
 
@@ -334,7 +370,7 @@
         8 * total * width + 12 * hid * width,
         flops=10 * total * hid * width,
         limit=BIG_LIMIT,
-        out_specs=[WHOLE, ANYWHERE, WHOLE, ANYWHERE],
+        out_specs=[ANYWHERE] * 4,
         scratch_shapes=[
             pltpu.VMEM((8 * len(firsts), width + tail), BF) for firsts, _ in pieces
         ]
@@ -347,6 +383,8 @@
             pltpu.VMEM((total, 2 * hid), F32),
             pltpu.VMEM((N_Z, block, 2 * hid), F32),
             pltpu.VMEM((total, 2 * hid), BF),
+            pltpu.VMEM((N_Z, block, 2 * hid), BF),
+            pltpu.VMEM((total, hid), BF),
             pltpu.VMEM((4, N_Z, block, cols), BF),
             pltpu.SemaphoreType.DMA((n + 16,)),
             pltpu.SemaphoreType.DMA((4, N_Z)),
@@ -360,14 +398,21 @@
     rows = lefts[0].shape[0]
 
     def kernel(order_ref, *refs):
-        give_ref, keep_ref, held, turned_ref, sems = refs[2 * n :]
+        give_ref, keep_ref, held, left_ref, turned_ref, sems, left_sems = refs[2 * n :]
+        come = [
+            pltpu.make_async_copy(ref, left_ref.at[i], left_sems.at[i])
+            for i, ref in enumerate(refs[:n])
+        ]
+        for copy in come:
+            copy.start()
         for b in range(4):
             where = pl.ds(pl.multiple_of(order_ref[b] * cols, cols), cols)
             for i, right in enumerate(refs[n : 2 * n]):
                 there = held.at[b, i * rows : (i + 1) * rows, :]
                 pltpu.make_async_copy(right.at[:, where], there, sems.at[b, i]).start()
-        left = jnp.concatenate([ref[...] for ref in refs[:n]], axis=0).T
-        turned_ref[...] = left
+        for copy in come:
+            copy.wait()
+        turned_ref[...] = jnp.concatenate([left_ref[i] for i in range(n)], axis=0).T
 
         def column_part(b, _):
             for i, right in enumerate(refs[n : 2 * n]):
@@ -390,14 +435,16 @@
     return call(
         kernel,
         [jax.ShapeDtypeStruct((2, hid, cols), BF), jax.ShapeDtypeStruct((2, hid, cols), F32)],
-        [SCALARS] + [WHOLE] * n + [ANYWHERE] * n,
+        [SCALARS] + [ANYWHERE] * (2 * n),
         12 * hid * cols + 8 * n * rows * cols,
         flops=8 * n * rows * hid * cols,
         limit=BIG_LIMIT,
         scratch_shapes=[
             pltpu.VMEM((4, n * rows, cols), BF),
+            pltpu.VMEM((n, rows, hid), BF),
             pltpu.VMEM((hid, n * rows), BF),
             pltpu.SemaphoreType.DMA((4, n)),
+            pltpu.SemaphoreType.DMA((n,)),
         ],
     )(order, *lefts, *rights)
 
@@ -446,11 +493,11 @@
     n2 = [fetch(n1[:, :cut], "y", 1), fetch(n3[:, cut:], "y", -1)]
     r1, r3 = fetch(rest, "y", 1), fetch(rest, "y", -1)
     away = [away[0], fetch(later, "x_hi", 1)]
-    n2, r1, r3, away = tie((n2, r1, r3, away))
+    n2, r1, r3, away, beside_turned = tie((n2, r1, r3, away, turn(beside_kept)))
     r2 = [fetch(r1[:, :cut], "y", 1), fetch(r3[:, cut:], "y", -1)]
     beside_away = [fetch(half, "core", 1) for half in away]
     blocks = [kept, away, beside_kept, beside_away]
-    turned = [kept_turned, turn(away), turn(beside_kept), turn(beside_away)]
+    turned = [kept_turned, turn(away), beside_turned, turn(beside_away)]
     tok, r2, turned = tie((tok, r2, turned))
     pieces = []
     for dy, n, r in ((0, [near], [rest]), (1, [n1], [r1]), (2, n2, r2), (3, [n3], [r3])):

time: 195 us -> 193 us (0.990)
  local copies, waits for them, and re-layouts: 17.8 us -> 9.24 us
  Pallas kernels: 37 us -> 40.9 us
  other arithmetic: 5.36 us -> 7.38 us
    unnamed x71 -> x51, local copies, waits for them, and re-layouts: 14.9 us -> 7.11 us
    pallas_call x5, Pallas kernels: 3.24 us -> 8.62 us  [the longest x4 8.25 us: turn(): call(kernel, jax.ShapeDtypeStruct((cols, 2 * rows), BF), [ANYWHERE] * 2,...]
  transfers between devices with their start and end apart: 36 -> 36, of which waited for: 16 -> 16; matrix products, arithmetic and copies ran while one was open for 5% -> 5% of each run, Pallas kernels for 10% -> 12%
where the time goes in v1:
time: 193 us
  waiting for transfers between devices  76.5 us (40%)
  starting transfers between devices  43.4 us (22%)
  Pallas kernels  40.9 us (21%)
  between operations  14.5 us (8%)
  local copies, waits for them, and re-layouts  9.24 us (5%)
  other arithmetic  7.38 us (4%)
    ppermute x34, starting transfers between devices, fetch(): lax.ppermute(block, axis, [(i, (i - offset) % size) for i in range(size)])  43.3 us
    ppermute x34, waiting for transfers between devices, fetch(): lax.ppermute(block, axis, [(i, (i - offset) % size) for i in range(size)])  41.9 us
    reduce_scatter x1, waiting for transfers between devices, per_device(): total = lax.psum_scatter(total, 'z', scatter_dimension=0, tiled=True)  34.6 us
    pallas_call x2, Pallas kernels, weight_grads(): call(kernel, [jax.ShapeDtypeStruct((2, hid, cols), BF), jax.ShapeDtypeStr...  15.2 us
    pallas_call x1, Pallas kernels, middle(): call(kernel, [jax.ShapeDtypeStruct((N_Z, block, 2 * hid), BF), jax.ShapeD...  14.2 us
    pallas_call x4, Pallas kernels, turn(): call(kernel, jax.ShapeDtypeStruct((cols, 2 * rows), BF), [ANYWHERE] * 2,...  8.25 us
    unnamed x51, local copies, waits for them, and re-layouts  7.11 us
  transfers between devices with their start and end apart: 36, of which 16 were waited for; matrix products, arithmetic and copies ran while one was open for 5% of the time, Pallas kernels for 12%

profile of v1, /device:TPU:2, one launch (start us, length us, event | category | flops | bytes accessed | tf_op | source)
XLA Modules:
  0.0 192.9 jit_solution(8346165604012526833)
XLA Ops:
  9.4 2.4 %collective-permute-start = (bf16[16,4608]{1,0:T(8,128)(2,1)S(1)}, bf16[16,4608]{1,0:T(8,128)(2,1)S(1)}, u32[]{:S(2)}, u32[]{:S(2)}) collective-permute-start(bf16[16,4608]{1,0:T(8,128)(2,1)S(1)} %shard_map.102.mine_ref), channel_id=1, source_target_pairs={{0,32},{32,0},{1,33},{33,1},{2,34},{34,2},{3,35},{35,3},{4,36},{36... | collective-permute-start | bytes 442376 | tf_op jit(solution)/shard_map/ppermute | solution.py:52
  12.9 1.0 copy-done.8
  14.0 1.0 copy-done.9
  15.0 1.0 copy-done.10
  16.4 1.8 collective-permute-start.3
  18.5 1.9 collective-permute-start.5
  20.4 5.9 %collective-permute-start.1 = (bf16[16,4608]{1,0:T(8,128)(2,1)S(1)}, bf16[16,4608]{1,0:T(8,128)(2,1)S(1)}, u32[]{:S(2)}, u32[]{:S(2)}) collective-permute-start(bf16[16,4608]{1,0:T(8,128)(2,1)S(1)} %get-tuple-element.73.refs_0_), channel_id=1, source_target_pairs={{0,7},{1,0},{2,1},{3,2},{4,3},{5,4},{6,5},{7,6},{8,15},{9,8},{10,9... | collective-permute-start | bytes 442376 | tf_op jit(solution)/shard_map/ppermute | solution.py:52
  27.1 1.8 collective-permute-done.1.refs_1_
  28.9 3.7 %collective-permute-done.2.refs_2_ = bf16[16,4608]{1,0:T(8,128)(2,1)S(1)} collective-permute-done((bf16[16,4608]{1,0:T(8,128)(2,1)S(1)}, bf16[16,4608]{1,0:T(8,128)(2,1)S(1)}, u32[]{:S(2)}, u32[]{:S(2)}) %collective-permute-start.2) | collective-permute-done | bytes 147488 | tf_op jit(solution)/shard_map/ppermute | solution.py:52
  34.7 1.6 collective-permute-start.7
  36.3 2.1 %collective-permute-start.16 = (bf16[384,1024]{1,0:T(8,128)(2,1)S(1)}, bf16[384,1024]{1,0:T(8,128)(2,1)}, u32[]{:S(2)}, u32[]{:S(2)}) collective-permute-start(bf16[384,1024]{1,0:T(8,128)(2,1)S(1)} %get-tuple-element.79.top.refs_14_), channel_id=1, source_target_pairs={{0,128},{128,0},{1,129},{129,1},{2,130},{130,2},{3,131},{131,3},{4... | collective-permute-start | bytes 2359304 | tf_op jit(solution)/shard_map/ppermute | solution.py:52
  38.4 1.7 collective-permute-done.6.refs_3_
  40.1 1.3 collective-permute-done.7.refs_4_
  42.6 1.1 collective-permute-start.11
  43.9 1.7 collective-permute-start.13
  45.7 7.1 %collective-permute-done.12.refs_0_ = bf16[16,4608]{1,0:T(8,128)(2,1)S(1)} collective-permute-done((bf16[16,4608]{1,0:T(8,128)(2,1)S(1)}, bf16[16,4608]{1,0:T(8,128)(2,1)S(1)}, u32[]{:S(2)}, u32[]{:S(2)}) %collective-permute-start.12) | collective-permute-done | bytes 147488 | tf_op jit(solution)/shard_map/ppermute | solution.py:52
  52.8 1.5 collective-permute-done.13.refs_1_
  54.5 1.8 collective-permute-start.15
  56.3 3.9 %collective-permute-done.14.refs_2_ = bf16[16,2304]{1,0:T(8,128)(2,1)S(1)} collective-permute-done((bf16[16,2304]{1,0:T(8,128)(2,1)S(1)}, bf16[16,2304]{1,0:T(8,128)(2,1)S(1)}, u32[]{:S(2)}, u32[]{:S(2)}) %collective-permute-start.14) | collective-permute-done | bytes 73760 | tf_op jit(solution)/shard_map/ppermute | solution.py:52
  60.2 1.5 collective-permute-done.15.refs_3_
  61.7 2.3 %collective-permute-start.21 = (bf16[384,1024]{1,0:T(8,128)(2,1)S(1)}, bf16[384,1024]{1,0:T(8,128)(2,1)}, u32[]{:S(2)}, u32[]{:S(2)}) collective-permute-start(bf16[384,1024]{1,0:T(8,128)(2,1)S(1)} %get-tuple-element.91.bottom.refs_15_), channel_id=1, source_target_pairs={{0,128},{128,0},{1,129},{129,1},{2,130},{130,2},{3,131},{131,3},{4... | collective-permute-start | bytes 2359304 | tf_op jit(solution)/shard_map/ppermute | solution.py:52
  64.0 1.8 shard_map.108.refs_10_
  66.0 1.8 collective-permute-start.19
  68.1 3.0 %collective-permute-start.17 = (bf16[80,2304]{1,0:T(8,128)(2,1)S(1)}, bf16[80,2304]{1,0:T(8,128)(2,1)S(1)}, u32[]{:S(2)}, u32[]{:S(2)}) collective-permute-start(bf16[80,2304]{1,0:T(8,128)(2,1)S(1)} %slice.62), channel_id=1, source_target_pairs={{0,24},{8,0},{16,8},{24,16},{1,25},{9,1},{17,9},{25,17},{2,26},{10... | collective-permute-start | bytes 1105928 | tf_op jit(solution)/shard_map/ppermute | solution.py:52
  71.3 1.8 shard_map.109.refs_12_
  73.1 7.0 %collective-permute-done.21.bottom.refs_17_ = bf16[384,1024]{1,0:T(8,128)(2,1)} collective-permute-done((bf16[384,1024]{1,0:T(8,128)(2,1)S(1)}, bf16[384,1024]{1,0:T(8,128)(2,1)}, u32[]{:S(2)}, u32[]{:S(2)}) %collective-permute-start.21) | collective-permute-done | bytes 786464 | tf_op jit(solution)/shard_map/ppermute | solution.py:52
  80.1 2.7 %collective-permute-done.17.refs_4_ = bf16[80,2304]{1,0:T(8,128)(2,1)S(1)} collective-permute-done((bf16[80,2304]{1,0:T(8,128)(2,1)S(1)}, bf16[80,2304]{1,0:T(8,128)(2,1)S(1)}, u32[]{:S(2)}, u32[]{:S(2)}) %collective-permute-start.17) | collective-permute-done | bytes 368672 | tf_op jit(solution)/shard_map/ppermute | solution.py:52
  82.8 2.2 %collective-permute-done.18.refs_5_ = bf16[80,2304]{1,0:T(8,128)(2,1)S(1)} collective-permute-done((bf16[80,2304]{1,0:T(8,128)(2,1)S(1)}, bf16[80,2304]{1,0:T(8,128)(2,1)S(1)}, u32[]{:S(2)}, u32[]{:S(2)}) %collective-permute-start.18) | collective-permute-done | bytes 368672 | tf_op jit(solution)/shard_map/ppermute | solution.py:52
  86.7 1.7 collective-permute-start.23
  88.6 2.8 %shard_map.110.refs_11_ = bf16[1024,768]{1,0:T(8,128)(2,1)} custom-call(bf16[384,1024]{1,0:T(8,128)(2,1)} %collective-permute-done.16.top.refs_16_, bf16[384,1024]{1,0:T(8,128)(2,1)} %collective-permute-done.21.bottom.refs_17_), custom_call_target="tpu_custom_call" | custom-call | bytes 3145728 | tf_op jit(solution)/shard_map/pallas_call | solution.py:180
  91.5 1.8 shard_map.111.refs_13_
  93.3 2.0 %collective-permute-done.23.refs_7_ = bf16[48,2304]{1,0:T(8,128)(2,1)S(1)} collective-permute-done((bf16[48,2304]{1,0:T(8,128)(2,1)}, bf16[48,2304]{1,0:T(8,128)(2,1)S(1)}, u32[]{:S(2)}, u32[]{:S(2)}) %collective-permute-start.23) | collective-permute-done | bytes 221216 | tf_op jit(solution)/shard_map/ppermute | solution.py:52
  95.3 14.2 %shard_map.112 = (bf16[8,72,512]{2,1,0:T(8,128)(2,1)}, bf16[576,4096]{1,0:T(8,128)(2,1)}, bf16[576,256]{1,0:T(8,128)(2,1)S(1)}, bf16[8,72,4096]{2,1,0:T(8,128)(2,1)}) custom-call(s32[1]{0:T(128)} %bitcast.4.z_ref, s32[4]{0:T(128)S(1)} %pad_add_fusion.place_ref, bf16[576,4096]{1,0:T(8,128)(2,1)} %all-gather.2.cloned.1.call-done.tok_ref.refs_1_, ...), custom_call_target="tpu_custom_call" | custom-call | flops 6039797760 | bytes 31457280 | tf_op jit(solution)/shard_map/pallas_call | solution.py:361
  110.7 9.1 %shard_map.114 = (bf16[2,512,1024]{2,1,0:T(8,128)(2,1)}, f32[2,512,1024]{2,1,0:T(8,128)}) custom-call(s32[4]{0:T(128)S(1)} %rev.3.order_ref, bf16[576,512]{1,0:T(8,128)(2,1)S(1)} %bitcast.52, bf16[576,4096]{1,0:T(8,128)(2,1)} %all-gather.2.cloned.1.call-done.tok_ref.refs_1_), custom_call_target="tpu_custom_call" | custom-call | flops 2415919104 | bytes 11010048 | tf_op jit(solution)/shard_map/pallas_call | solution.py:435
  119.8 6.1 %shard_map.115 = (bf16[2,256,1024]{2,1,0:T(8,128)(2,1)S(1)}, f32[2,256,1024]{2,1,0:T(8,128)}) custom-call(s32[4]{0:T(128)S(1)} %rev.3.order_ref, bf16[576,256]{1,0:T(8,128)(2,1)S(1)} %get-tuple-element.117.refs_0_, bf16[576,4096]{1,0:T(8,128)(2,1)} %get-tuple-element.118.refs_1_), custom_call_target="tpu_custom_call" | custom-call | flops 1207959552 | bytes 7864320 | tf_op jit(solution)/shard_map/pallas_call | solution.py:435
  126.6 1.4 fusion.1
  127.9 1.4 collective-permute-start.30
  130.3 2.1 %collective-permute-start.32 = (bf16[256,1024]{1,0:T(8,128)(2,1)}, bf16[256,1024]{1,0:T(8,128)(2,1)}, u32[]{:S(2)}, u32[]{:S(2)}) collective-permute-start(bf16[256,1024]{1,0:T(8,128)(2,1)} %fusion.3), channel_id=1, source_target_pairs={{0,128},{128,0},{1,129},{129,1},{2,130},{130,2},{3,131},{131,3},{4... | collective-permute-start | bytes 1572872 | tf_op jit(solution)/shard_map/ppermute | solution.py:52
  132.6 34.6 %reduce-scatter.2.cloned.1.call-done.ref = bf16[72,4096]{1,0:T(8,128)(2,1)} async-done(((bf16[576,4096]{1,0:T(8,128)(2,1)}), bf16[72,4096]{1,0:T(8,128)(2,1)}) %reduce-scatter.2.cloned.1.call-update) | async-done | bytes 589840 | tf_op jit(solution)/shard_map/reduce_scatter | solution.py:507
  167.2 1.1 copy-done.7
  168.4 1.5 collective-permute-start.26
  170.0 1.8 collective-permute-start.27
  171.8 1.8 collective-permute-start.28
  173.6 2.7 %bitcast_add_fusion = f32[512,1024]{1,0:T(8,128)S(1)} fusion(bf16[512,1024]{1,0:T(8,128)(2,1)} %collective-permute-done.30, f32[2,512,1024]{2,1,0:T(8,128)} %get-tuple-element.115, bf16[2,512,1024]{2,1,0:T(8,128)(2,1)} %copy-done.18), kind=kLoop, calls=%fused_computation.2 | loop fusion | flops 2097152 | bytes 6291456 | tf_op jit(solution)/shard_map/add | solution.py:519
  176.5 2.1 %fusion.2 = bf16[256,1024]{1,0:T(8,128)(2,1)} fusion(bf16[256,1024]{1,0:T(8,128)(2,1)} %collective-permute-done.32, f32[2,256,1024]{2,1,0:T(8,128)S(1)} %copy-done.17, bf16[2,256,1024]{2,1,0:T(8,128)(2,1)S(1)} %collective-permute-done.31, f32[2,1024]{1,0:T(2,128)S(1)} %bitcast.56), kind=kLoop, calls=%fused_computation.6 | loop fusion | flops 1572864 | bytes 2629632 | tf_op jit(solution)/shard_map/convert_element_type | solution.py:521
  180.2 1.0 slice_bitcast_fusion
  181.3 3.6 %collective-permute-done.33.other_ref = f32[8,4608]{1,0:T(8,128)S(1)} collective-permute-done((f32[8,4608]{1,0:T(8,128)S(1)}, f32[8,4608]{1,0:T(8,128)S(1)}, u32[]{:S(2)}, u32[]{:S(2)}) %collective-permute-start.33) | collective-permute-done | bytes 147488 | tf_op jit(solution)/shard_map/ppermute | solution.py:52
  184.8 1.2 shard_map.117
  (115 shorter events, 15.7 us)
Async XLA Ops:
  7.2 88.2 %all-gather.2.cloned.1.call-start = ((), (), s32[]{:S(2)}) async-start(), calls=%async_computation.1 | async-start | bytes 5308416 | tf_op jit(solution)/shard_map/all_gather | solution.py:480
  9.4 6.9 %collective-permute-start = (bf16[16,4608]{1,0:T(8,128)(2,1)S(1)}, bf16[16,4608]{1,0:T(8,128)(2,1)S(1)}, u32[]{:S(2)}, u32[]{:S(2)}) collective-permute-start(bf16[16,4608]{1,0:T(8,128)(2,1)S(1)} %shard_map.102.mine_ref), channel_id=1, source_target_pairs={{0,32},{32,0},{1,33},{33,1},{2,34},{34,2},{3,35},{35,3},{4,36},{36... | collective-permute-start | bytes 442376 | tf_op jit(solution)/shard_map/ppermute | solution.py:52
  12.8 116.5 %copy-start.23 = (f32[3,2,8]{2,1,0:T(2,128)}, f32[3,2,8]{2,1,0:T(2,128)S(1)}, u32[]{:S(2)}) copy-start(f32[3,2,8]{2,1,0:T(2,128)S(1)} %dynamic-slice_bitcast_fusion) | copy-start | bytes 580
  16.3 49.5 %copy-start = (bf16[384,1024]{1,0:T(8,128)(2,1)}, bf16[384,1024]{1,0:T(8,128)(2,1)S(1)}, u32[]{:S(2)}) copy-start(bf16[384,1024]{1,0:T(8,128)(2,1)S(1)} %get-tuple-element.79.top.refs_14_) | copy-start | bytes 2359300
  16.3 49.5 %copy-start.1 = (bf16[384,1024]{1,0:T(8,128)(2,1)}, bf16[384,1024]{1,0:T(8,128)(2,1)S(1)}, u32[]{:S(2)}) copy-start(bf16[384,1024]{1,0:T(8,128)(2,1)S(1)} %get-tuple-element.91.bottom.refs_15_) | copy-start | bytes 2359300
  16.4 9.9 %collective-permute-start.3 = (bf16[16,4608]{1,0:T(8,128)(2,1)S(1)}, bf16[16,4608]{1,0:T(8,128)(2,1)S(1)}, u32[]{:S(2)}, u32[]{:S(2)}) collective-permute-start(bf16[16,4608]{1,0:T(8,128)(2,1)S(1)} %get-tuple-element.72.refs_0_), channel_id=1, source_target_pairs={{0,24},{8,0},{16,8},{24,16},{1,25},{9,1},{17,9},{25,17},{2,26},{10... | collective-permute-start | bytes 442376 | tf_op jit(solution)/shard_map/ppermute | solution.py:52
  18.2 8.9 %collective-permute-start.4 = (bf16[16,4608]{1,0:T(8,128)(2,1)S(1)}, bf16[16,4608]{1,0:T(8,128)(2,1)S(1)}, u32[]{:S(2)}, u32[]{:S(2)}) collective-permute-start(bf16[16,4608]{1,0:T(8,128)(2,1)S(1)} %get-tuple-element.72.refs_0_), channel_id=1, source_target_pairs={{0,8},{8,16},{16,24},{24,0},{1,9},{9,17},{17,25},{25,1},{2,10},{10... | collective-permute-start | bytes 442376 | tf_op jit(solution)/shard_map/ppermute | solution.py:52
  18.5 8.7 %collective-permute-start.5 = (bf16[16,4608]{1,0:T(8,128)(2,1)S(1)}, bf16[16,4608]{1,0:T(8,128)(2,1)S(1)}, u32[]{:S(2)}, u32[]{:S(2)}) collective-permute-start(bf16[16,4608]{1,0:T(8,128)(2,1)S(1)} %get-tuple-element.72.refs_0_), channel_id=1, source_target_pairs={{0,16},{8,24},{16,0},{24,8},{1,17},{9,25},{17,1},{25,9},{2,18},{10... | collective-permute-start | bytes 442376 | tf_op jit(solution)/shard_map/ppermute | solution.py:52
  20.4 8.5 %collective-permute-start.1 = (bf16[16,4608]{1,0:T(8,128)(2,1)S(1)}, bf16[16,4608]{1,0:T(8,128)(2,1)S(1)}, u32[]{:S(2)}, u32[]{:S(2)}) collective-permute-start(bf16[16,4608]{1,0:T(8,128)(2,1)S(1)} %get-tuple-element.73.refs_0_), channel_id=1, source_target_pairs={{0,7},{1,0},{2,1},{3,2},{4,3},{5,4},{6,5},{7,6},{8,15},{9,8},{10,9... | collective-permute-start | bytes 442376 | tf_op jit(solution)/shard_map/ppermute | solution.py:52
  26.2 6.4 %collective-permute-start.2 = (bf16[16,4608]{1,0:T(8,128)(2,1)S(1)}, bf16[16,4608]{1,0:T(8,128)(2,1)S(1)}, u32[]{:S(2)}, u32[]{:S(2)}) collective-permute-start(bf16[16,4608]{1,0:T(8,128)(2,1)S(1)} %get-tuple-element.73.refs_0_), channel_id=1, source_target_pairs={{0,1},{1,2},{2,3},{3,4},{4,5},{5,6},{6,7},{7,0},{8,9},{9,10},{10,1... | collective-permute-start | bytes 442376 | tf_op jit(solution)/shard_map/ppermute | solution.py:52
  33.6 133.5 %reduce-scatter.2.cloned.1.call-start = ((), (), s32[]{:S(2)}) async-start(), calls=%async_computation.2 | async-start | bytes 5308416 | tf_op jit(solution)/shard_map/reduce_scatter | solution.py:507
  33.7 7.8 %collective-permute-start.8 = (bf16[384,1024]{1,0:T(8,128)(2,1)S(1)}, bf16[384,1024]{1,0:T(8,128)(2,1)S(1)}, u32[]{:S(2)}, u32[]{:S(2)}) collective-permute-start(bf16[384,1024]{1,0:T(8,128)(2,1)S(1)} %get-tuple-element.79.top.refs_14_), channel_id=1, source_target_pairs={{0,64},{64,0},{1,65},{65,1},{2,66},{66,2},{3,67},{67,3},{4,68},{68... | collective-permute-start | bytes 2359304 | tf_op jit(solution)/shard_map/ppermute | solution.py:52
  33.8 7.7 %collective-permute-start.9 = (bf16[384,1024]{1,0:T(8,128)(2,1)S(1)}, bf16[384,1024]{1,0:T(8,128)(2,1)S(1)}, u32[]{:S(2)}, u32[]{:S(2)}) collective-permute-start(bf16[384,1024]{1,0:T(8,128)(2,1)S(1)} %get-tuple-element.91.bottom.refs_15_), channel_id=1, source_target_pairs={{0,64},{64,0},{1,65},{65,1},{2,66},{66,2},{3,67},{67,3},{4,68},{68... | collective-permute-start | bytes 2359304 | tf_op jit(solution)/shard_map/ppermute | solution.py:52
  34.3 5.9 %collective-permute-start.6 = (bf16[16,4608]{1,0:T(8,128)(2,1)S(1)}, bf16[16,4608]{1,0:T(8,128)(2,1)S(1)}, u32[]{:S(2)}, u32[]{:S(2)}) collective-permute-start(bf16[16,4608]{1,0:T(8,128)(2,1)S(1)} %collective-permute-done.1.refs_1_), channel_id=1, source_target_pairs={{0,7},{1,0},{2,1},{3,2},{4,3},{5,4},{6,5},{7,6},{8,15},{9,8},{10,9... | collective-permute-start | bytes 442376 | tf_op jit(solution)/shard_map/ppermute | solution.py:52
  34.7 6.8 %collective-permute-start.7 = (bf16[16,4608]{1,0:T(8,128)(2,1)S(1)}, bf16[16,4608]{1,0:T(8,128)(2,1)S(1)}, u32[]{:S(2)}, u32[]{:S(2)}) collective-permute-start(bf16[16,4608]{1,0:T(8,128)(2,1)S(1)} %collective-permute-done.2.refs_2_), channel_id=1, source_target_pairs={{0,1},{1,2},{2,3},{3,4},{4,5},{5,6},{6,7},{7,0},{8,9},{9,10},{10,1... | collective-permute-start | bytes 442376 | tf_op jit(solution)/shard_map/ppermute | solution.py:52
  36.3 29.6 %collective-permute-start.16 = (bf16[384,1024]{1,0:T(8,128)(2,1)S(1)}, bf16[384,1024]{1,0:T(8,128)(2,1)}, u32[]{:S(2)}, u32[]{:S(2)}) collective-permute-start(bf16[384,1024]{1,0:T(8,128)(2,1)S(1)} %get-tuple-element.79.top.refs_14_), channel_id=1, source_target_pairs={{0,128},{128,0},{1,129},{129,1},{2,130},{130,2},{3,131},{131,3},{4... | collective-permute-start | bytes 2359304 | tf_op jit(solution)/shard_map/ppermute | solution.py:52
  41.4 29.8 %copy-start.2 = (bf16[384,1024]{1,0:T(8,128)(2,1)}, bf16[384,1024]{1,0:T(8,128)(2,1)S(1)}, u32[]{:S(2)}) copy-start(bf16[384,1024]{1,0:T(8,128)(2,1)S(1)} %collective-permute-done.8.top.refs_18_) | copy-start | bytes 2359300
  41.5 29.8 %copy-start.3 = (bf16[384,1024]{1,0:T(8,128)(2,1)}, bf16[384,1024]{1,0:T(8,128)(2,1)S(1)}, u32[]{:S(2)}) copy-start(bf16[384,1024]{1,0:T(8,128)(2,1)S(1)} %collective-permute-done.9.bottom.refs_19_) | copy-start | bytes 2359300
  41.5 24.4 %copy-start.6 = (bf16[80,4608]{1,0:T(8,128)(2,1)}, bf16[80,4608]{1,0:T(8,128)(2,1)S(1)}, u32[]{:S(2)}) copy-start(bf16[80,4608]{1,0:T(8,128)(2,1)S(1)} %shard_map.106.refs_0_) | copy-start | bytes 2211844
  41.5 24.4 %collective-permute-start.10 = (bf16[80,4608]{1,0:T(8,128)(2,1)S(1)}, bf16[80,4608]{1,0:T(8,128)(2,1)S(1)}, u32[]{:S(2)}, u32[]{:S(2)}) collective-permute-start(bf16[80,4608]{1,0:T(8,128)(2,1)S(1)} %shard_map.106.refs_0_), channel_id=1, source_target_pairs={{0,24},{8,0},{16,8},{24,16},{1,25},{9,1},{17,9},{25,17},{2,26},{10... | collective-permute-start | bytes 2211848 | tf_op jit(solution)/shard_map/ppermute | solution.py:52
  42.6 23.4 %collective-permute-start.11 = (bf16[80,4608]{1,0:T(8,128)(2,1)S(1)}, bf16[80,4608]{1,0:T(8,128)(2,1)S(1)}, u32[]{:S(2)}, u32[]{:S(2)}) collective-permute-start(bf16[80,4608]{1,0:T(8,128)(2,1)S(1)} %shard_map.106.refs_0_), channel_id=1, source_target_pairs={{0,8},{8,16},{16,24},{24,0},{1,9},{9,17},{17,25},{25,1},{2,10},{10... | collective-permute-start | bytes 2211848 | tf_op jit(solution)/shard_map/ppermute | solution.py:52
  43.6 9.1 %collective-permute-start.12 = (bf16[16,4608]{1,0:T(8,128)(2,1)S(1)}, bf16[16,4608]{1,0:T(8,128)(2,1)S(1)}, u32[]{:S(2)}, u32[]{:S(2)}) collective-permute-start(bf16[16,4608]{1,0:T(8,128)(2,1)S(1)} %collective-permute-done.6.refs_3_), channel_id=1, source_target_pairs={{0,7},{1,0},{2,1},{3,2},{4,3},{5,4},{6,5},{7,6},{8,15},{9,8},{10,9... | collective-permute-start | bytes 442376 | tf_op jit(solution)/shard_map/ppermute | solution.py:52
  43.9 10.3 %collective-permute-start.13 = (bf16[16,4608]{1,0:T(8,128)(2,1)S(1)}, bf16[16,4608]{1,0:T(8,128)(2,1)S(1)}, u32[]{:S(2)}, u32[]{:S(2)}) collective-permute-start(bf16[16,4608]{1,0:T(8,128)(2,1)S(1)} %collective-permute-done.7.refs_4_), channel_id=1, source_target_pairs={{0,1},{1,2},{2,3},{3,4},{4,5},{5,6},{6,7},{7,0},{8,9},{9,10},{10,1... | collective-permute-start | bytes 442376 | tf_op jit(solution)/shard_map/ppermute | solution.py:52
  54.3 5.9 %collective-permute-start.14 = (bf16[16,2304]{1,0:T(8,128)(2,1)S(1)}, bf16[16,2304]{1,0:T(8,128)(2,1)S(1)}, u32[]{:S(2)}, u32[]{:S(2)}) collective-permute-start(bf16[16,2304]{1,0:T(8,128)(2,1)S(1)} %slice.60), channel_id=1, source_target_pairs={{0,7},{1,0},{2,1},{3,2},{4,3},{5,4},{6,5},{7,6},{8,15},{9,8},{10,9... | collective-permute-start | bytes 221192 | tf_op jit(solution)/shard_map/ppermute | solution.py:52
  54.5 7.2 %collective-permute-start.15 = (bf16[16,2304]{1,0:T(8,128)(2,1)S(1)}, bf16[16,2304]{1,0:T(8,128)(2,1)S(1)}, u32[]{:S(2)}, u32[]{:S(2)}) collective-permute-start(bf16[16,2304]{1,0:T(8,128)(2,1)S(1)} %slice.61), channel_id=1, source_target_pairs={{0,1},{1,2},{2,3},{3,4},{4,5},{5,6},{6,7},{7,0},{8,9},{9,10},{10,1... | collective-permute-start | bytes 221192 | tf_op jit(solution)/shard_map/ppermute | solution.py:52
  61.7 18.4 %collective-permute-start.21 = (bf16[384,1024]{1,0:T(8,128)(2,1)S(1)}, bf16[384,1024]{1,0:T(8,128)(2,1)}, u32[]{:S(2)}, u32[]{:S(2)}) collective-permute-start(bf16[384,1024]{1,0:T(8,128)(2,1)S(1)} %get-tuple-element.91.bottom.refs_15_), channel_id=1, source_target_pairs={{0,128},{128,0},{1,129},{129,1},{2,130},{130,2},{3,131},{131,3},{4... | collective-permute-start | bytes 2359304 | tf_op jit(solution)/shard_map/ppermute | solution.py:52
  65.9 7.2 %copy-start.11 = (bf16[48,4608]{1,0:T(8,128)(2,1)}, bf16[48,4608]{1,0:T(8,128)(2,1)S(1)}, u32[]{:S(2)}) copy-start(bf16[48,4608]{1,0:T(8,128)(2,1)S(1)} %shard_map.107.refs_1_) | copy-start | bytes 1327108
  65.9 7.1 %copy-start.19 = (bf16[80,4608]{1,0:T(8,128)(2,1)}, bf16[80,4608]{1,0:T(8,128)(2,1)S(1)}, u32[]{:S(2)}) copy-start(bf16[80,4608]{1,0:T(8,128)(2,1)S(1)} %collective-permute-done.10.refs_2_) | copy-start | bytes 2211844
  66.0 7.1 %copy-start.20 = (bf16[80,4608]{1,0:T(8,128)(2,1)}, bf16[80,4608]{1,0:T(8,128)(2,1)S(1)}, u32[]{:S(2)}) copy-start(bf16[80,4608]{1,0:T(8,128)(2,1)S(1)} %collective-permute-done.11.refs_8_) | copy-start | bytes 2211844
  66.0 19.1 %collective-permute-start.19 = (bf16[48,4608]{1,0:T(8,128)(2,1)S(1)}, bf16[48,4608]{1,0:T(8,128)(2,1)S(1)}, u32[]{:S(2)}, u32[]{:S(2)}) collective-permute-start(bf16[48,4608]{1,0:T(8,128)(2,1)S(1)} %shard_map.107.refs_1_), channel_id=1, source_target_pairs={{0,24},{8,0},{16,8},{24,16},{1,25},{9,1},{17,9},{25,17},{2,26},{10... | collective-permute-start | bytes 1327112 | tf_op jit(solution)/shard_map/ppermute | solution.py:52
  67.8 17.3 %collective-permute-start.20 = (bf16[48,4608]{1,0:T(8,128)(2,1)S(1)}, bf16[48,4608]{1,0:T(8,128)(2,1)S(1)}, u32[]{:S(2)}, u32[]{:S(2)}) collective-permute-start(bf16[48,4608]{1,0:T(8,128)(2,1)S(1)} %shard_map.107.refs_1_), channel_id=1, source_target_pairs={{0,8},{8,16},{16,24},{24,0},{1,9},{9,17},{17,25},{25,1},{2,10},{10... | collective-permute-start | bytes 1327112 | tf_op jit(solution)/shard_map/ppermute | solution.py:52
  68.1 14.7 %collective-permute-start.17 = (bf16[80,2304]{1,0:T(8,128)(2,1)S(1)}, bf16[80,2304]{1,0:T(8,128)(2,1)S(1)}, u32[]{:S(2)}, u32[]{:S(2)}) collective-permute-start(bf16[80,2304]{1,0:T(8,128)(2,1)S(1)} %slice.62), channel_id=1, source_target_pairs={{0,24},{8,0},{16,8},{24,16},{1,25},{9,1},{17,9},{25,17},{2,26},{10... | collective-permute-start | bytes 1105928 | tf_op jit(solution)/shard_map/ppermute | solution.py:52
  71.1 13.9 %collective-permute-start.18 = (bf16[80,2304]{1,0:T(8,128)(2,1)S(1)}, bf16[80,2304]{1,0:T(8,128)(2,1)S(1)}, u32[]{:S(2)}, u32[]{:S(2)}) collective-permute-start(bf16[80,2304]{1,0:T(8,128)(2,1)S(1)} %slice.63), channel_id=1, source_target_pairs={{0,8},{8,16},{16,24},{24,0},{1,9},{9,17},{17,25},{25,1},{2,10},{10... | collective-permute-start | bytes 1105928 | tf_op jit(solution)/shard_map/ppermute | solution.py:52
  85.1 6.4 %collective-permute-start.24 = (bf16[384,1024]{1,0:T(8,128)(2,1)}, bf16[384,1024]{1,0:T(8,128)(2,1)S(1)}, u32[]{:S(2)}, u32[]{:S(2)}) collective-permute-start(bf16[384,1024]{1,0:T(8,128)(2,1)} %collective-permute-done.16.top.refs_16_), channel_id=1, source_target_pairs={{0,64},{64,0},{1,65},{65,1},{2,66},{66,2},{3,67},{67,3},{4,68},{68... | collective-permute-start | bytes 2359304 | tf_op jit(solution)/shard_map/ppermute | solution.py:52
  85.2 6.3 %collective-permute-start.25 = (bf16[384,1024]{1,0:T(8,128)(2,1)}, bf16[384,1024]{1,0:T(8,128)(2,1)S(1)}, u32[]{:S(2)}, u32[]{:S(2)}) collective-permute-start(bf16[384,1024]{1,0:T(8,128)(2,1)} %collective-permute-done.21.bottom.refs_17_), channel_id=1, source_target_pairs={{0,64},{64,0},{1,65},{65,1},{2,66},{66,2},{3,67},{67,3},{4,68},{68... | collective-permute-start | bytes 2359304 | tf_op jit(solution)/shard_map/ppermute | solution.py:52
  85.7 7.6 %collective-permute-start.22 = (bf16[48,2304]{1,0:T(8,128)(2,1)S(1)}, bf16[48,2304]{1,0:T(8,128)(2,1)S(1)}, u32[]{:S(2)}, u32[]{:S(2)}) collective-permute-start(bf16[48,2304]{1,0:T(8,128)(2,1)S(1)} %slice.64), channel_id=1, source_target_pairs={{0,24},{8,0},{16,8},{24,16},{1,25},{9,1},{17,9},{25,17},{2,26},{10... | collective-permute-start | bytes 663560 | tf_op jit(solution)/shard_map/ppermute | solution.py:52
  86.7 8.6 %collective-permute-start.23 = (bf16[48,2304]{1,0:T(8,128)(2,1)}, bf16[48,2304]{1,0:T(8,128)(2,1)S(1)}, u32[]{:S(2)}, u32[]{:S(2)}) collective-permute-start(bf16[48,2304]{1,0:T(8,128)(2,1)} %slice.65), channel_id=1, source_target_pairs={{0,8},{8,16},{16,24},{24,0},{1,9},{9,17},{17,25},{25,1},{2,10},{10... | collective-permute-start | bytes 663560 | tf_op jit(solution)/shard_map/ppermute | solution.py:52
  91.4 3.9 %copy-start.12 = (bf16[48,4608]{1,0:T(8,128)(2,1)S(1)}, bf16[48,4608]{1,0:T(8,128)(2,1)}, u32[]{:S(2)}) copy-start(bf16[48,4608]{1,0:T(8,128)(2,1)} %copy-done.11) | copy-start | bytes 1327108
  91.4 3.9 %copy-start.4 = (bf16[384,1024]{1,0:T(8,128)(2,1)}, bf16[384,1024]{1,0:T(8,128)(2,1)S(1)}, u32[]{:S(2)}) copy-start(bf16[384,1024]{1,0:T(8,128)(2,1)S(1)} %collective-permute-done.24.top.refs_20_) | copy-start | bytes 2359300
  119.7 6.2 %collective-permute-start.29 = (bf16[2,512,1024]{2,1,0:T(8,128)(2,1)}, bf16[2,512,1024]{2,1,0:T(8,128)(2,1)S(1)}, u32[]{:S(2)}, u32[]{:S(2)}) collective-permute-start(bf16[2,512,1024]{2,1,0:T(8,128)(2,1)} %get-tuple-element.116), channel_id=1, source_target_pairs={{0,64},{64,0},{1,65},{65,1},{2,66},{66,2},{3,67},{67,3},{4,68},{68... | collective-permute-start | bytes 6291464 | tf_op jit(solution)/shard_map/ppermute | solution.py:52
  119.8 6.7 %copy-start.16 = (f32[2,512,1024]{2,1,0:T(8,128)S(1)}, f32[2,512,1024]{2,1,0:T(8,128)}, u32[]{:S(2)}) copy-start(f32[2,512,1024]{2,1,0:T(8,128)} %get-tuple-element.115) | copy-start | bytes 12582916
  126.0 3.3 %collective-permute-start.31 = (bf16[2,256,1024]{2,1,0:T(8,128)(2,1)S(1)}, bf16[2,256,1024]{2,1,0:T(8,128)(2,1)S(1)}, u32[]{:S(2)}, u32[]{:S(2)}) collective-permute-start(bf16[2,256,1024]{2,1,0:T(8,128)(2,1)S(1)} %get-tuple-element.123), channel_id=1, source_target_pairs={{0,64},{64,0},{1,65},{65,1},{2,66},{66,2},{3,67},{67,3},{4,68},{68... | collective-permute-start | bytes 3145736 | tf_op jit(solution)/shard_map/ppermute | solution.py:52
  127.9 45.6 %collective-permute-start.30 = (bf16[512,1024]{1,0:T(8,128)(2,1)}, bf16[512,1024]{1,0:T(8,128)(2,1)}, u32[]{:S(2)}, u32[]{:S(2)}) collective-permute-start(bf16[512,1024]{1,0:T(8,128)(2,1)} %fusion.1), channel_id=1, source_target_pairs={{0,128},{128,0},{1,129},{129,1},{2,130},{130,2},{3,131},{131,3},{4... | collective-permute-start | bytes 3145736 | tf_op jit(solution)/shard_map/ppermute | solution.py:52
  130.3 46.2 %collective-permute-start.32 = (bf16[256,1024]{1,0:T(8,128)(2,1)}, bf16[256,1024]{1,0:T(8,128)(2,1)}, u32[]{:S(2)}, u32[]{:S(2)}) collective-permute-start(bf16[256,1024]{1,0:T(8,128)(2,1)} %fusion.3), channel_id=1, source_target_pairs={{0,128},{128,0},{1,129},{129,1},{2,130},{130,2},{3,131},{131,3},{4... | collective-permute-start | bytes 1572872 | tf_op jit(solution)/shard_map/ppermute | solution.py:52
  168.4 10.2 %collective-permute-start.26 = (bf16[16,4608]{1,0:T(8,128)(2,1)S(1)}, bf16[16,4608]{1,0:T(8,128)(2,1)S(1)}, u32[]{:S(2)}, u32[]{:S(2)}) collective-permute-start(bf16[16,4608]{1,0:T(8,128)(2,1)S(1)} %get-tuple-element.111), channel_id=1, source_target_pairs={{0,8},{8,16},{16,24},{24,0},{1,9},{9,17},{17,25},{25,1},{2,10},{10... | collective-permute-start | bytes 442376 | tf_op jit(solution)/shard_map/ppermute | solution.py:52
  170.0 8.6 %collective-permute-start.27 = (bf16[16,4608]{1,0:T(8,128)(2,1)S(1)}, bf16[16,4608]{1,0:T(8,128)(2,1)S(1)}, u32[]{:S(2)}, u32[]{:S(2)}) collective-permute-start(bf16[16,4608]{1,0:T(8,128)(2,1)S(1)} %get-tuple-element.112), channel_id=1, source_target_pairs={{0,24},{8,0},{16,8},{24,16},{1,25},{9,1},{17,9},{25,17},{2,26},{10... | collective-permute-start | bytes 442376 | tf_op jit(solution)/shard_map/ppermute | solution.py:52
  171.8 7.7 %collective-permute-start.28 = (bf16[16,4608]{1,0:T(8,128)(2,1)S(1)}, bf16[16,4608]{1,0:T(8,128)(2,1)S(1)}, u32[]{:S(2)}, u32[]{:S(2)}) collective-permute-start(bf16[16,4608]{1,0:T(8,128)(2,1)S(1)} %get-tuple-element.113), channel_id=1, source_target_pairs={{0,16},{8,24},{16,0},{24,8},{1,17},{9,25},{17,1},{25,9},{2,18},{10... | collective-permute-start | bytes 442376 | tf_op jit(solution)/shard_map/ppermute | solution.py:52
  179.6 5.2 %collective-permute-start.33 = (f32[8,4608]{1,0:T(8,128)S(1)}, f32[8,4608]{1,0:T(8,128)S(1)}, u32[]{:S(2)}, u32[]{:S(2)}) collective-permute-start(f32[8,4608]{1,0:T(8,128)S(1)} %get-tuple-element.129), channel_id=1, source_target_pairs={{0,32},{32,0},{1,33},{33,1},{2,34},{34,2},{3,35},{35,3},{4,36},{36... | collective-permute-start | bytes 442376 | tf_op jit(solution)/shard_map/ppermute | solution.py:52
  (13 other events, 21.5 us)
Sparse Core Ops, SparseCore 0:
  33.7 60.5 all-gather.1
  109.7 57.3 reduce-scatter.1

commit v2 on v1

--- a/solution.py
+++ b/solution.py
@@ -76,7 +76,7 @@
         4 * own * width * n,
         limit=BIG_LIMIT,
         scratch_shapes=[pltpu.VMEM((n, own, width), BF), pltpu.SemaphoreType.DMA((n,))],
-    )(*arrays)
+    )(*(pltpu.with_memory_space_constraint(a, pltpu.HBM) for a in arrays))
 
 
 def by_array(mine, other):
@@ -197,17 +197,27 @@
     unit, rows, tail = N_X * own, own - 1, width // (own - 1)
     count = total.shape[0] // unit
 
-    def kernel(ref, *out):
+    def kernel(ref, *refs):
+        out, held, sem = refs[:count], refs[count], refs[count + 1]
+        come = pltpu.make_async_copy(ref, held, sem)
+        come.start()
+        come.wait()
         for u in range(count):
             for k in range(N_X):
                 top = u * unit + k * own
-                out[u][k * rows : (k + 1) * rows, :width] = ref[top : top + rows, :]
+                out[u][k * rows : (k + 1) * rows, :width] = held[top : top + rows, :]
                 for i in range(rows):
-                    part = ref[top + rows : top + own, i * tail : (i + 1) * tail]
+                    part = held[top + rows : top + own, i * tail : (i + 1) * tail]
                     out[u][k * rows + i : k * rows + i + 1, width:] = part
 
     spec = [jax.ShapeDtypeStruct((N_X * rows, width + tail), BF)] * count
-    return call(kernel, spec, [WHOLE], 6 * total.shape[0] * width)(total)
+    return call(
+        kernel,
+        spec,
+        [ANYWHERE],
+        6 * total.shape[0] * width,
+        scratch_shapes=[pltpu.VMEM(total.shape, BF), pltpu.SemaphoreType.DMA],
+    )(pltpu.with_memory_space_constraint(total, pltpu.HBM))
 
 
 def place_rows(place, mine, other):
@@ -488,12 +498,14 @@
     z4 = [fetch(z3[:, :cut], "z", 1), fetch(z5[:, cut:], "z", -1)]
     z4, later = tie((z4, kept[1]))
     rest = join([[z3], [z5], z4])
-    kept_turned = turn(kept)
-    n1, n3, rest, kept_turned, away = tie((n1, n3, rest, kept_turned, away))
+    n1, n3, rest, away = tie((n1, n3, rest, away))
     n2 = [fetch(n1[:, :cut], "y", 1), fetch(n3[:, cut:], "y", -1)]
     r1, r3 = fetch(rest, "y", 1), fetch(rest, "y", -1)
     away = [away[0], fetch(later, "x_hi", 1)]
-    n2, r1, r3, away, beside_turned = tie((n2, r1, r3, away, turn(beside_kept)))
+    kept_turned, beside_turned = turn(kept), turn(beside_kept)
+    n2, r1, r3, away, kept_turned, beside_turned = tie(
+        (n2, r1, r3, away, kept_turned, beside_turned)
+    )
     r2 = [fetch(r1[:, :cut], "y", 1), fetch(r3[:, cut:], "y", -1)]
     beside_away = [fetch(half, "core", 1) for half in away]
     blocks = [kept, away, beside_kept, beside_away]

time: 193 us -> 192 us (level)
  local copies, waits for them, and re-layouts: 9.24 us -> 6.39 us
    unnamed x51 -> x45, local copies, waits for them, and re-layouts: 7.11 us -> 4.24 us
  transfers between devices with their start and end apart: 36 -> 36, of which waited for: 16 -> 17; matrix products, arithmetic and copies ran while one was open for 5% -> 6% of each run, Pallas kernels for 12% -> 13%
where the time goes in v2:
time: 192 us
  waiting for transfers between devices  76.5 us (40%)
  starting transfers between devices  43.4 us (23%)
  Pallas kernels  42.5 us (22%)
  between operations  14.5 us (8%)
  other arithmetic  7.36 us (4%)
  local copies, waits for them, and re-layouts  6.39 us (3%)
    ppermute x34, starting transfers between devices, fetch(): lax.ppermute(block, axis, [(i, (i - offset) % size) for i in range(size)])  43.3 us
    ppermute x34, waiting for transfers between devices, fetch(): lax.ppermute(block, axis, [(i, (i - offset) % size) for i in range(size)])  40 us
    reduce_scatter x1, waiting for transfers between devices, per_device(): total = lax.psum_scatter(total, 'z', scatter_dimension=0, tiled=True)  35.6 us
    pallas_call x2, Pallas kernels, weight_grads(): call(kernel, [jax.ShapeDtypeStruct((2, hid, cols), BF), jax.ShapeDtypeStr...  15.2 us
    pallas_call x1, Pallas kernels, middle(): call(kernel, [jax.ShapeDtypeStruct((N_Z, block, 2 * hid), BF), jax.ShapeD...  14.1 us
    pallas_call x4, Pallas kernels, turn(): call(kernel, jax.ShapeDtypeStruct((cols, 2 * rows), BF), [ANYWHERE] * 2,...  8.27 us
    unnamed x45, local copies, waits for them, and re-layouts  4.24 us
  transfers between devices with their start and end apart: 36, of which 17 were waited for; matrix products, arithmetic and copies ran while one was open for 6% of the time, Pallas kernels for 13%

profile of v2, /device:TPU:2, one launch (start us, length us, event | category | flops | bytes accessed | tf_op | source)
XLA Modules:
  0.0 191.7 jit_solution(1038789519715089339)
XLA Ops:
  8.2 2.4 %collective-permute-start = (bf16[16,4608]{1,0:T(8,128)(2,1)S(1)}, bf16[16,4608]{1,0:T(8,128)(2,1)S(1)}, u32[]{:S(2)}, u32[]{:S(2)}) collective-permute-start(bf16[16,4608]{1,0:T(8,128)(2,1)S(1)} %shard_map.102.mine_ref), channel_id=1, source_target_pairs={{0,32},{32,0},{1,33},{33,1},{2,34},{34,2},{3,35},{35,3},{4,36},{36... | collective-permute-start | bytes 442376 | tf_op jit(solution)/shard_map/ppermute | solution.py:52
  11.8 1.0 copy-done.7
  12.8 1.0 copy-done.8
  13.8 1.0 copy-done.9
  15.2 1.8 collective-permute-start.3
  17.3 1.9 %collective-permute-start.5 = (bf16[16,4608]{1,0:T(8,128)(2,1)S(1)}, bf16[16,4608]{1,0:T(8,128)(2,1)S(1)}, u32[]{:S(2)}, u32[]{:S(2)}) collective-permute-start(bf16[16,4608]{1,0:T(8,128)(2,1)S(1)} %get-tuple-element.72.refs_0_), channel_id=1, source_target_pairs={{0,16},{8,24},{16,0},{24,8},{1,17},{9,25},{17,1},{25,9},{2,18},{10... | collective-permute-start | bytes 442376 | tf_op jit(solution)/shard_map/ppermute | solution.py:52
  19.2 5.9 %collective-permute-start.1 = (bf16[16,4608]{1,0:T(8,128)(2,1)S(1)}, bf16[16,4608]{1,0:T(8,128)(2,1)S(1)}, u32[]{:S(2)}, u32[]{:S(2)}) collective-permute-start(bf16[16,4608]{1,0:T(8,128)(2,1)S(1)} %get-tuple-element.73.refs_0_), channel_id=1, source_target_pairs={{0,7},{1,0},{2,1},{3,2},{4,3},{5,4},{6,5},{7,6},{8,15},{9,8},{10,9... | collective-permute-start | bytes 442376 | tf_op jit(solution)/shard_map/ppermute | solution.py:52
  26.0 1.8 collective-permute-done.1.refs_1_
  27.8 3.7 %collective-permute-done.2.refs_2_ = bf16[16,4608]{1,0:T(8,128)(2,1)S(1)} collective-permute-done((bf16[16,4608]{1,0:T(8,128)(2,1)S(1)}, bf16[16,4608]{1,0:T(8,128)(2,1)S(1)}, u32[]{:S(2)}, u32[]{:S(2)}) %collective-permute-start.2) | collective-permute-done | bytes 147488 | tf_op jit(solution)/shard_map/ppermute | solution.py:52
  33.5 1.6 collective-permute-start.7
  35.1 2.1 %collective-permute-start.16 = (bf16[384,1024]{1,0:T(8,128)(2,1)S(1)}, bf16[384,1024]{1,0:T(8,128)(2,1)}, u32[]{:S(2)}, u32[]{:S(2)}) collective-permute-start(bf16[384,1024]{1,0:T(8,128)(2,1)S(1)} %get-tuple-element.79.top.refs_14_), channel_id=1, source_target_pairs={{0,128},{128,0},{1,129},{129,1},{2,130},{130,2},{3,131},{131,3},{4... | collective-permute-start | bytes 2359304 | tf_op jit(solution)/shard_map/ppermute | solution.py:52
  37.3 1.7 collective-permute-done.6.refs_3_
  39.0 1.3 collective-permute-done.7.refs_4_
  40.4 1.0 collective-permute-start.10
  41.4 1.1 collective-permute-start.11
  42.8 1.7 collective-permute-start.13
  44.5 7.1 %collective-permute-done.12.refs_0_ = bf16[16,4608]{1,0:T(8,128)(2,1)S(1)} collective-permute-done((bf16[16,4608]{1,0:T(8,128)(2,1)S(1)}, bf16[16,4608]{1,0:T(8,128)(2,1)S(1)}, u32[]{:S(2)}, u32[]{:S(2)}) %collective-permute-start.12) | collective-permute-done | bytes 147488 | tf_op jit(solution)/shard_map/ppermute | solution.py:52
  51.6 1.5 collective-permute-done.13.refs_1_
  53.3 1.8 collective-permute-start.15
  55.1 3.9 %collective-permute-done.14.refs_2_ = bf16[16,2304]{1,0:T(8,128)(2,1)S(1)} collective-permute-done((bf16[16,2304]{1,0:T(8,128)(2,1)S(1)}, bf16[16,2304]{1,0:T(8,128)(2,1)S(1)}, u32[]{:S(2)}, u32[]{:S(2)}) %collective-permute-start.14) | collective-permute-done | bytes 73760 | tf_op jit(solution)/shard_map/ppermute | solution.py:52
  59.0 1.5 collective-permute-done.15.refs_3_
  60.5 2.3 %collective-permute-start.21 = (bf16[384,1024]{1,0:T(8,128)(2,1)S(1)}, bf16[384,1024]{1,0:T(8,128)(2,1)}, u32[]{:S(2)}, u32[]{:S(2)}) collective-permute-start(bf16[384,1024]{1,0:T(8,128)(2,1)S(1)} %get-tuple-element.91.bottom.refs_15_), channel_id=1, source_target_pairs={{0,128},{128,0},{1,129},{129,1},{2,130},{130,2},{3,131},{131,3},{4... | collective-permute-start | bytes 2359304 | tf_op jit(solution)/shard_map/ppermute | solution.py:52
  63.0 1.8 collective-permute-start.19
  65.1 3.0 %collective-permute-start.17 = (bf16[80,2304]{1,0:T(8,128)(2,1)S(1)}, bf16[80,2304]{1,0:T(8,128)(2,1)S(1)}, u32[]{:S(2)}, u32[]{:S(2)}) collective-permute-start(bf16[80,2304]{1,0:T(8,128)(2,1)S(1)} %slice.62), channel_id=1, source_target_pairs={{0,24},{8,0},{16,8},{24,16},{1,25},{9,1},{17,9},{25,17},{2,26},{10... | collective-permute-start | bytes 1105928 | tf_op jit(solution)/shard_map/ppermute | solution.py:52
  68.3 1.8 shard_map.108.refs_10_
  70.1 1.8 shard_map.109.refs_12_
  71.9 7.0 %collective-permute-done.21.bottom.refs_17_ = bf16[384,1024]{1,0:T(8,128)(2,1)} collective-permute-done((bf16[384,1024]{1,0:T(8,128)(2,1)S(1)}, bf16[384,1024]{1,0:T(8,128)(2,1)}, u32[]{:S(2)}, u32[]{:S(2)}) %collective-permute-start.21) | collective-permute-done | bytes 786464 | tf_op jit(solution)/shard_map/ppermute | solution.py:52
  79.8 2.2 %collective-permute-done.18.refs_5_ = bf16[80,2304]{1,0:T(8,128)(2,1)S(1)} collective-permute-done((bf16[80,2304]{1,0:T(8,128)(2,1)S(1)}, bf16[80,2304]{1,0:T(8,128)(2,1)S(1)}, u32[]{:S(2)}, u32[]{:S(2)}) %collective-permute-start.18) | collective-permute-done | bytes 368672 | tf_op jit(solution)/shard_map/ppermute | solution.py:52
  83.7 1.7 collective-permute-start.23
  85.6 2.8 %shard_map.110.refs_11_ = bf16[1024,768]{1,0:T(8,128)(2,1)} custom-call(bf16[384,1024]{1,0:T(8,128)(2,1)} %collective-permute-done.16.top.refs_16_, bf16[384,1024]{1,0:T(8,128)(2,1)} %collective-permute-done.21.bottom.refs_17_), custom_call_target="tpu_custom_call" | custom-call | bytes 3145728 | tf_op jit(solution)/shard_map/pallas_call | solution.py:180
  88.5 1.8 shard_map.111.refs_13_
  90.3 2.0 %collective-permute-done.23.refs_7_ = bf16[48,2304]{1,0:T(8,128)(2,1)S(1)} collective-permute-done((bf16[48,2304]{1,0:T(8,128)(2,1)}, bf16[48,2304]{1,0:T(8,128)(2,1)S(1)}, u32[]{:S(2)}, u32[]{:S(2)}) %collective-permute-start.23) | collective-permute-done | bytes 221216 | tf_op jit(solution)/shard_map/ppermute | solution.py:52
  93.2 14.1 %shard_map.112 = (bf16[8,72,512]{2,1,0:T(8,128)(2,1)}, bf16[576,4096]{1,0:T(8,128)(2,1)}, bf16[576,256]{1,0:T(8,128)(2,1)S(1)}, bf16[8,72,4096]{2,1,0:T(8,128)(2,1)}) custom-call(s32[1]{0:T(128)} %bitcast.4.z_ref, s32[4]{0:T(128)S(1)} %pad_add_fusion.place_ref, bf16[576,4096]{1,0:T(8,128)(2,1)} %all-gather.2.cloned.1.call-done.tok_ref.refs_1_, ...), custom_call_target="tpu_custom_call" | custom-call | flops 6039797760 | bytes 31457280 | tf_op jit(solution)/shard_map/pallas_call | solution.py:371
  108.4 9.0 %shard_map.114 = (bf16[2,512,1024]{2,1,0:T(8,128)(2,1)}, f32[2,512,1024]{2,1,0:T(8,128)}) custom-call(s32[4]{0:T(128)S(1)} %rev.3.order_ref, bf16[576,512]{1,0:T(8,128)(2,1)S(1)} %bitcast.52, bf16[576,4096]{1,0:T(8,128)(2,1)} %all-gather.2.cloned.1.call-done.tok_ref.refs_1_), custom_call_target="tpu_custom_call" | custom-call | flops 2415919104 | bytes 11010048 | tf_op jit(solution)/shard_map/pallas_call | solution.py:445
  117.6 6.1 %shard_map.115 = (bf16[2,256,1024]{2,1,0:T(8,128)(2,1)S(1)}, f32[2,256,1024]{2,1,0:T(8,128)}) custom-call(s32[4]{0:T(128)S(1)} %rev.3.order_ref, bf16[576,256]{1,0:T(8,128)(2,1)S(1)} %get-tuple-element.117.refs_0_, bf16[576,4096]{1,0:T(8,128)(2,1)} %get-tuple-element.118.refs_1_), custom_call_target="tpu_custom_call" | custom-call | flops 1207959552 | bytes 7864320 | tf_op jit(solution)/shard_map/pallas_call | solution.py:445
  124.3 1.3 fusion.1
  125.6 2.1 %collective-permute-start.30 = (bf16[512,1024]{1,0:T(8,128)(2,1)}, bf16[512,1024]{1,0:T(8,128)(2,1)}, u32[]{:S(2)}, u32[]{:S(2)}) collective-permute-start(bf16[512,1024]{1,0:T(8,128)(2,1)} %fusion.1), channel_id=1, source_target_pairs={{0,128},{128,0},{1,129},{129,1},{2,130},{130,2},{3,131},{131,3},{4... | collective-permute-start | bytes 3145736 | tf_op jit(solution)/shard_map/ppermute | solution.py:52
  128.7 1.4 collective-permute-start.32
  130.3 35.6 %reduce-scatter.2.cloned.1.call-done.ref = bf16[72,4096]{1,0:T(8,128)(2,1)} async-done(((bf16[576,4096]{1,0:T(8,128)(2,1)}), bf16[72,4096]{1,0:T(8,128)(2,1)}) %reduce-scatter.2.cloned.1.call-update) | async-done | bytes 589840 | tf_op jit(solution)/shard_map/reduce_scatter | solution.py:519
  165.9 1.3 shard_map.113
  167.2 1.6 collective-permute-start.26
  168.8 1.7 collective-permute-start.27
  170.6 1.8 collective-permute-start.28
  172.4 2.7 %bitcast_add_fusion = f32[512,1024]{1,0:T(8,128)S(1)} fusion(bf16[512,1024]{1,0:T(8,128)(2,1)} %collective-permute-done.30, f32[2,512,1024]{2,1,0:T(8,128)} %get-tuple-element.115, bf16[2,512,1024]{2,1,0:T(8,128)(2,1)} %copy-done.15), kind=kLoop, calls=%fused_computation.2 | loop fusion | flops 2097152 | bytes 6291456 | tf_op jit(solution)/shard_map/add | solution.py:531
  175.3 2.1 %fusion.2 = bf16[256,1024]{1,0:T(8,128)(2,1)} fusion(bf16[256,1024]{1,0:T(8,128)(2,1)} %collective-permute-done.32, f32[2,256,1024]{2,1,0:T(8,128)S(1)} %copy-done.14, bf16[2,256,1024]{2,1,0:T(8,128)(2,1)S(1)} %collective-permute-done.31, f32[2,1024]{1,0:T(2,128)S(1)} %bitcast.56), kind=kLoop, calls=%fused_computation.6 | loop fusion | flops 1572864 | bytes 2629632 | tf_op jit(solution)/shard_map/convert_element_type | solution.py:533
  179.0 1.0 slice_bitcast_fusion
  180.1 3.6 %collective-permute-done.33.other_ref = f32[8,4608]{1,0:T(8,128)S(1)} collective-permute-done((f32[8,4608]{1,0:T(8,128)S(1)}, f32[8,4608]{1,0:T(8,128)S(1)}, u32[]{:S(2)}, u32[]{:S(2)}) %collective-permute-start.33) | collective-permute-done | bytes 147488 | tf_op jit(solution)/shard_map/ppermute | solution.py:52
  183.6 1.2 shard_map.117
  (109 shorter events, 15.0 us)
Async XLA Ops:
  7.2 86.0 %all-gather.2.cloned.1.call-start = ((), (), s32[]{:S(2)}) async-start(), calls=%async_computation.1 | async-start | bytes 5308416 | tf_op jit(solution)/shard_map/all_gather | solution.py:490
  8.2 6.9 %collective-permute-start = (bf16[16,4608]{1,0:T(8,128)(2,1)S(1)}, bf16[16,4608]{1,0:T(8,128)(2,1)S(1)}, u32[]{:S(2)}, u32[]{:S(2)}) collective-permute-start(bf16[16,4608]{1,0:T(8,128)(2,1)S(1)} %shard_map.102.mine_ref), channel_id=1, source_target_pairs={{0,32},{32,0},{1,33},{33,1},{2,34},{34,2},{3,35},{35,3},{4,36},{36... | collective-permute-start | bytes 442376 | tf_op jit(solution)/shard_map/ppermute | solution.py:52
  11.6 116.1 %copy-start.20 = (f32[3,2,8]{2,1,0:T(2,128)}, f32[3,2,8]{2,1,0:T(2,128)S(1)}, u32[]{:S(2)}) copy-start(f32[3,2,8]{2,1,0:T(2,128)S(1)} %dynamic-slice_bitcast_fusion) | copy-start | bytes 580
  15.1 53.1 %copy-start = (bf16[384,1024]{1,0:T(8,128)(2,1)}, bf16[384,1024]{1,0:T(8,128)(2,1)S(1)}, u32[]{:S(2)}) copy-start(bf16[384,1024]{1,0:T(8,128)(2,1)S(1)} %get-tuple-element.79.top.refs_14_) | copy-start | bytes 2359300
  15.1 53.1 %copy-start.1 = (bf16[384,1024]{1,0:T(8,128)(2,1)}, bf16[384,1024]{1,0:T(8,128)(2,1)S(1)}, u32[]{:S(2)}) copy-start(bf16[384,1024]{1,0:T(8,128)(2,1)S(1)} %get-tuple-element.91.bottom.refs_15_) | copy-start | bytes 2359300
  15.2 9.9 %collective-permute-start.3 = (bf16[16,4608]{1,0:T(8,128)(2,1)S(1)}, bf16[16,4608]{1,0:T(8,128)(2,1)S(1)}, u32[]{:S(2)}, u32[]{:S(2)}) collective-permute-start(bf16[16,4608]{1,0:T(8,128)(2,1)S(1)} %get-tuple-element.72.refs_0_), channel_id=1, source_target_pairs={{0,24},{8,0},{16,8},{24,16},{1,25},{9,1},{17,9},{25,17},{2,26},{10... | collective-permute-start | bytes 442376 | tf_op jit(solution)/shard_map/ppermute | solution.py:52
  17.0 8.9 %collective-permute-start.4 = (bf16[16,4608]{1,0:T(8,128)(2,1)S(1)}, bf16[16,4608]{1,0:T(8,128)(2,1)S(1)}, u32[]{:S(2)}, u32[]{:S(2)}) collective-permute-start(bf16[16,4608]{1,0:T(8,128)(2,1)S(1)} %get-tuple-element.72.refs_0_), channel_id=1, source_target_pairs={{0,8},{8,16},{16,24},{24,0},{1,9},{9,17},{17,25},{25,1},{2,10},{10... | collective-permute-start | bytes 442376 | tf_op jit(solution)/shard_map/ppermute | solution.py:52
  17.3 8.7 %collective-permute-start.5 = (bf16[16,4608]{1,0:T(8,128)(2,1)S(1)}, bf16[16,4608]{1,0:T(8,128)(2,1)S(1)}, u32[]{:S(2)}, u32[]{:S(2)}) collective-permute-start(bf16[16,4608]{1,0:T(8,128)(2,1)S(1)} %get-tuple-element.72.refs_0_), channel_id=1, source_target_pairs={{0,16},{8,24},{16,0},{24,8},{1,17},{9,25},{17,1},{25,9},{2,18},{10... | collective-permute-start | bytes 442376 | tf_op jit(solution)/shard_map/ppermute | solution.py:52
  19.2 8.5 %collective-permute-start.1 = (bf16[16,4608]{1,0:T(8,128)(2,1)S(1)}, bf16[16,4608]{1,0:T(8,128)(2,1)S(1)}, u32[]{:S(2)}, u32[]{:S(2)}) collective-permute-start(bf16[16,4608]{1,0:T(8,128)(2,1)S(1)} %get-tuple-element.73.refs_0_), channel_id=1, source_target_pairs={{0,7},{1,0},{2,1},{3,2},{4,3},{5,4},{6,5},{7,6},{8,15},{9,8},{10,9... | collective-permute-start | bytes 442376 | tf_op jit(solution)/shard_map/ppermute | solution.py:52
  25.1 6.4 %collective-permute-start.2 = (bf16[16,4608]{1,0:T(8,128)(2,1)S(1)}, bf16[16,4608]{1,0:T(8,128)(2,1)S(1)}, u32[]{:S(2)}, u32[]{:S(2)}) collective-permute-start(bf16[16,4608]{1,0:T(8,128)(2,1)S(1)} %get-tuple-element.73.refs_0_), channel_id=1, source_target_pairs={{0,1},{1,2},{2,3},{3,4},{4,5},{5,6},{6,7},{7,0},{8,9},{9,10},{10,1... | collective-permute-start | bytes 442376 | tf_op jit(solution)/shard_map/ppermute | solution.py:52
  32.5 133.5 %reduce-scatter.2.cloned.1.call-start = ((), (), s32[]{:S(2)}) async-start(), calls=%async_computation.2 | async-start | bytes 5308416 | tf_op jit(solution)/shard_map/reduce_scatter | solution.py:519
  32.5 7.8 %collective-permute-start.8 = (bf16[384,1024]{1,0:T(8,128)(2,1)S(1)}, bf16[384,1024]{1,0:T(8,128)(2,1)S(1)}, u32[]{:S(2)}, u32[]{:S(2)}) collective-permute-start(bf16[384,1024]{1,0:T(8,128)(2,1)S(1)} %get-tuple-element.79.top.refs_14_), channel_id=1, source_target_pairs={{0,64},{64,0},{1,65},{65,1},{2,66},{66,2},{3,67},{67,3},{4,68},{68... | collective-permute-start | bytes 2359304 | tf_op jit(solution)/shard_map/ppermute | solution.py:52
  32.6 7.7 %collective-permute-start.9 = (bf16[384,1024]{1,0:T(8,128)(2,1)S(1)}, bf16[384,1024]{1,0:T(8,128)(2,1)S(1)}, u32[]{:S(2)}, u32[]{:S(2)}) collective-permute-start(bf16[384,1024]{1,0:T(8,128)(2,1)S(1)} %get-tuple-element.91.bottom.refs_15_), channel_id=1, source_target_pairs={{0,64},{64,0},{1,65},{65,1},{2,66},{66,2},{3,67},{67,3},{4,68},{68... | collective-permute-start | bytes 2359304 | tf_op jit(solution)/shard_map/ppermute | solution.py:52
  33.1 5.9 %collective-permute-start.6 = (bf16[16,4608]{1,0:T(8,128)(2,1)S(1)}, bf16[16,4608]{1,0:T(8,128)(2,1)S(1)}, u32[]{:S(2)}, u32[]{:S(2)}) collective-permute-start(bf16[16,4608]{1,0:T(8,128)(2,1)S(1)} %collective-permute-done.1.refs_1_), channel_id=1, source_target_pairs={{0,7},{1,0},{2,1},{3,2},{4,3},{5,4},{6,5},{7,6},{8,15},{9,8},{10,9... | collective-permute-start | bytes 442376 | tf_op jit(solution)/shard_map/ppermute | solution.py:52
  33.5 6.8 %collective-permute-start.7 = (bf16[16,4608]{1,0:T(8,128)(2,1)S(1)}, bf16[16,4608]{1,0:T(8,128)(2,1)S(1)}, u32[]{:S(2)}, u32[]{:S(2)}) collective-permute-start(bf16[16,4608]{1,0:T(8,128)(2,1)S(1)} %collective-permute-done.2.refs_2_), channel_id=1, source_target_pairs={{0,1},{1,2},{2,3},{3,4},{4,5},{5,6},{6,7},{7,0},{8,9},{9,10},{10,1... | collective-permute-start | bytes 442376 | tf_op jit(solution)/shard_map/ppermute | solution.py:52
  35.1 27.8 %collective-permute-start.16 = (bf16[384,1024]{1,0:T(8,128)(2,1)S(1)}, bf16[384,1024]{1,0:T(8,128)(2,1)}, u32[]{:S(2)}, u32[]{:S(2)}) collective-permute-start(bf16[384,1024]{1,0:T(8,128)(2,1)S(1)} %get-tuple-element.79.top.refs_14_), channel_id=1, source_target_pairs={{0,128},{128,0},{1,129},{129,1},{2,130},{130,2},{3,131},{131,3},{4... | collective-permute-start | bytes 2359304 | tf_op jit(solution)/shard_map/ppermute | solution.py:52
  40.3 29.8 %copy-start.2 = (bf16[384,1024]{1,0:T(8,128)(2,1)}, bf16[384,1024]{1,0:T(8,128)(2,1)S(1)}, u32[]{:S(2)}) copy-start(bf16[384,1024]{1,0:T(8,128)(2,1)S(1)} %collective-permute-done.8.top.refs_18_) | copy-start | bytes 2359300
  40.3 29.8 %copy-start.3 = (bf16[384,1024]{1,0:T(8,128)(2,1)}, bf16[384,1024]{1,0:T(8,128)(2,1)S(1)}, u32[]{:S(2)}) copy-start(bf16[384,1024]{1,0:T(8,128)(2,1)S(1)} %collective-permute-done.9.bottom.refs_19_) | copy-start | bytes 2359300
  40.4 22.6 %copy-start.6 = (bf16[80,4608]{1,0:T(8,128)(2,1)}, bf16[80,4608]{1,0:T(8,128)(2,1)S(1)}, u32[]{:S(2)}) copy-start(bf16[80,4608]{1,0:T(8,128)(2,1)S(1)} %shard_map.106.refs_0_) | copy-start | bytes 2211844
  40.4 22.6 %collective-permute-start.10 = (bf16[80,4608]{1,0:T(8,128)(2,1)S(1)}, bf16[80,4608]{1,0:T(8,128)(2,1)S(1)}, u32[]{:S(2)}, u32[]{:S(2)}) collective-permute-start(bf16[80,4608]{1,0:T(8,128)(2,1)S(1)} %shard_map.106.refs_0_), channel_id=1, source_target_pairs={{0,24},{8,0},{16,8},{24,16},{1,25},{9,1},{17,9},{25,17},{2,26},{10... | collective-permute-start | bytes 2211848 | tf_op jit(solution)/shard_map/ppermute | solution.py:52
  41.4 21.6 %collective-permute-start.11 = (bf16[80,4608]{1,0:T(8,128)(2,1)S(1)}, bf16[80,4608]{1,0:T(8,128)(2,1)S(1)}, u32[]{:S(2)}, u32[]{:S(2)}) collective-permute-start(bf16[80,4608]{1,0:T(8,128)(2,1)S(1)} %shard_map.106.refs_0_), channel_id=1, source_target_pairs={{0,8},{8,16},{16,24},{24,0},{1,9},{9,17},{17,25},{25,1},{2,10},{10... | collective-permute-start | bytes 2211848 | tf_op jit(solution)/shard_map/ppermute | solution.py:52
  42.5 9.1 %collective-permute-start.12 = (bf16[16,4608]{1,0:T(8,128)(2,1)S(1)}, bf16[16,4608]{1,0:T(8,128)(2,1)S(1)}, u32[]{:S(2)}, u32[]{:S(2)}) collective-permute-start(bf16[16,4608]{1,0:T(8,128)(2,1)S(1)} %collective-permute-done.6.refs_3_), channel_id=1, source_target_pairs={{0,7},{1,0},{2,1},{3,2},{4,3},{5,4},{6,5},{7,6},{8,15},{9,8},{10,9... | collective-permute-start | bytes 442376 | tf_op jit(solution)/shard_map/ppermute | solution.py:52
  42.8 10.3 %collective-permute-start.13 = (bf16[16,4608]{1,0:T(8,128)(2,1)S(1)}, bf16[16,4608]{1,0:T(8,128)(2,1)S(1)}, u32[]{:S(2)}, u32[]{:S(2)}) collective-permute-start(bf16[16,4608]{1,0:T(8,128)(2,1)S(1)} %collective-permute-done.7.refs_4_), channel_id=1, source_target_pairs={{0,1},{1,2},{2,3},{3,4},{4,5},{5,6},{6,7},{7,0},{8,9},{9,10},{10,1... | collective-permute-start | bytes 442376 | tf_op jit(solution)/shard_map/ppermute | solution.py:52
  53.1 5.9 %collective-permute-start.14 = (bf16[16,2304]{1,0:T(8,128)(2,1)S(1)}, bf16[16,2304]{1,0:T(8,128)(2,1)S(1)}, u32[]{:S(2)}, u32[]{:S(2)}) collective-permute-start(bf16[16,2304]{1,0:T(8,128)(2,1)S(1)} %slice.60), channel_id=1, source_target_pairs={{0,7},{1,0},{2,1},{3,2},{4,3},{5,4},{6,5},{7,6},{8,15},{9,8},{10,9... | collective-permute-start | bytes 221192 | tf_op jit(solution)/shard_map/ppermute | solution.py:52
  53.3 7.2 %collective-permute-start.15 = (bf16[16,2304]{1,0:T(8,128)(2,1)S(1)}, bf16[16,2304]{1,0:T(8,128)(2,1)S(1)}, u32[]{:S(2)}, u32[]{:S(2)}) collective-permute-start(bf16[16,2304]{1,0:T(8,128)(2,1)S(1)} %slice.61), channel_id=1, source_target_pairs={{0,1},{1,2},{2,3},{3,4},{4,5},{5,6},{6,7},{7,0},{8,9},{9,10},{10,1... | collective-permute-start | bytes 221192 | tf_op jit(solution)/shard_map/ppermute | solution.py:52
  60.5 18.4 %collective-permute-start.21 = (bf16[384,1024]{1,0:T(8,128)(2,1)S(1)}, bf16[384,1024]{1,0:T(8,128)(2,1)}, u32[]{:S(2)}, u32[]{:S(2)}) collective-permute-start(bf16[384,1024]{1,0:T(8,128)(2,1)S(1)} %get-tuple-element.91.bottom.refs_15_), channel_id=1, source_target_pairs={{0,128},{128,0},{1,129},{129,1},{2,130},{130,2},{3,131},{131,3},{4... | collective-permute-start | bytes 2359304 | tf_op jit(solution)/shard_map/ppermute | solution.py:52
  62.9 7.2 %copy-start.10 = (bf16[48,4608]{1,0:T(8,128)(2,1)}, bf16[48,4608]{1,0:T(8,128)(2,1)S(1)}, u32[]{:S(2)}) copy-start(bf16[48,4608]{1,0:T(8,128)(2,1)S(1)} %shard_map.107.refs_1_) | copy-start | bytes 1327108
  62.9 7.2 %copy-start.16 = (bf16[80,4608]{1,0:T(8,128)(2,1)}, bf16[80,4608]{1,0:T(8,128)(2,1)S(1)}, u32[]{:S(2)}) copy-start(bf16[80,4608]{1,0:T(8,128)(2,1)S(1)} %collective-permute-done.10.refs_2_) | copy-start | bytes 2211844
  63.0 7.1 %copy-start.17 = (bf16[80,4608]{1,0:T(8,128)(2,1)}, bf16[80,4608]{1,0:T(8,128)(2,1)S(1)}, u32[]{:S(2)}) copy-start(bf16[80,4608]{1,0:T(8,128)(2,1)S(1)} %collective-permute-done.11.refs_8_) | copy-start | bytes 2211844
  63.0 19.1 %collective-permute-start.19 = (bf16[48,4608]{1,0:T(8,128)(2,1)S(1)}, bf16[48,4608]{1,0:T(8,128)(2,1)S(1)}, u32[]{:S(2)}, u32[]{:S(2)}) collective-permute-start(bf16[48,4608]{1,0:T(8,128)(2,1)S(1)} %shard_map.107.refs_1_), channel_id=1, source_target_pairs={{0,24},{8,0},{16,8},{24,16},{1,25},{9,1},{17,9},{25,17},{2,26},{10... | collective-permute-start | bytes 1327112 | tf_op jit(solution)/shard_map/ppermute | solution.py:52
  64.8 17.3 %collective-permute-start.20 = (bf16[48,4608]{1,0:T(8,128)(2,1)S(1)}, bf16[48,4608]{1,0:T(8,128)(2,1)S(1)}, u32[]{:S(2)}, u32[]{:S(2)}) collective-permute-start(bf16[48,4608]{1,0:T(8,128)(2,1)S(1)} %shard_map.107.refs_1_), channel_id=1, source_target_pairs={{0,8},{8,16},{16,24},{24,0},{1,9},{9,17},{17,25},{25,1},{2,10},{10... | collective-permute-start | bytes 1327112 | tf_op jit(solution)/shard_map/ppermute | solution.py:52
  65.1 14.7 %collective-permute-start.17 = (bf16[80,2304]{1,0:T(8,128)(2,1)S(1)}, bf16[80,2304]{1,0:T(8,128)(2,1)S(1)}, u32[]{:S(2)}, u32[]{:S(2)}) collective-permute-start(bf16[80,2304]{1,0:T(8,128)(2,1)S(1)} %slice.62), channel_id=1, source_target_pairs={{0,24},{8,0},{16,8},{24,16},{1,25},{9,1},{17,9},{25,17},{2,26},{10... | collective-permute-start | bytes 1105928 | tf_op jit(solution)/shard_map/ppermute | solution.py:52
  68.1 13.9 %collective-permute-start.18 = (bf16[80,2304]{1,0:T(8,128)(2,1)S(1)}, bf16[80,2304]{1,0:T(8,128)(2,1)S(1)}, u32[]{:S(2)}, u32[]{:S(2)}) collective-permute-start(bf16[80,2304]{1,0:T(8,128)(2,1)S(1)} %slice.63), channel_id=1, source_target_pairs={{0,8},{8,16},{16,24},{24,0},{1,9},{9,17},{17,25},{25,1},{2,10},{10... | collective-permute-start | bytes 1105928 | tf_op jit(solution)/shard_map/ppermute | solution.py:52
  82.1 6.4 %collective-permute-start.24 = (bf16[384,1024]{1,0:T(8,128)(2,1)}, bf16[384,1024]{1,0:T(8,128)(2,1)S(1)}, u32[]{:S(2)}, u32[]{:S(2)}) collective-permute-start(bf16[384,1024]{1,0:T(8,128)(2,1)} %collective-permute-done.16.top.refs_16_), channel_id=1, source_target_pairs={{0,64},{64,0},{1,65},{65,1},{2,66},{66,2},{3,67},{67,3},{4,68},{68... | collective-permute-start | bytes 2359304 | tf_op jit(solution)/shard_map/ppermute | solution.py:52
  82.2 6.3 %collective-permute-start.25 = (bf16[384,1024]{1,0:T(8,128)(2,1)}, bf16[384,1024]{1,0:T(8,128)(2,1)S(1)}, u32[]{:S(2)}, u32[]{:S(2)}) collective-permute-start(bf16[384,1024]{1,0:T(8,128)(2,1)} %collective-permute-done.21.bottom.refs_17_), channel_id=1, source_target_pairs={{0,64},{64,0},{1,65},{65,1},{2,66},{66,2},{3,67},{67,3},{4,68},{68... | collective-permute-start | bytes 2359304 | tf_op jit(solution)/shard_map/ppermute | solution.py:52
  82.7 7.6 %collective-permute-start.22 = (bf16[48,2304]{1,0:T(8,128)(2,1)S(1)}, bf16[48,2304]{1,0:T(8,128)(2,1)S(1)}, u32[]{:S(2)}, u32[]{:S(2)}) collective-permute-start(bf16[48,2304]{1,0:T(8,128)(2,1)S(1)} %slice.64), channel_id=1, source_target_pairs={{0,24},{8,0},{16,8},{24,16},{1,25},{9,1},{17,9},{25,17},{2,26},{10... | collective-permute-start | bytes 663560 | tf_op jit(solution)/shard_map/ppermute | solution.py:52
  83.7 8.6 %collective-permute-start.23 = (bf16[48,2304]{1,0:T(8,128)(2,1)}, bf16[48,2304]{1,0:T(8,128)(2,1)S(1)}, u32[]{:S(2)}, u32[]{:S(2)}) collective-permute-start(bf16[48,2304]{1,0:T(8,128)(2,1)} %slice.65), channel_id=1, source_target_pairs={{0,8},{8,16},{16,24},{24,0},{1,9},{9,17},{17,25},{25,1},{2,10},{10... | collective-permute-start | bytes 663560 | tf_op jit(solution)/shard_map/ppermute | solution.py:52
  88.4 4.8 %copy-start.11 = (bf16[48,4608]{1,0:T(8,128)(2,1)S(1)}, bf16[48,4608]{1,0:T(8,128)(2,1)}, u32[]{:S(2)}) copy-start(bf16[48,4608]{1,0:T(8,128)(2,1)} %copy-done.10) | copy-start | bytes 1327108
  88.4 4.7 %copy-start.4 = (bf16[384,1024]{1,0:T(8,128)(2,1)}, bf16[384,1024]{1,0:T(8,128)(2,1)S(1)}, u32[]{:S(2)}) copy-start(bf16[384,1024]{1,0:T(8,128)(2,1)S(1)} %collective-permute-done.24.top.refs_20_) | copy-start | bytes 2359300
  117.5 6.3 %collective-permute-start.29 = (bf16[2,512,1024]{2,1,0:T(8,128)(2,1)}, bf16[2,512,1024]{2,1,0:T(8,128)(2,1)S(1)}, u32[]{:S(2)}, u32[]{:S(2)}) collective-permute-start(bf16[2,512,1024]{2,1,0:T(8,128)(2,1)} %get-tuple-element.116), channel_id=1, source_target_pairs={{0,64},{64,0},{1,65},{65,1},{2,66},{66,2},{3,67},{67,3},{4,68},{68... | collective-permute-start | bytes 6291464 | tf_op jit(solution)/shard_map/ppermute | solution.py:52
  117.6 6.7 %copy-start.13 = (f32[2,512,1024]{2,1,0:T(8,128)S(1)}, f32[2,512,1024]{2,1,0:T(8,128)}, u32[]{:S(2)}) copy-start(f32[2,512,1024]{2,1,0:T(8,128)} %get-tuple-element.115) | copy-start | bytes 12582916
  123.7 4.0 %collective-permute-start.31 = (bf16[2,256,1024]{2,1,0:T(8,128)(2,1)S(1)}, bf16[2,256,1024]{2,1,0:T(8,128)(2,1)S(1)}, u32[]{:S(2)}, u32[]{:S(2)}) collective-permute-start(bf16[2,256,1024]{2,1,0:T(8,128)(2,1)S(1)} %get-tuple-element.123), channel_id=1, source_target_pairs={{0,64},{64,0},{1,65},{65,1},{2,66},{66,2},{3,67},{67,3},{4,68},{68... | collective-permute-start | bytes 3145736 | tf_op jit(solution)/shard_map/ppermute | solution.py:52
  125.6 46.7 %collective-permute-start.30 = (bf16[512,1024]{1,0:T(8,128)(2,1)}, bf16[512,1024]{1,0:T(8,128)(2,1)}, u32[]{:S(2)}, u32[]{:S(2)}) collective-permute-start(bf16[512,1024]{1,0:T(8,128)(2,1)} %fusion.1), channel_id=1, source_target_pairs={{0,128},{128,0},{1,129},{129,1},{2,130},{130,2},{3,131},{131,3},{4... | collective-permute-start | bytes 3145736 | tf_op jit(solution)/shard_map/ppermute | solution.py:52
  128.7 46.6 %collective-permute-start.32 = (bf16[256,1024]{1,0:T(8,128)(2,1)}, bf16[256,1024]{1,0:T(8,128)(2,1)}, u32[]{:S(2)}, u32[]{:S(2)}) collective-permute-start(bf16[256,1024]{1,0:T(8,128)(2,1)} %fusion.3), channel_id=1, source_target_pairs={{0,128},{128,0},{1,129},{129,1},{2,130},{130,2},{3,131},{131,3},{4... | collective-permute-start | bytes 1572872 | tf_op jit(solution)/shard_map/ppermute | solution.py:52
  167.2 10.2 %collective-permute-start.26 = (bf16[16,4608]{1,0:T(8,128)(2,1)S(1)}, bf16[16,4608]{1,0:T(8,128)(2,1)S(1)}, u32[]{:S(2)}, u32[]{:S(2)}) collective-permute-start(bf16[16,4608]{1,0:T(8,128)(2,1)S(1)} %get-tuple-element.111), channel_id=1, source_target_pairs={{0,8},{8,16},{16,24},{24,0},{1,9},{9,17},{17,25},{25,1},{2,10},{10... | collective-permute-start | bytes 442376 | tf_op jit(solution)/shard_map/ppermute | solution.py:52
  168.8 8.6 %collective-permute-start.27 = (bf16[16,4608]{1,0:T(8,128)(2,1)S(1)}, bf16[16,4608]{1,0:T(8,128)(2,1)S(1)}, u32[]{:S(2)}, u32[]{:S(2)}) collective-permute-start(bf16[16,4608]{1,0:T(8,128)(2,1)S(1)} %get-tuple-element.112), channel_id=1, source_target_pairs={{0,24},{8,0},{16,8},{24,16},{1,25},{9,1},{17,9},{25,17},{2,26},{10... | collective-permute-start | bytes 442376 | tf_op jit(solution)/shard_map/ppermute | solution.py:52
  170.6 7.8 %collective-permute-start.28 = (bf16[16,4608]{1,0:T(8,128)(2,1)S(1)}, bf16[16,4608]{1,0:T(8,128)(2,1)S(1)}, u32[]{:S(2)}, u32[]{:S(2)}) collective-permute-start(bf16[16,4608]{1,0:T(8,128)(2,1)S(1)} %get-tuple-element.113), channel_id=1, source_target_pairs={{0,16},{8,24},{16,0},{24,8},{1,17},{9,25},{17,1},{25,9},{2,18},{10... | collective-permute-start | bytes 442376 | tf_op jit(solution)/shard_map/ppermute | solution.py:52
  178.4 5.2 %collective-permute-start.33 = (f32[8,4608]{1,0:T(8,128)S(1)}, f32[8,4608]{1,0:T(8,128)S(1)}, u32[]{:S(2)}, u32[]{:S(2)}) collective-permute-start(f32[8,4608]{1,0:T(8,128)S(1)} %get-tuple-element.129), channel_id=1, source_target_pairs={{0,32},{32,0},{1,33},{33,1},{2,34},{34,2},{3,35},{35,3},{4,36},{36... | collective-permute-start | bytes 442376 | tf_op jit(solution)/shard_map/ppermute | solution.py:52
  (10 other events, 19.5 us)
Sparse Core Ops, SparseCore 0:
  32.6 60.5 all-gather.1
  107.5 58.4 reduce-scatter.1

commit v3 on v2

--- a/solution.py
+++ b/solution.py
@@ -253,7 +253,7 @@
         piece_refs, turned_refs, block_refs = refs[:n], refs[n : n + 4], refs[n + 4 : n + 12]
         first_out, grd_out, hidden_out, out = refs[n + 12 : n + 16]
         packed = refs[n + 16 : n + 16 + m]
-        x, wt, w, grd, g, total_ref, pre, by_z, first_ref, hidden_ref, held, sems, out_sems = refs[n + 16 + m :]
+        x, wt, w, grd, g, total_ref, by_z, first_ref, hidden_ref, held, sems, out_sems = refs[n + 16 + m :]
 
         def bring(source, target, i):
             copy = pltpu.make_async_copy(source, target, sems.at[i])
@@ -296,8 +296,6 @@
             return 0
 
         lax.fori_loop(0, 4, pre_part, 0)
-        for i in range(N_Z):
-            pre[i] = total_ref[i * block : (i + 1) * block, :]
         for copy in come:
             copy.wait()
         for source, (firsts, _) in zip(packed, pieces):
@@ -327,7 +325,8 @@
 
         lax.fori_loop(0, 4, grad_part, 0)
         for dz in range(N_Z):
-            gate_pre, up_pre = pre[spot(dz), :, :hid], pre[spot(dz), :, hid:]
+            held_rows = pl.ds(pl.multiple_of(spot(dz) * block, block), block)
+            gate_pre, up_pre = total_ref[held_rows, :hid], total_ref[held_rows, hid:]
             rows = [slice((dy * N_Z + dz) * unit, (dy * N_Z + dz + 1) * unit) for dy in range(N_Y)]
             grad = jnp.concatenate([g[r, :] for r in rows], axis=0)
             sigma = jax.nn.sigmoid(gate_pre)
@@ -391,7 +390,6 @@
             pltpu.VMEM((total, width), BF),
             pltpu.VMEM((total, hid), F32),
             pltpu.VMEM((total, 2 * hid), F32),
-            pltpu.VMEM((N_Z, block, 2 * hid), F32),
             pltpu.VMEM((total, 2 * hid), BF),
             pltpu.VMEM((N_Z, block, 2 * hid), BF),
             pltpu.VMEM((total, hid), BF),
@@ -536,7 +534,7 @@
     down_grad = finish(keep_b, give_b, far_b, keep[2:])
 
     parts = deal(total, own)
-    parts = [parts[0]] + [fetch(parts[dy], "y", -dy) for dy in (1, 3, 2)]
+    parts = [parts[0]] + [fetch(parts[dy], "y", -dy) for dy in (2, 1, 3)]
 
     def last(*parts):
         both = sum(part.astype(F32) for part in parts)

time: 192 us -> 192 us (level)
  transfers between devices with their start and end apart: 36 -> 36, of which waited for: 17 -> 16; matrix products, arithmetic and copies ran while one was open for 6% -> 6% of each run, Pallas kernels for 13% -> 13%
where the time goes in v3:
time: 192 us
  waiting for transfers between devices  75.6 us (39%)
  starting transfers between devices  44.6 us (23%)
  Pallas kernels  42.5 us (22%)
  between operations  14.5 us (8%)
  other arithmetic  7.36 us (4%)
  local copies, waits for them, and re-layouts  6.39 us (3%)
    ppermute x34, starting transfers between devices, fetch(): lax.ppermute(block, axis, [(i, (i - offset) % size) for i in range(size)])  44.5 us
    ppermute x34, waiting for transfers between devices, fetch(): lax.ppermute(block, axis, [(i, (i - offset) % size) for i in range(size)])  39.1 us
    reduce_scatter x1, waiting for transfers between devices, per_device(): total = lax.psum_scatter(total, 'z', scatter_dimension=0, tiled=True)  35.6 us
    pallas_call x2, Pallas kernels, weight_grads(): call(kernel, [jax.ShapeDtypeStruct((2, hid, cols), BF), jax.ShapeDtypeStr...  15.2 us
    pallas_call x1, Pallas kernels, middle(): call(kernel, [jax.ShapeDtypeStruct((N_Z, block, 2 * hid), BF), jax.ShapeD...  14.1 us
    pallas_call x4, Pallas kernels, turn(): call(kernel, jax.ShapeDtypeStruct((cols, 2 * rows), BF), [ANYWHERE] * 2,...  8.27 us
    unnamed x45, local copies, waits for them, and re-layouts  4.24 us
  transfers between devices with their start and end apart: 36, of which 16 were waited for; matrix products, arithmetic and copies ran while one was open for 6% of the time, Pallas kernels for 13%

profile of v3, /device:TPU:2, one launch (start us, length us, event | category | flops | bytes accessed | tf_op | source)
XLA Modules:
  0.0 191.9 jit_solution(241798875566975435)
XLA Ops:
  7.2 1.0 shard_map.102.mine_ref
  8.2 2.4 %collective-permute-start = (bf16[16,4608]{1,0:T(8,128)(2,1)S(1)}, bf16[16,4608]{1,0:T(8,128)(2,1)S(1)}, u32[]{:S(2)}, u32[]{:S(2)}) collective-permute-start(bf16[16,4608]{1,0:T(8,128)(2,1)S(1)} %shard_map.102.mine_ref), channel_id=1, source_target_pairs={{0,32},{32,0},{1,33},{33,1},{2,34},{34,2},{3,35},{35,3},{4,36},{36... | collective-permute-start | bytes 442376 | tf_op jit(solution)/shard_map/ppermute | solution.py:52
  11.8 1.0 copy-done.7
  12.8 1.0 copy-done.8
  13.8 1.0 copy-done.9
  15.2 1.8 collective-permute-start.3
  17.3 1.9 collective-permute-start.5
  19.2 5.9 %collective-permute-start.1 = (bf16[16,4608]{1,0:T(8,128)(2,1)S(1)}, bf16[16,4608]{1,0:T(8,128)(2,1)S(1)}, u32[]{:S(2)}, u32[]{:S(2)}) collective-permute-start(bf16[16,4608]{1,0:T(8,128)(2,1)S(1)} %get-tuple-element.73.refs_0_), channel_id=1, source_target_pairs={{0,7},{1,0},{2,1},{3,2},{4,3},{5,4},{6,5},{7,6},{8,15},{9,8},{10,9... | collective-permute-start | bytes 442376 | tf_op jit(solution)/shard_map/ppermute | solution.py:52
  26.0 1.8 collective-permute-done.1.refs_1_
  27.8 3.7 %collective-permute-done.2.refs_2_ = bf16[16,4608]{1,0:T(8,128)(2,1)S(1)} collective-permute-done((bf16[16,4608]{1,0:T(8,128)(2,1)S(1)}, bf16[16,4608]{1,0:T(8,128)(2,1)S(1)}, u32[]{:S(2)}, u32[]{:S(2)}) %collective-permute-start.2) | collective-permute-done | bytes 147488 | tf_op jit(solution)/shard_map/ppermute | solution.py:52
  33.5 1.6 collective-permute-start.7
  35.1 2.1 %collective-permute-start.16 = (bf16[384,1024]{1,0:T(8,128)(2,1)S(1)}, bf16[384,1024]{1,0:T(8,128)(2,1)}, u32[]{:S(2)}, u32[]{:S(2)}) collective-permute-start(bf16[384,1024]{1,0:T(8,128)(2,1)S(1)} %get-tuple-element.79.top.refs_14_), channel_id=1, source_target_pairs={{0,128},{128,0},{1,129},{129,1},{2,130},{130,2},{3,131},{131,3},{4... | collective-permute-start | bytes 2359304 | tf_op jit(solution)/shard_map/ppermute | solution.py:52
  37.3 1.7 collective-permute-done.6.refs_3_
  39.0 1.3 collective-permute-done.7.refs_4_
  40.4 1.0 collective-permute-start.10
  41.4 1.1 collective-permute-start.11
  42.8 1.7 collective-permute-start.13
  44.5 7.1 %collective-permute-done.12.refs_0_ = bf16[16,4608]{1,0:T(8,128)(2,1)S(1)} collective-permute-done((bf16[16,4608]{1,0:T(8,128)(2,1)S(1)}, bf16[16,4608]{1,0:T(8,128)(2,1)S(1)}, u32[]{:S(2)}, u32[]{:S(2)}) %collective-permute-start.12) | collective-permute-done | bytes 147488 | tf_op jit(solution)/shard_map/ppermute | solution.py:52
  51.6 1.5 collective-permute-done.13.refs_1_
  53.3 1.8 collective-permute-start.15
  55.1 3.9 %collective-permute-done.14.refs_2_ = bf16[16,2304]{1,0:T(8,128)(2,1)S(1)} collective-permute-done((bf16[16,2304]{1,0:T(8,128)(2,1)S(1)}, bf16[16,2304]{1,0:T(8,128)(2,1)S(1)}, u32[]{:S(2)}, u32[]{:S(2)}) %collective-permute-start.14) | collective-permute-done | bytes 73760 | tf_op jit(solution)/shard_map/ppermute | solution.py:52
  59.0 1.5 collective-permute-done.15.refs_3_
  60.5 2.3 %collective-permute-start.21 = (bf16[384,1024]{1,0:T(8,128)(2,1)S(1)}, bf16[384,1024]{1,0:T(8,128)(2,1)}, u32[]{:S(2)}, u32[]{:S(2)}) collective-permute-start(bf16[384,1024]{1,0:T(8,128)(2,1)S(1)} %get-tuple-element.91.bottom.refs_15_), channel_id=1, source_target_pairs={{0,128},{128,0},{1,129},{129,1},{2,130},{130,2},{3,131},{131,3},{4... | collective-permute-start | bytes 2359304 | tf_op jit(solution)/shard_map/ppermute | solution.py:52
  63.0 1.8 collective-permute-start.19
  65.1 3.0 %collective-permute-start.17 = (bf16[80,2304]{1,0:T(8,128)(2,1)S(1)}, bf16[80,2304]{1,0:T(8,128)(2,1)S(1)}, u32[]{:S(2)}, u32[]{:S(2)}) collective-permute-start(bf16[80,2304]{1,0:T(8,128)(2,1)S(1)} %slice.62), channel_id=1, source_target_pairs={{0,24},{8,0},{16,8},{24,16},{1,25},{9,1},{17,9},{25,17},{2,26},{10... | collective-permute-start | bytes 1105928 | tf_op jit(solution)/shard_map/ppermute | solution.py:52
  68.3 1.8 shard_map.108.refs_10_
  70.1 1.8 shard_map.109.refs_12_
  71.9 7.0 %collective-permute-done.21.bottom.refs_17_ = bf16[384,1024]{1,0:T(8,128)(2,1)} collective-permute-done((bf16[384,1024]{1,0:T(8,128)(2,1)S(1)}, bf16[384,1024]{1,0:T(8,128)(2,1)}, u32[]{:S(2)}, u32[]{:S(2)}) %collective-permute-start.21) | collective-permute-done | bytes 786464 | tf_op jit(solution)/shard_map/ppermute | solution.py:52
  79.8 2.2 %collective-permute-done.18.refs_5_ = bf16[80,2304]{1,0:T(8,128)(2,1)S(1)} collective-permute-done((bf16[80,2304]{1,0:T(8,128)(2,1)S(1)}, bf16[80,2304]{1,0:T(8,128)(2,1)S(1)}, u32[]{:S(2)}, u32[]{:S(2)}) %collective-permute-start.18) | collective-permute-done | bytes 368672 | tf_op jit(solution)/shard_map/ppermute | solution.py:52
  83.7 1.7 collective-permute-start.23
  85.6 2.8 %shard_map.110.refs_11_ = bf16[1024,768]{1,0:T(8,128)(2,1)} custom-call(bf16[384,1024]{1,0:T(8,128)(2,1)} %collective-permute-done.16.top.refs_16_, bf16[384,1024]{1,0:T(8,128)(2,1)} %collective-permute-done.21.bottom.refs_17_), custom_call_target="tpu_custom_call" | custom-call | bytes 3145728 | tf_op jit(solution)/shard_map/pallas_call | solution.py:180
  88.5 1.8 shard_map.111.refs_13_
  90.3 2.0 %collective-permute-done.23.refs_7_ = bf16[48,2304]{1,0:T(8,128)(2,1)S(1)} collective-permute-done((bf16[48,2304]{1,0:T(8,128)(2,1)}, bf16[48,2304]{1,0:T(8,128)(2,1)S(1)}, u32[]{:S(2)}, u32[]{:S(2)}) %collective-permute-start.23) | collective-permute-done | bytes 221216 | tf_op jit(solution)/shard_map/ppermute | solution.py:52
  93.2 14.1 %shard_map.112 = (bf16[8,72,512]{2,1,0:T(8,128)(2,1)}, bf16[576,4096]{1,0:T(8,128)(2,1)}, bf16[576,256]{1,0:T(8,128)(2,1)S(1)}, bf16[8,72,4096]{2,1,0:T(8,128)(2,1)}) custom-call(s32[1]{0:T(128)} %bitcast.4.z_ref, s32[4]{0:T(128)S(1)} %pad_add_fusion.place_ref, bf16[576,4096]{1,0:T(8,128)(2,1)} %all-gather.2.cloned.1.call-done.tok_ref.refs_1_, ...), custom_call_target="tpu_custom_call" | custom-call | flops 6039797760 | bytes 31457280 | tf_op jit(solution)/shard_map/pallas_call | solution.py:370
  108.3 9.0 %shard_map.114 = (bf16[2,512,1024]{2,1,0:T(8,128)(2,1)}, f32[2,512,1024]{2,1,0:T(8,128)}) custom-call(s32[4]{0:T(128)S(1)} %rev.3.order_ref, bf16[576,512]{1,0:T(8,128)(2,1)S(1)} %bitcast.52, bf16[576,4096]{1,0:T(8,128)(2,1)} %all-gather.2.cloned.1.call-done.tok_ref.refs_1_), custom_call_target="tpu_custom_call" | custom-call | flops 2415919104 | bytes 11010048 | tf_op jit(solution)/shard_map/pallas_call | solution.py:443
  117.5 6.1 %shard_map.115 = (bf16[2,256,1024]{2,1,0:T(8,128)(2,1)S(1)}, f32[2,256,1024]{2,1,0:T(8,128)}) custom-call(s32[4]{0:T(128)S(1)} %rev.3.order_ref, bf16[576,256]{1,0:T(8,128)(2,1)S(1)} %get-tuple-element.117.refs_0_, bf16[576,4096]{1,0:T(8,128)(2,1)} %get-tuple-element.118.refs_1_), custom_call_target="tpu_custom_call" | custom-call | flops 1207959552 | bytes 7864320 | tf_op jit(solution)/shard_map/pallas_call | solution.py:443
  124.2 1.3 fusion.1
  125.6 2.1 %collective-permute-start.30 = (bf16[512,1024]{1,0:T(8,128)(2,1)}, bf16[512,1024]{1,0:T(8,128)(2,1)}, u32[]{:S(2)}, u32[]{:S(2)}) collective-permute-start(bf16[512,1024]{1,0:T(8,128)(2,1)} %fusion.1), channel_id=1, source_target_pairs={{0,128},{128,0},{1,129},{129,1},{2,130},{130,2},{3,131},{131,3},{4... | collective-permute-start | bytes 3145736 | tf_op jit(solution)/shard_map/ppermute | solution.py:52
  128.6 1.4 collective-permute-start.32
  130.2 35.6 %reduce-scatter.2.cloned.1.call-done.ref = bf16[72,4096]{1,0:T(8,128)(2,1)} async-done(((bf16[576,4096]{1,0:T(8,128)(2,1)}), bf16[72,4096]{1,0:T(8,128)(2,1)}) %reduce-scatter.2.cloned.1.call-update) | async-done | bytes 589840 | tf_op jit(solution)/shard_map/reduce_scatter | solution.py:517
  165.9 1.3 shard_map.113
  167.2 3.1 %collective-permute-start.26 = (bf16[16,4608]{1,0:T(8,128)(2,1)S(1)}, bf16[16,4608]{1,0:T(8,128)(2,1)S(1)}, u32[]{:S(2)}, u32[]{:S(2)}) collective-permute-start(bf16[16,4608]{1,0:T(8,128)(2,1)S(1)} %get-tuple-element.111), channel_id=1, source_target_pairs={{0,16},{8,24},{16,0},{24,8},{1,17},{9,25},{17,1},{25,9},{2,18},{10... | collective-permute-start | bytes 442376 | tf_op jit(solution)/shard_map/ppermute | solution.py:52
  170.9 2.7 %collective-permute-start.28 = (bf16[16,4608]{1,0:T(8,128)(2,1)S(1)}, bf16[16,4608]{1,0:T(8,128)(2,1)S(1)}, u32[]{:S(2)}, u32[]{:S(2)}) collective-permute-start(bf16[16,4608]{1,0:T(8,128)(2,1)S(1)} %get-tuple-element.113), channel_id=1, source_target_pairs={{0,24},{8,0},{16,8},{24,16},{1,25},{9,1},{17,9},{25,17},{2,26},{10... | collective-permute-start | bytes 442376 | tf_op jit(solution)/shard_map/ppermute | solution.py:52
  173.5 2.7 %bitcast_add_fusion = f32[512,1024]{1,0:T(8,128)S(1)} fusion(bf16[512,1024]{1,0:T(8,128)(2,1)} %collective-permute-done.30, f32[2,512,1024]{2,1,0:T(8,128)} %get-tuple-element.115, bf16[2,512,1024]{2,1,0:T(8,128)(2,1)} %copy-done.15), kind=kLoop, calls=%fused_computation.2 | loop fusion | flops 2097152 | bytes 6291456 | tf_op jit(solution)/shard_map/add | solution.py:529
  176.4 2.1 %fusion.2 = bf16[256,1024]{1,0:T(8,128)(2,1)} fusion(bf16[256,1024]{1,0:T(8,128)(2,1)} %collective-permute-done.32, f32[2,256,1024]{2,1,0:T(8,128)S(1)} %copy-done.14, bf16[2,256,1024]{2,1,0:T(8,128)(2,1)S(1)} %collective-permute-done.31, f32[2,1024]{1,0:T(2,128)S(1)} %bitcast.56), kind=kLoop, calls=%fused_computation.6 | loop fusion | flops 1572864 | bytes 2629632 | tf_op jit(solution)/shard_map/convert_element_type | solution.py:531
  179.3 1.0 slice_bitcast_fusion
  180.3 3.6 %collective-permute-done.33.other_ref = f32[8,4608]{1,0:T(8,128)S(1)} collective-permute-done((f32[8,4608]{1,0:T(8,128)S(1)}, f32[8,4608]{1,0:T(8,128)S(1)}, u32[]{:S(2)}, u32[]{:S(2)}) %collective-permute-start.33) | collective-permute-done | bytes 147488 | tf_op jit(solution)/shard_map/ppermute | solution.py:52
  183.9 1.2 shard_map.117
  (109 shorter events, 13.7 us)
Async XLA Ops:
  7.2 86.0 %all-gather.2.cloned.1.call-start = ((), (), s32[]{:S(2)}) async-start(), calls=%async_computation.1 | async-start | bytes 5308416 | tf_op jit(solution)/shard_map/all_gather | solution.py:488
  8.2 6.9 %collective-permute-start = (bf16[16,4608]{1,0:T(8,128)(2,1)S(1)}, bf16[16,4608]{1,0:T(8,128)(2,1)S(1)}, u32[]{:S(2)}, u32[]{:S(2)}) collective-permute-start(bf16[16,4608]{1,0:T(8,128)(2,1)S(1)} %shard_map.102.mine_ref), channel_id=1, source_target_pairs={{0,32},{32,0},{1,33},{33,1},{2,34},{34,2},{3,35},{35,3},{4,36},{36... | collective-permute-start | bytes 442376 | tf_op jit(solution)/shard_map/ppermute | solution.py:52
  11.6 116.0 %copy-start.20 = (f32[3,2,8]{2,1,0:T(2,128)}, f32[3,2,8]{2,1,0:T(2,128)S(1)}, u32[]{:S(2)}) copy-start(f32[3,2,8]{2,1,0:T(2,128)S(1)} %dynamic-slice_bitcast_fusion) | copy-start | bytes 580
  15.1 53.1 %copy-start = (bf16[384,1024]{1,0:T(8,128)(2,1)}, bf16[384,1024]{1,0:T(8,128)(2,1)S(1)}, u32[]{:S(2)}) copy-start(bf16[384,1024]{1,0:T(8,128)(2,1)S(1)} %get-tuple-element.79.top.refs_14_) | copy-start | bytes 2359300
  15.1 53.1 %copy-start.1 = (bf16[384,1024]{1,0:T(8,128)(2,1)}, bf16[384,1024]{1,0:T(8,128)(2,1)S(1)}, u32[]{:S(2)}) copy-start(bf16[384,1024]{1,0:T(8,128)(2,1)S(1)} %get-tuple-element.91.bottom.refs_15_) | copy-start | bytes 2359300
  15.2 9.9 %collective-permute-start.3 = (bf16[16,4608]{1,0:T(8,128)(2,1)S(1)}, bf16[16,4608]{1,0:T(8,128)(2,1)S(1)}, u32[]{:S(2)}, u32[]{:S(2)}) collective-permute-start(bf16[16,4608]{1,0:T(8,128)(2,1)S(1)} %get-tuple-element.72.refs_0_), channel_id=1, source_target_pairs={{0,24},{8,0},{16,8},{24,16},{1,25},{9,1},{17,9},{25,17},{2,26},{10... | collective-permute-start | bytes 442376 | tf_op jit(solution)/shard_map/ppermute | solution.py:52
  17.0 8.9 %collective-permute-start.4 = (bf16[16,4608]{1,0:T(8,128)(2,1)S(1)}, bf16[16,4608]{1,0:T(8,128)(2,1)S(1)}, u32[]{:S(2)}, u32[]{:S(2)}) collective-permute-start(bf16[16,4608]{1,0:T(8,128)(2,1)S(1)} %get-tuple-element.72.refs_0_), channel_id=1, source_target_pairs={{0,8},{8,16},{16,24},{24,0},{1,9},{9,17},{17,25},{25,1},{2,10},{10... | collective-permute-start | bytes 442376 | tf_op jit(solution)/shard_map/ppermute | solution.py:52
  17.3 8.7 %collective-permute-start.5 = (bf16[16,4608]{1,0:T(8,128)(2,1)S(1)}, bf16[16,4608]{1,0:T(8,128)(2,1)S(1)}, u32[]{:S(2)}, u32[]{:S(2)}) collective-permute-start(bf16[16,4608]{1,0:T(8,128)(2,1)S(1)} %get-tuple-element.72.refs_0_), channel_id=1, source_target_pairs={{0,16},{8,24},{16,0},{24,8},{1,17},{9,25},{17,1},{25,9},{2,18},{10... | collective-permute-start | bytes 442376 | tf_op jit(solution)/shard_map/ppermute | solution.py:52
  19.2 8.5 %collective-permute-start.1 = (bf16[16,4608]{1,0:T(8,128)(2,1)S(1)}, bf16[16,4608]{1,0:T(8,128)(2,1)S(1)}, u32[]{:S(2)}, u32[]{:S(2)}) collective-permute-start(bf16[16,4608]{1,0:T(8,128)(2,1)S(1)} %get-tuple-element.73.refs_0_), channel_id=1, source_target_pairs={{0,7},{1,0},{2,1},{3,2},{4,3},{5,4},{6,5},{7,6},{8,15},{9,8},{10,9... | collective-permute-start | bytes 442376 | tf_op jit(solution)/shard_map/ppermute | solution.py:52
  25.1 6.4 %collective-permute-start.2 = (bf16[16,4608]{1,0:T(8,128)(2,1)S(1)}, bf16[16,4608]{1,0:T(8,128)(2,1)S(1)}, u32[]{:S(2)}, u32[]{:S(2)}) collective-permute-start(bf16[16,4608]{1,0:T(8,128)(2,1)S(1)} %get-tuple-element.73.refs_0_), channel_id=1, source_target_pairs={{0,1},{1,2},{2,3},{3,4},{4,5},{5,6},{6,7},{7,0},{8,9},{9,10},{10,1... | collective-permute-start | bytes 442376 | tf_op jit(solution)/shard_map/ppermute | solution.py:52
  32.5 133.4 %reduce-scatter.2.cloned.1.call-start = ((), (), s32[]{:S(2)}) async-start(), calls=%async_computation.2 | async-start | bytes 5308416 | tf_op jit(solution)/shard_map/reduce_scatter | solution.py:517
  32.5 7.8 %collective-permute-start.8 = (bf16[384,1024]{1,0:T(8,128)(2,1)S(1)}, bf16[384,1024]{1,0:T(8,128)(2,1)S(1)}, u32[]{:S(2)}, u32[]{:S(2)}) collective-permute-start(bf16[384,1024]{1,0:T(8,128)(2,1)S(1)} %get-tuple-element.79.top.refs_14_), channel_id=1, source_target_pairs={{0,64},{64,0},{1,65},{65,1},{2,66},{66,2},{3,67},{67,3},{4,68},{68... | collective-permute-start | bytes 2359304 | tf_op jit(solution)/shard_map/ppermute | solution.py:52
  32.6 7.7 %collective-permute-start.9 = (bf16[384,1024]{1,0:T(8,128)(2,1)S(1)}, bf16[384,1024]{1,0:T(8,128)(2,1)S(1)}, u32[]{:S(2)}, u32[]{:S(2)}) collective-permute-start(bf16[384,1024]{1,0:T(8,128)(2,1)S(1)} %get-tuple-element.91.bottom.refs_15_), channel_id=1, source_target_pairs={{0,64},{64,0},{1,65},{65,1},{2,66},{66,2},{3,67},{67,3},{4,68},{68... | collective-permute-start | bytes 2359304 | tf_op jit(solution)/shard_map/ppermute | solution.py:52
  33.1 5.9 %collective-permute-start.6 = (bf16[16,4608]{1,0:T(8,128)(2,1)S(1)}, bf16[16,4608]{1,0:T(8,128)(2,1)S(1)}, u32[]{:S(2)}, u32[]{:S(2)}) collective-permute-start(bf16[16,4608]{1,0:T(8,128)(2,1)S(1)} %collective-permute-done.1.refs_1_), channel_id=1, source_target_pairs={{0,7},{1,0},{2,1},{3,2},{4,3},{5,4},{6,5},{7,6},{8,15},{9,8},{10,9... | collective-permute-start | bytes 442376 | tf_op jit(solution)/shard_map/ppermute | solution.py:52
  33.5 6.8 %collective-permute-start.7 = (bf16[16,4608]{1,0:T(8,128)(2,1)S(1)}, bf16[16,4608]{1,0:T(8,128)(2,1)S(1)}, u32[]{:S(2)}, u32[]{:S(2)}) collective-permute-start(bf16[16,4608]{1,0:T(8,128)(2,1)S(1)} %collective-permute-done.2.refs_2_), channel_id=1, source_target_pairs={{0,1},{1,2},{2,3},{3,4},{4,5},{5,6},{6,7},{7,0},{8,9},{9,10},{10,1... | collective-permute-start | bytes 442376 | tf_op jit(solution)/shard_map/ppermute | solution.py:52
  35.1 27.8 %collective-permute-start.16 = (bf16[384,1024]{1,0:T(8,128)(2,1)S(1)}, bf16[384,1024]{1,0:T(8,128)(2,1)}, u32[]{:S(2)}, u32[]{:S(2)}) collective-permute-start(bf16[384,1024]{1,0:T(8,128)(2,1)S(1)} %get-tuple-element.79.top.refs_14_), channel_id=1, source_target_pairs={{0,128},{128,0},{1,129},{129,1},{2,130},{130,2},{3,131},{131,3},{4... | collective-permute-start | bytes 2359304 | tf_op jit(solution)/shard_map/ppermute | solution.py:52
  40.3 29.8 %copy-start.2 = (bf16[384,1024]{1,0:T(8,128)(2,1)}, bf16[384,1024]{1,0:T(8,128)(2,1)S(1)}, u32[]{:S(2)}) copy-start(bf16[384,1024]{1,0:T(8,128)(2,1)S(1)} %collective-permute-done.8.top.refs_18_) | copy-start | bytes 2359300
  40.3 29.8 %copy-start.3 = (bf16[384,1024]{1,0:T(8,128)(2,1)}, bf16[384,1024]{1,0:T(8,128)(2,1)S(1)}, u32[]{:S(2)}) copy-start(bf16[384,1024]{1,0:T(8,128)(2,1)S(1)} %collective-permute-done.9.bottom.refs_19_) | copy-start | bytes 2359300
  40.4 22.6 %copy-start.6 = (bf16[80,4608]{1,0:T(8,128)(2,1)}, bf16[80,4608]{1,0:T(8,128)(2,1)S(1)}, u32[]{:S(2)}) copy-start(bf16[80,4608]{1,0:T(8,128)(2,1)S(1)} %shard_map.106.refs_0_) | copy-start | bytes 2211844
  40.4 22.6 %collective-permute-start.10 = (bf16[80,4608]{1,0:T(8,128)(2,1)S(1)}, bf16[80,4608]{1,0:T(8,128)(2,1)S(1)}, u32[]{:S(2)}, u32[]{:S(2)}) collective-permute-start(bf16[80,4608]{1,0:T(8,128)(2,1)S(1)} %shard_map.106.refs_0_), channel_id=1, source_target_pairs={{0,24},{8,0},{16,8},{24,16},{1,25},{9,1},{17,9},{25,17},{2,26},{10... | collective-permute-start | bytes 2211848 | tf_op jit(solution)/shard_map/ppermute | solution.py:52
  41.4 21.6 %collective-permute-start.11 = (bf16[80,4608]{1,0:T(8,128)(2,1)S(1)}, bf16[80,4608]{1,0:T(8,128)(2,1)S(1)}, u32[]{:S(2)}, u32[]{:S(2)}) collective-permute-start(bf16[80,4608]{1,0:T(8,128)(2,1)S(1)} %shard_map.106.refs_0_), channel_id=1, source_target_pairs={{0,8},{8,16},{16,24},{24,0},{1,9},{9,17},{17,25},{25,1},{2,10},{10... | collective-permute-start | bytes 2211848 | tf_op jit(solution)/shard_map/ppermute | solution.py:52
  42.5 9.1 %collective-permute-start.12 = (bf16[16,4608]{1,0:T(8,128)(2,1)S(1)}, bf16[16,4608]{1,0:T(8,128)(2,1)S(1)}, u32[]{:S(2)}, u32[]{:S(2)}) collective-permute-start(bf16[16,4608]{1,0:T(8,128)(2,1)S(1)} %collective-permute-done.6.refs_3_), channel_id=1, source_target_pairs={{0,7},{1,0},{2,1},{3,2},{4,3},{5,4},{6,5},{7,6},{8,15},{9,8},{10,9... | collective-permute-start | bytes 442376 | tf_op jit(solution)/shard_map/ppermute | solution.py:52
  42.8 10.3 %collective-permute-start.13 = (bf16[16,4608]{1,0:T(8,128)(2,1)S(1)}, bf16[16,4608]{1,0:T(8,128)(2,1)S(1)}, u32[]{:S(2)}, u32[]{:S(2)}) collective-permute-start(bf16[16,4608]{1,0:T(8,128)(2,1)S(1)} %collective-permute-done.7.refs_4_), channel_id=1, source_target_pairs={{0,1},{1,2},{2,3},{3,4},{4,5},{5,6},{6,7},{7,0},{8,9},{9,10},{10,1... | collective-permute-start | bytes 442376 | tf_op jit(solution)/shard_map/ppermute | solution.py:52
  53.1 5.9 %collective-permute-start.14 = (bf16[16,2304]{1,0:T(8,128)(2,1)S(1)}, bf16[16,2304]{1,0:T(8,128)(2,1)S(1)}, u32[]{:S(2)}, u32[]{:S(2)}) collective-permute-start(bf16[16,2304]{1,0:T(8,128)(2,1)S(1)} %slice.60), channel_id=1, source_target_pairs={{0,7},{1,0},{2,1},{3,2},{4,3},{5,4},{6,5},{7,6},{8,15},{9,8},{10,9... | collective-permute-start | bytes 221192 | tf_op jit(solution)/shard_map/ppermute | solution.py:52
  53.3 7.2 %collective-permute-start.15 = (bf16[16,2304]{1,0:T(8,128)(2,1)S(1)}, bf16[16,2304]{1,0:T(8,128)(2,1)S(1)}, u32[]{:S(2)}, u32[]{:S(2)}) collective-permute-start(bf16[16,2304]{1,0:T(8,128)(2,1)S(1)} %slice.61), channel_id=1, source_target_pairs={{0,1},{1,2},{2,3},{3,4},{4,5},{5,6},{6,7},{7,0},{8,9},{9,10},{10,1... | collective-permute-start | bytes 221192 | tf_op jit(solution)/shard_map/ppermute | solution.py:52
  60.5 18.4 %collective-permute-start.21 = (bf16[384,1024]{1,0:T(8,128)(2,1)S(1)}, bf16[384,1024]{1,0:T(8,128)(2,1)}, u32[]{:S(2)}, u32[]{:S(2)}) collective-permute-start(bf16[384,1024]{1,0:T(8,128)(2,1)S(1)} %get-tuple-element.91.bottom.refs_15_), channel_id=1, source_target_pairs={{0,128},{128,0},{1,129},{129,1},{2,130},{130,2},{3,131},{131,3},{4... | collective-permute-start | bytes 2359304 | tf_op jit(solution)/shard_map/ppermute | solution.py:52
  62.9 7.2 %copy-start.10 = (bf16[48,4608]{1,0:T(8,128)(2,1)}, bf16[48,4608]{1,0:T(8,128)(2,1)S(1)}, u32[]{:S(2)}) copy-start(bf16[48,4608]{1,0:T(8,128)(2,1)S(1)} %shard_map.107.refs_1_) | copy-start | bytes 1327108
  62.9 7.2 %copy-start.16 = (bf16[80,4608]{1,0:T(8,128)(2,1)}, bf16[80,4608]{1,0:T(8,128)(2,1)S(1)}, u32[]{:S(2)}) copy-start(bf16[80,4608]{1,0:T(8,128)(2,1)S(1)} %collective-permute-done.10.refs_2_) | copy-start | bytes 2211844
  63.0 7.1 %copy-start.17 = (bf16[80,4608]{1,0:T(8,128)(2,1)}, bf16[80,4608]{1,0:T(8,128)(2,1)S(1)}, u32[]{:S(2)}) copy-start(bf16[80,4608]{1,0:T(8,128)(2,1)S(1)} %collective-permute-done.11.refs_8_) | copy-start | bytes 2211844
  63.0 19.1 %collective-permute-start.19 = (bf16[48,4608]{1,0:T(8,128)(2,1)S(1)}, bf16[48,4608]{1,0:T(8,128)(2,1)S(1)}, u32[]{:S(2)}, u32[]{:S(2)}) collective-permute-start(bf16[48,4608]{1,0:T(8,128)(2,1)S(1)} %shard_map.107.refs_1_), channel_id=1, source_target_pairs={{0,24},{8,0},{16,8},{24,16},{1,25},{9,1},{17,9},{25,17},{2,26},{10... | collective-permute-start | bytes 1327112 | tf_op jit(solution)/shard_map/ppermute | solution.py:52
  64.8 17.3 %collective-permute-start.20 = (bf16[48,4608]{1,0:T(8,128)(2,1)S(1)}, bf16[48,4608]{1,0:T(8,128)(2,1)S(1)}, u32[]{:S(2)}, u32[]{:S(2)}) collective-permute-start(bf16[48,4608]{1,0:T(8,128)(2,1)S(1)} %shard_map.107.refs_1_), channel_id=1, source_target_pairs={{0,8},{8,16},{16,24},{24,0},{1,9},{9,17},{17,25},{25,1},{2,10},{10... | collective-permute-start | bytes 1327112 | tf_op jit(solution)/shard_map/ppermute | solution.py:52
  65.1 14.7 %collective-permute-start.17 = (bf16[80,2304]{1,0:T(8,128)(2,1)S(1)}, bf16[80,2304]{1,0:T(8,128)(2,1)S(1)}, u32[]{:S(2)}, u32[]{:S(2)}) collective-permute-start(bf16[80,2304]{1,0:T(8,128)(2,1)S(1)} %slice.62), channel_id=1, source_target_pairs={{0,24},{8,0},{16,8},{24,16},{1,25},{9,1},{17,9},{25,17},{2,26},{10... | collective-permute-start | bytes 1105928 | tf_op jit(solution)/shard_map/ppermute | solution.py:52
  68.1 13.9 %collective-permute-start.18 = (bf16[80,2304]{1,0:T(8,128)(2,1)S(1)}, bf16[80,2304]{1,0:T(8,128)(2,1)S(1)}, u32[]{:S(2)}, u32[]{:S(2)}) collective-permute-start(bf16[80,2304]{1,0:T(8,128)(2,1)S(1)} %slice.63), channel_id=1, source_target_pairs={{0,8},{8,16},{16,24},{24,0},{1,9},{9,17},{17,25},{25,1},{2,10},{10... | collective-permute-start | bytes 1105928 | tf_op jit(solution)/shard_map/ppermute | solution.py:52
  82.1 6.4 %collective-permute-start.24 = (bf16[384,1024]{1,0:T(8,128)(2,1)}, bf16[384,1024]{1,0:T(8,128)(2,1)S(1)}, u32[]{:S(2)}, u32[]{:S(2)}) collective-permute-start(bf16[384,1024]{1,0:T(8,128)(2,1)} %collective-permute-done.16.top.refs_16_), channel_id=1, source_target_pairs={{0,64},{64,0},{1,65},{65,1},{2,66},{66,2},{3,67},{67,3},{4,68},{68... | collective-permute-start | bytes 2359304 | tf_op jit(solution)/shard_map/ppermute | solution.py:52
  82.2 6.3 %collective-permute-start.25 = (bf16[384,1024]{1,0:T(8,128)(2,1)}, bf16[384,1024]{1,0:T(8,128)(2,1)S(1)}, u32[]{:S(2)}, u32[]{:S(2)}) collective-permute-start(bf16[384,1024]{1,0:T(8,128)(2,1)} %collective-permute-done.21.bottom.refs_17_), channel_id=1, source_target_pairs={{0,64},{64,0},{1,65},{65,1},{2,66},{66,2},{3,67},{67,3},{4,68},{68... | collective-permute-start | bytes 2359304 | tf_op jit(solution)/shard_map/ppermute | solution.py:52
  82.7 7.6 %collective-permute-start.22 = (bf16[48,2304]{1,0:T(8,128)(2,1)S(1)}, bf16[48,2304]{1,0:T(8,128)(2,1)S(1)}, u32[]{:S(2)}, u32[]{:S(2)}) collective-permute-start(bf16[48,2304]{1,0:T(8,128)(2,1)S(1)} %slice.64), channel_id=1, source_target_pairs={{0,24},{8,0},{16,8},{24,16},{1,25},{9,1},{17,9},{25,17},{2,26},{10... | collective-permute-start | bytes 663560 | tf_op jit(solution)/shard_map/ppermute | solution.py:52
  83.7 8.6 %collective-permute-start.23 = (bf16[48,2304]{1,0:T(8,128)(2,1)}, bf16[48,2304]{1,0:T(8,128)(2,1)S(1)}, u32[]{:S(2)}, u32[]{:S(2)}) collective-permute-start(bf16[48,2304]{1,0:T(8,128)(2,1)} %slice.65), channel_id=1, source_target_pairs={{0,8},{8,16},{16,24},{24,0},{1,9},{9,17},{17,25},{25,1},{2,10},{10... | collective-permute-start | bytes 663560 | tf_op jit(solution)/shard_map/ppermute | solution.py:52
  88.4 4.8 %copy-start.11 = (bf16[48,4608]{1,0:T(8,128)(2,1)S(1)}, bf16[48,4608]{1,0:T(8,128)(2,1)}, u32[]{:S(2)}) copy-start(bf16[48,4608]{1,0:T(8,128)(2,1)} %copy-done.10) | copy-start | bytes 1327108
  88.4 4.7 %copy-start.4 = (bf16[384,1024]{1,0:T(8,128)(2,1)}, bf16[384,1024]{1,0:T(8,128)(2,1)S(1)}, u32[]{:S(2)}) copy-start(bf16[384,1024]{1,0:T(8,128)(2,1)S(1)} %collective-permute-done.24.top.refs_20_) | copy-start | bytes 2359300
  117.4 6.2 %collective-permute-start.29 = (bf16[2,512,1024]{2,1,0:T(8,128)(2,1)}, bf16[2,512,1024]{2,1,0:T(8,128)(2,1)S(1)}, u32[]{:S(2)}, u32[]{:S(2)}) collective-permute-start(bf16[2,512,1024]{2,1,0:T(8,128)(2,1)} %get-tuple-element.116), channel_id=1, source_target_pairs={{0,64},{64,0},{1,65},{65,1},{2,66},{66,2},{3,67},{67,3},{4,68},{68... | collective-permute-start | bytes 6291464 | tf_op jit(solution)/shard_map/ppermute | solution.py:52
  117.5 6.7 %copy-start.13 = (f32[2,512,1024]{2,1,0:T(8,128)S(1)}, f32[2,512,1024]{2,1,0:T(8,128)}, u32[]{:S(2)}) copy-start(f32[2,512,1024]{2,1,0:T(8,128)} %get-tuple-element.115) | copy-start | bytes 12582916
  123.6 4.0 %collective-permute-start.31 = (bf16[2,256,1024]{2,1,0:T(8,128)(2,1)S(1)}, bf16[2,256,1024]{2,1,0:T(8,128)(2,1)S(1)}, u32[]{:S(2)}, u32[]{:S(2)}) collective-permute-start(bf16[2,256,1024]{2,1,0:T(8,128)(2,1)S(1)} %get-tuple-element.123), channel_id=1, source_target_pairs={{0,64},{64,0},{1,65},{65,1},{2,66},{66,2},{3,67},{67,3},{4,68},{68... | collective-permute-start | bytes 3145736 | tf_op jit(solution)/shard_map/ppermute | solution.py:52
  125.6 48.0 %collective-permute-start.30 = (bf16[512,1024]{1,0:T(8,128)(2,1)}, bf16[512,1024]{1,0:T(8,128)(2,1)}, u32[]{:S(2)}, u32[]{:S(2)}) collective-permute-start(bf16[512,1024]{1,0:T(8,128)(2,1)} %fusion.1), channel_id=1, source_target_pairs={{0,128},{128,0},{1,129},{129,1},{2,130},{130,2},{3,131},{131,3},{4... | collective-permute-start | bytes 3145736 | tf_op jit(solution)/shard_map/ppermute | solution.py:52
  128.6 47.8 %collective-permute-start.32 = (bf16[256,1024]{1,0:T(8,128)(2,1)}, bf16[256,1024]{1,0:T(8,128)(2,1)}, u32[]{:S(2)}, u32[]{:S(2)}) collective-permute-start(bf16[256,1024]{1,0:T(8,128)(2,1)} %fusion.3), channel_id=1, source_target_pairs={{0,128},{128,0},{1,129},{129,1},{2,130},{130,2},{3,131},{131,3},{4... | collective-permute-start | bytes 1572872 | tf_op jit(solution)/shard_map/ppermute | solution.py:52
  167.2 11.4 %collective-permute-start.26 = (bf16[16,4608]{1,0:T(8,128)(2,1)S(1)}, bf16[16,4608]{1,0:T(8,128)(2,1)S(1)}, u32[]{:S(2)}, u32[]{:S(2)}) collective-permute-start(bf16[16,4608]{1,0:T(8,128)(2,1)S(1)} %get-tuple-element.111), channel_id=1, source_target_pairs={{0,16},{8,24},{16,0},{24,8},{1,17},{9,25},{17,1},{25,9},{2,18},{10... | collective-permute-start | bytes 442376 | tf_op jit(solution)/shard_map/ppermute | solution.py:52
  170.3 8.3 %collective-permute-start.27 = (bf16[16,4608]{1,0:T(8,128)(2,1)S(1)}, bf16[16,4608]{1,0:T(8,128)(2,1)S(1)}, u32[]{:S(2)}, u32[]{:S(2)}) collective-permute-start(bf16[16,4608]{1,0:T(8,128)(2,1)S(1)} %get-tuple-element.112), channel_id=1, source_target_pairs={{0,8},{8,16},{16,24},{24,0},{1,9},{9,17},{17,25},{25,1},{2,10},{10... | collective-permute-start | bytes 442376 | tf_op jit(solution)/shard_map/ppermute | solution.py:52
  170.9 7.7 %collective-permute-start.28 = (bf16[16,4608]{1,0:T(8,128)(2,1)S(1)}, bf16[16,4608]{1,0:T(8,128)(2,1)S(1)}, u32[]{:S(2)}, u32[]{:S(2)}) collective-permute-start(bf16[16,4608]{1,0:T(8,128)(2,1)S(1)} %get-tuple-element.113), channel_id=1, source_target_pairs={{0,24},{8,0},{16,8},{24,16},{1,25},{9,1},{17,9},{25,17},{2,26},{10... | collective-permute-start | bytes 442376 | tf_op jit(solution)/shard_map/ppermute | solution.py:52
  178.6 5.2 %collective-permute-start.33 = (f32[8,4608]{1,0:T(8,128)S(1)}, f32[8,4608]{1,0:T(8,128)S(1)}, u32[]{:S(2)}, u32[]{:S(2)}) collective-permute-start(f32[8,4608]{1,0:T(8,128)S(1)} %get-tuple-element.129), channel_id=1, source_target_pairs={{0,32},{32,0},{1,33},{33,1},{2,34},{34,2},{3,35},{35,3},{4,36},{36... | collective-permute-start | bytes 442376 | tf_op jit(solution)/shard_map/ppermute | solution.py:52
  (10 other events, 19.5 us)
Sparse Core Ops, SparseCore 0:
  32.6 60.5 all-gather.1
  107.4 58.4 reduce-scatter.1
